TPU v7x, 128 devices: a whole 4x4x4 slice. The times are simulated.
128 devices in a mesh: replica: 16 (over x, y_lo, core), expert: 4 (over z), tensor: 2 (over y_hi).
Axes of the slice: x: 4, y: 4 (y_hi: 2, y_lo: 2; y = y_hi * 2 + y_lo), z: 4, core: 2. Of those that a mesh axis runs over, the one named last changes fastest.
Arguments:
- kv_param: float32 [4, 64, 128, 128], P('tensor', ('replica', 'expert')), may hold values from -60 to 60, as said below
- kv_grad: float32 [4, 64, 128, 128], P('tensor', ('replica', 'expert')), as said below
- kv_mean: float32 [4, 64, 128, 128], P('tensor', ('replica', 'expert')), as said below
- kv_square: float32 [4, 64, 128, 128], P('tensor', ('replica', 'expert')), as said below
- exp_param: float32 [4, 2, 192, 128, 128], P(None, 'tensor', ('replica', 'expert')), may hold values from -60 to 60, as said below
- exp_grad: float32 [4, 2, 192, 128, 128], P(None, 'tensor', ('replica', 'expert')), as said below
- exp_mean: float32 [4, 2, 192, 128, 128], P(None, 'tensor', ('replica', 'expert')), as said below
- exp_square: float32 [4, 2, 192, 128, 128], P(None, 'tensor', ('replica', 'expert')), as said below
- expert_owner: int32 [4], replicated, may hold values from 0 to 3, as said below
Outputs:
- kv_param_new: float32 [4, 64, 128, 128], P('tensor', ('replica', 'expert'))
- exp_param_new: float32 [4, 2, 192, 128, 128], P(None, 'tensor', ('replica', 'expert'))
- kv_rollout: bfloat16 [4, 64, 128, 128], P('tensor')
- kv_scales: float32 [4, 64], P('tensor')
- exp_rollout: bfloat16 [8, 2, 192, 128, 128], P('expert', 'tensor')
- exp_scales: float32 [8, 2, 192], P('expert', 'tensor')
Inputs may be any that keep to these rules, and one draw needn't show every extreme that they name: `expert_owner`: each of the 4 rollout expert shards owns at most 2 experts; in every draw one shard owns exactly 2. `kv_param`: master blocks of order one. `exp_param`: master blocks of order one. `kv_grad`: gradient entries of order one over the square root of the parameter count, give or take a factor of ten. `exp_grad`: gradient entries of order one over the square root of the parameter count, give or take a factor of ten. `kv_mean`: first moments of the gradients' order. `exp_mean`: first moments of the gradients' order. `kv_square`: positive second moments. `exp_square`: positive second moments.
All inputs are finite; a program needn't handle non-finite values. Where the computation divides by a largest or mean magnitude, that divisor is 1e-20 or more.
Results may differ from a plain program's by a relative error of at most 0.001.
The roundings to bfloat16 on the way count: a program that leaves them out, or rounds other values in their place, can miss the bound.
Values may be sent and summed in bfloat16 or wider, within the bound.
No kernel may reach another device: no remote copies, remote signals or barrier semaphores. Data moves between devices by JAX's collectives and lax.ppermute only.
A program may use at most 192 MiB of HBM per device.

v0:
```python
import jax
import jax.numpy as jnp
from jax import lax
from jax.sharding import PartitionSpec as P

SLOTS = 2


beta_one = 0.9
beta_two = 0.95
learn_rate = 0.25
decay_rate = 0.01
adam_eps = 1e-08
step_count = 20.0
clip_norm = 1.0
scale_eps = 1e-06


def clip_factor(grad_total):
    return jnp.minimum(1.0, clip_norm / (jnp.sqrt(grad_total) + 1e-06))


def adam_update(master, gradient, moment_one, moment_two, factor):
    scaled = factor * gradient
    mean_new = beta_one * moment_one + (1.0 - beta_one) * scaled
    square_new = beta_two * moment_two + (1.0 - beta_two) * scaled * scaled
    corr_one = 1.0 - beta_one**step_count
    corr_two = 1.0 - beta_two**step_count
    update = mean_new / corr_one / (jnp.sqrt(square_new / corr_two) + adam_eps)
    return master - learn_rate * (update + decay_rate * master)


def quantize(master):
    weights = lax.optimization_barrier(master.astype(jnp.bfloat16)).astype(jnp.float32)
    magnitude = jnp.max(jnp.abs(weights), axis=(-2, -1))
    values = (weights / (magnitude[..., None, None] + scale_eps)).astype(jnp.bfloat16)
    return (values, magnitude)


def slot_table(owner, shard_count):
    count = owner.shape[0]
    positions = jnp.arange(count, dtype=jnp.int32)
    earlier_same = (owner[:, None] == owner[None, :]) & (positions[None, :] < positions[:, None])
    slot_rank = jnp.sum(earlier_same.astype(jnp.int32), axis=1)
    shard_ids = jnp.arange(shard_count, dtype=jnp.int32)
    slot_ids = jnp.arange(SLOTS, dtype=jnp.int32)
    matched = (owner[None, None, :] == shard_ids[:, None, None]) & (
        slot_rank[None, None, :] == slot_ids[None, :, None]
    )
    occupied = jnp.any(matched, axis=2)
    chosen = jnp.sum(matched.astype(jnp.int32) * positions[None, None, :], axis=2)
    return (chosen, occupied)


def masked(values, occupied_mask):
    view = occupied_mask.reshape(occupied_mask.shape + (1,) * (values.ndim - occupied_mask.ndim))
    return jnp.where(view, values, jnp.zeros_like(values))


def per_device(
    kv_param, kv_grad, kv_mean, kv_square, exp_param, exp_grad, exp_mean, exp_square, expert_owner
):
    local_total = jnp.sum(kv_grad * kv_grad) + jnp.sum(exp_grad * exp_grad)
    grad_total = lax.psum(local_total, ("replica", "expert", "tensor"))
    factor = clip_factor(grad_total)
    kv_param_new = adam_update(kv_param, kv_grad, kv_mean, kv_square, factor)
    exp_param_new = adam_update(exp_param, exp_grad, exp_mean, exp_square, factor)
    kv_values, kv_magnitude = quantize(kv_param_new)
    kv_rollout, kv_wire_scales = (
        lax.all_gather(kv_values, ("replica", "expert"), axis=1, tiled=True),
        lax.all_gather(
            kv_magnitude.astype(jnp.bfloat16), ("replica", "expert"), axis=1, tiled=True
        ),
    )
    exp_values, exp_magnitude = quantize(exp_param_new)
    exp_wire_scales = exp_magnitude.astype(jnp.bfloat16)
    chosen, occupied = slot_table(expert_owner, lax.axis_size("expert"))
    whole_values, whole_scales = (
        lax.all_gather(exp_values, ("replica", "expert"), axis=2, tiled=True),
        lax.all_gather(exp_wire_scales, ("replica", "expert"), axis=2, tiled=True),
    )
    shard_index = lax.axis_index("expert")
    picked = jnp.take(chosen, shard_index, axis=0)
    filled = jnp.take(occupied, shard_index, axis=0)
    exp_rollout = masked(jnp.take(whole_values, picked, axis=0), filled)
    rollout_scales = masked(jnp.take(whole_scales, picked, axis=0), filled)
    return (
        kv_param_new,
        exp_param_new,
        kv_rollout,
        kv_wire_scales.astype(jnp.float32),
        exp_rollout,
        rollout_scales.astype(jnp.float32),
    )


def solution(mesh):
    return jax.shard_map(
        per_device,
        mesh=mesh,
        in_specs=(
            P("tensor", ("replica", "expert"), None, None),
            P("tensor", ("replica", "expert"), None, None),
            P("tensor", ("replica", "expert"), None, None),
            P("tensor", ("replica", "expert"), None, None),
            P(None, "tensor", ("replica", "expert"), None, None),
            P(None, "tensor", ("replica", "expert"), None, None),
            P(None, "tensor", ("replica", "expert"), None, None),
            P(None, "tensor", ("replica", "expert"), None, None),
            P(),
        ),
        out_specs=(
            P("tensor", ("replica", "expert"), None, None),
            P(None, "tensor", ("replica", "expert"), None, None),
            P("tensor", None, None, None),
            P("tensor", None),
            P("expert", "tensor", None, None, None),
            P("expert", "tensor", None),
        ),
        check_vma=False,
    )
```

profile of v0, /device:TPU:1, one launch (start us, length us, event | category | flops | bytes accessed | tf_op | source)
XLA Modules:
  0.0 498.6 jit_solution(13228453852503958050)
XLA Ops:
  7.2 0.0 all-gather.6.cloned.1.call-start
  7.2 1.5 multiply_reduce_fusion.1
  8.8 1.9 multiply_reduce_fusion
  12.0 68.7 %psum.7 = f32[]{:T(128)} all-reduce(f32[]{:T(128)S(6)} %add.77), channel_id=1, replica_groups=mesh['replica'=16,'expert'=4,'tensor'=2] {'replica','expert','tensor'}, use_global_device_ids=true, to_apply=%region_2.0 | all-reduce | flops 1 | bytes 8 | tf_op jit(solution)/shard_map/psum | solution.py:64
  81.4 1.9 fusion.22
  83.3 0.1 fusion.9
  83.4 0.7 fusion.10
  84.1 0.0 all-gather.6.cloned.1.call-update
  84.1 0.0 all-gather.8.cloned.1.call-start
  84.2 3.4 fusion.21
  87.6 0.2 fusion.1
  87.7 0.9 fusion.2
  88.7 0.0 all-gather.8.cloned.1.call-update
  88.7 130.3 %all-gather.1 = bf16[64,1,2]{2,1,0:T(2,128)(2,1)S(1)} all-gather(bf16[1,1,2]{2,1,0:T(2,128)(2,1)S(1)} %get-tuple-element.104), channel_id=1, replica_groups=mesh['replica'=16,'expert'=4,'tensor'=2] {'replica','expert'}, dimensions={0}, use_global_device_ids=true | all-gather | bytes 260 | tf_op jit(solution)/shard_map/all_gather | solution.py:71
  219.0 0.1 copy.35
  219.1 0.1 copy.36
  219.2 137.4 %all-gather.2 = bf16[64,3,4]{2,1,0:T(4,128)(2,1)S(1)} all-gather(bf16[1,3,4]{2,1,0:T(4,128)(2,1)S(1)} %bitcast.28), channel_id=2, replica_groups=mesh['replica'=16,'expert'=4,'tensor'=2] {'replica','expert'}, dimensions={0}, use_global_device_ids=true | all-gather | bytes 1560 | tf_op jit(solution)/shard_map/all_gather | solution.py:80
  356.6 0.1 copy.39
  356.7 0.9 convert_reduce_fusion
  357.6 0.7 iota_compare_fusion.1
  358.3 0.1 fusion.17
  358.4 0.2 select_reduce_fusion.1
  358.6 0.6 gather_fusion
  359.2 0.1 and_reduce_fusion
  359.4 0.2 select_reduce_fusion
  359.6 0.1 fusion.19
  359.6 0.6 copy.38
  360.2 0.6 convert_bitcast_fusion
  360.8 0.0 all-gather.6.cloned.1.call-done
  360.8 70.7 %all-gather.8.cloned.1.call-done = bf16[4,1,192,128,128]{4,3,2,1,0:T(8,128)(2,1)} async-done(((bf16[4,1,3,128,128]{4,3,2,1,0:T(8,128)(2,1)}), bf16[4,1,192,128,128]{4,3,2,1,0:T(8,128)(2,1)}) %all-gather.8.cloned.1.call-update) | async-done | bytes 25165840 | tf_op jit(solution)/shard_map/all_gather | solution.py:79
  431.5 10.5 %mini-gather-slice.3 = bf16[4,1,64,128,128]{4,3,2,1,0:T(8,128)(2,1)} slice(bf16[4,1,192,128,128]{4,3,2,1,0:T(8,128)(2,1)} %all-gather.8.cloned.1.call-done), slice={[0:4], [0:1], [128:192], [0:128], [0:128]} | slice | bytes 16777216 | tf_op jit(solution)/shard_map/jit(_take)/gather | solution.py:85
  442.0 8.8 %while.5 = (s32[]{:T(128)}, bf16[4,1,64,128,128]{4,3,2,1,0:T(8,128)(2,1)}, s32[2,1]{0,1:T(1,128)S(1)}, bf16[2,1,64,128,128]{4,3,2,1,0:T(8,128)(2,1)}, s32[]{:T(128)}) while((s32[]{:T(128)}, bf16[4,1,64,128,128]{4,3,2,1,0:T(8,128)(2,1)}, s32[2,1]{0,1:T(1,128)S(1)}, bf16[2,1,64,128,128]{4,3,2,1,0:T(8,128)(2,1)}, s32[]{:T(128)}) %tuple.52), condition=%wide.while_cond.3, body=%wide.while_body.3.sunk | while | flops 2 | bytes 4194901 | solution.py:85
  442.0 0.6 constant_dynamic-slice_fusion.5
  442.6 3.8 dynamic-slice_dynamic-update-slice_fusion.5
  446.4 0.6 constant_dynamic-slice_fusion.5
  447.0 3.8 dynamic-slice_dynamic-update-slice_fusion.5
  450.8 14.1 %mini-gather-slice.2 = bf16[4,1,128,128,128]{4,3,2,1,0:T(8,128)(2,1)} slice(bf16[4,1,192,128,128]{4,3,2,1,0:T(8,128)(2,1)} %all-gather.8.cloned.1.call-done), slice={[0:4], [0:1], [0:128], [0:128], [0:128]} | slice | bytes 33554432 | tf_op jit(solution)/shard_map/jit(_take)/gather | solution.py:85
  464.9 11.9 %while.4 = (s32[]{:T(128)}, bf16[4,1,128,128,128]{4,3,2,1,0:T(8,128)(2,1)}, s32[2,1]{0,1:T(1,128)S(1)}, bf16[2,1,128,128,128]{4,3,2,1,0:T(8,128)(2,1)}, s32[]{:T(128)}) while((s32[]{:T(128)}, bf16[4,1,128,128,128]{4,3,2,1,0:T(8,128)(2,1)}, s32[2,1]{0,1:T(1,128)S(1)}, bf16[2,1,128,128,128]{4,3,2,1,0:T(8,128)(2,1)}, s32[]{:T(128)}) %tuple.64), condition=%wide.while_cond.2, body=%wide.while_body.2.sunk | while | flops 2 | bytes 8389205 | solution.py:85
  464.9 0.6 constant_dynamic-slice_fusion.4
  465.5 5.3 %dynamic-slice_dynamic-update-slice_fusion.4 = bf16[2,1,128,128,128]{4,3,2,1,0:T(8,128)(2,1)} fusion(bf16[2,1,128,128,128]{4,3,2,1,0:T(8,128)(2,1)} %get-tuple-element.179, s32[]{:T(128)S(6)} %copy.50, bf16[4,1,128,128,128]{4,3,2,1,0:T(8,128)(2,1)} %get-tuple-element.182, s32[]{:T(128)} %bitcast.25), kind=kLoop, calls=%fused_computation.1.clone.1 | loop fusion | bytes 8389124 | tf_op jit(solution)/shard_map/jit(_take)/gather
  470.8 0.6 constant_dynamic-slice_fusion.4
  471.4 5.4 %dynamic-slice_dynamic-update-slice_fusion.4 = bf16[2,1,128,128,128]{4,3,2,1,0:T(8,128)(2,1)} fusion(bf16[2,1,128,128,128]{4,3,2,1,0:T(8,128)(2,1)} %get-tuple-element.179, s32[]{:T(128)S(6)} %copy.50, bf16[4,1,128,128,128]{4,3,2,1,0:T(8,128)(2,1)} %get-tuple-element.182, s32[]{:T(128)} %bitcast.25), kind=kLoop, calls=%fused_computation.1.clone.1 | loop fusion | bytes 8389124 | tf_op jit(solution)/shard_map/jit(_take)/gather
  476.7 0.0 copy-start
  476.7 13.0 %fusion = bf16[2,1,192,128,128]{4,3,2,1,0:T(8,128)(2,1)} fusion(bf16[2,1,64,128,128]{4,3,2,1,0:T(8,128)(2,1)} %get-tuple-element.37, bf16[2,1,128,128,128]{4,3,2,1,0:T(8,128)(2,1)} %get-tuple-element.29, pred[2]{0:T(512)(128)(4,1)S(1)} %compare_and_fusion, pred[2]{0:T(512)(128)(4,1)S(1)} %select_reduce_fusion), kind=kLoop, calls=%fused_computation.6 | loop fusion | flops 18874368 | bytes 25165828 | tf_op jit(solution)/shard_map/jit(_where)/select_n | solution.py:57
  489.7 0.0 copy-done
  489.8 2.0 copy.56
  (9 shorter events, 0.1 us)
Async XLA Ops:
  7.2 353.6 %all-gather.6.cloned.1.call-start = ((), (), s32[]{:S(2)}) async-start(), calls=%async_computation | async-start | bytes 4259840 | tf_op jit(solution)/shard_map/all_gather | solution.py:70
  84.1 347.4 %all-gather.8.cloned.1.call-start = ((), (), s32[]{:S(2)}) async-start(), calls=%async_computation.1 | async-start | bytes 25559040 | tf_op jit(solution)/shard_map/all_gather | solution.py:79
  476.7 13.0 %copy-start = (bf16[2,64,128,128]{3,2,1,0:T(8,128)(2,1)S(1)}, bf16[2,64,128,128]{3,2,1,0:T(8,128)(2,1)}, u32[]{:S(2)}) copy-start(bf16[2,64,128,128]{3,2,1,0:T(8,128)(2,1)} %all-gather.6.cloned.1.call-done) | copy-start | bytes 12582916
Sparse Core Ops, SparseCore 0:
  84.3 157.0 all-gather.5
  243.6 187.8 all-gather.7
where the time goes:
time: 499 us
  blocking collectives  336 us (67%)
  waiting for transfers between devices  70.8 us (14%)
  local copies, waits for them, and re-layouts  48.7 us (10%)
  other arithmetic  26.6 us (5%)
  between operations  16.1 us (3%)
    all_gather x1, blocking collectives, per_device(): lax.all_gather(exp_wire_scales, ('replica', 'expert'), axis=2, tiled=True)  137 us
    all_gather x1, blocking collectives, per_device(): lax.all_gather(kv_magnitude.astype(jnp.bfloat16), ('replica', 'expert'),...  130 us
    all_gather x1, waiting for transfers between devices, per_device(): lax.all_gather(exp_values, ('replica', 'expert'), axis=2, tiled=True)  70.7 us
    psum x1, blocking collectives, per_device(): grad_total = lax.psum(local_total, ('replica', 'expert', 'tensor'))  68.7 us
    gather x2, local copies, waits for them, and re-layouts, per_device(): exp_rollout = masked(jnp.take(whole_values, picked, axis=0), filled)  24.6 us
    gather x8, local copies, waits for them, and re-layouts  20.6 us
    select_n x1, other arithmetic, masked(): return jnp.where(view, values, jnp.zeros_like(values))  13 us
  transfers between devices with their start and end apart: 2, of which 1 were waited for; matrix products, arithmetic and copies ran while one was open for 2% of the time, Pallas kernels for 0%

commit v1 on v0

v1 whole, which is shorter than its diff:
```python
import jax
import jax.numpy as jnp
from jax import lax
from jax.experimental import pallas as pl
from jax.experimental.pallas import tpu as pltpu
from jax.sharding import Mesh, PartitionSpec as P

SLOTS = 2
EXPERTS = 4
BLK = 128
LANES = 128

beta_one = 0.9
beta_two = 0.95
learn_rate = 0.25
decay_rate = 0.01
adam_eps = 1e-08
step_count = 20.0
clip_norm = 1.0
scale_eps = 1e-06

REPLICA = ("x", "yl", "c")
SHARD = ("x", "yl", "c", "z")
VMEM = pltpu.VMEM
SMEM = pltpu.SMEM


def ring(n, k):
    return [(i, (i + k) % n) for i in range(n)]


def sum_of_squares(kv_grad, exp_grad):
    def kernel(kv_ref, exp_ref, out_ref):
        total = jnp.zeros((8, LANES), jnp.float32)
        for i in range(2):
            g = kv_ref[i, 0]
            total += jnp.sum((g * g).reshape(BLK // 8, 8, LANES), axis=0)
        for e in range(EXPERTS):
            for j in range(3):
                g = exp_ref[e, 0, j]
                total += jnp.sum((g * g).reshape(BLK // 8, 8, LANES), axis=0)
        out_ref[...] = total

    return pl.pallas_call(
        kernel,
        out_shape=jax.ShapeDtypeStruct((8, LANES), jnp.float32),
        in_specs=[pl.BlockSpec(memory_space=VMEM)] * 2,
        out_specs=pl.BlockSpec(memory_space=VMEM),
        name="sum_of_squares",
    )(kv_grad, exp_grad)


def sum_over_devices(v):
    for axis in ("c", "yl", "yh"):
        v = v + lax.ppermute(v, axis, ring(2, 1))
    for axis in ("x", "z"):
        others = [lax.ppermute(v, axis, ring(4, k)) for k in (1, 2, 3)]
        v = v + others[0] + others[1] + others[2]
    return v


def adam(master, gradient, moment_one, moment_two, factor):
    scaled = factor * gradient
    mean_new = beta_one * moment_one + (1.0 - beta_one) * scaled
    square_new = beta_two * moment_two + (1.0 - beta_two) * scaled * scaled
    corr_one = 1.0 - beta_one**step_count
    corr_two = 1.0 - beta_two**step_count
    update = mean_new / corr_one / (jnp.sqrt(square_new / corr_two) + adam_eps)
    return master - learn_rate * (update + decay_rate * master)


def slot_of(owner, shard, slot):
    chosen = jnp.int32(0)
    occupied = jnp.int32(0)
    for e in range(EXPERTS):
        rank = jnp.int32(0)
        for f in range(e):
            rank += (owner[f] == owner[e]).astype(jnp.int32)
        matched = jnp.logical_and(owner[e] == shard, rank == slot).astype(jnp.int32)
        chosen += matched * e
        occupied += matched
    return chosen, occupied


def update(place, owner, total, kv, exp):
    def kernel(place_ref, owner_ref, total_ref, *refs):
        kv_in, exp_in = refs[0:4], refs[4:8]
        kv_new, exp_new, kv_val, routed, scales, values = refs[8:]
        norm = jnp.sqrt(jnp.sum(total_ref[...], keepdims=True)) + 1e-06
        factor = jnp.minimum(1.0, clip_norm / norm)
        lane = lax.broadcasted_iota(jnp.int32, (1, LANES), 1)
        mine = lane == place_ref[0]
        scales[...] = jnp.zeros_like(scales)

        def block(ins, out, val, at, to, row):
            new = adam(ins[0][at], ins[1][at], ins[2][at], ins[3][at], factor)
            out[at] = new
            weights = new.astype(jnp.bfloat16).astype(jnp.float32)
            magnitude = jnp.max(jnp.abs(weights), keepdims=True)
            val[to] = (weights / (magnitude + scale_eps)).astype(jnp.bfloat16)
            scales[pl.ds(row, 1), :] = jnp.where(mine, magnitude, 0.0)

        for i in range(2):
            block(kv_in, kv_new, kv_val, (i, 0), (i, 0), i)
        for e in range(EXPERTS):
            for j in range(3):
                block(exp_in, exp_new, values, (e, 0, j), (e, j), 2 + 3 * e + j)
        owners = [owner_ref[e] for e in range(EXPERTS)]
        for z in range(4):
            for s in range(SLOTS):
                chosen, occupied = slot_of(owners, z, s)
                picked = values[chosen]
                routed[z, s] = jnp.where(occupied > 0, picked, jnp.zeros_like(picked))

    f32, bf16 = jnp.float32, jnp.bfloat16
    return pl.pallas_call(
        kernel,
        out_shape=(
            jax.ShapeDtypeStruct((2, 1, BLK, BLK), f32),
            jax.ShapeDtypeStruct((EXPERTS, 1, 3, BLK, BLK), f32),
            jax.ShapeDtypeStruct((2, 1, BLK, BLK), bf16),
            jax.ShapeDtypeStruct((4, SLOTS, 3, BLK, BLK), bf16),
            jax.ShapeDtypeStruct((16, LANES), f32),
        ),
        in_specs=[pl.BlockSpec(memory_space=SMEM)] * 2 + [pl.BlockSpec(memory_space=VMEM)] * 9,
        out_specs=[pl.BlockSpec(memory_space=VMEM)] * 5,
        scratch_shapes=[pltpu.VMEM((EXPERTS, 3, BLK, BLK), bf16)],
        compiler_params=pltpu.CompilerParams(vmem_limit_bytes=32 * 1024 * 1024),
        name="update",
    )(place, owner, total, *kv, *exp)


def per_device(
    kv_param, kv_grad, kv_mean, kv_square, exp_param, exp_grad, exp_mean, exp_square, expert_owner
):
    total = sum_over_devices(sum_of_squares(kv_grad, exp_grad))
    place = lax.axis_index(SHARD).astype(jnp.int32).reshape(1)
    kv_new, exp_new, kv_val, routed, scales = update(
        place,
        expert_owner,
        total,
        (kv_param, kv_grad, kv_mean, kv_square),
        (exp_param, exp_grad, exp_mean, exp_square),
    )
    arrived = lax.all_to_all(routed, "z", 0, 0, tiled=True)
    arrived = arrived.transpose(1, 0, 2, 3, 4).reshape(SLOTS, 1, 12, BLK, BLK)
    exp_rollout = lax.all_gather(arrived, REPLICA, axis=2, tiled=True)
    kv_plane = lax.all_gather(kv_val, "z", axis=1, tiled=True)
    kv_rollout = lax.all_gather(kv_plane, REPLICA, axis=1, tiled=True)
    for axis in ("c", "x", "yl", "z"):
        scales = lax.psum(scales, axis)
    kv_scales = scales[0:2, 0:64]
    by_expert = scales[2:14, 0:64].reshape(EXPERTS, 3, 64).transpose(0, 2, 1).reshape(EXPERTS, 192)
    shard = lax.axis_index("z").astype(jnp.int32)
    rows = []
    for s in range(SLOTS):
        chosen, occupied = slot_of(expert_owner, shard, s)
        row = lax.dynamic_index_in_dim(by_expert, chosen, 0, keepdims=False)
        rows.append(jnp.where(occupied > 0, row, 0.0))
    exp_scales = jnp.stack(rows).reshape(SLOTS, 1, 192)
    return kv_new, exp_new, kv_rollout, kv_scales, exp_rollout, exp_scales


def solution(mesh):
    fine = Mesh(mesh.devices.reshape(4, 2, 2, 4, 2), ("x", "yl", "c", "z", "yh"))
    kv = P("yh", SHARD, None, None)
    exp = P(None, "yh", SHARD, None, None)
    return jax.shard_map(
        per_device,
        mesh=fine,
        in_specs=(kv, kv, kv, kv, exp, exp, exp, exp, P()),
        out_specs=(
            kv,
            exp,
            P("yh", None, None, None),
            P("yh", None),
            P("z", "yh", None, None, None),
            P("z", "yh", None),
        ),
        check_vma=False,
    )
```

time: 499 us -> 198 us (0.40)
  blocking collectives: 336 us -> 53.4 us
  other arithmetic: 26.6 us -> 0.73 us
  local copies, waits for them, and re-layouts: 48.7 us -> 28.1 us
  starting transfers between devices: 0.08 us -> 16.1 us
  between operations: 16.1 us -> 24.2 us
    all_gather x2 -> x1, blocking collectives: 268 us -> 10.1 us  [per_device(): kv_plane = lax.all_gather(kv_val, 'z', axis=1, tiled=True)]
    gather x11 -> x0, local copies, waits for them, and re-layouts: 45.8 us -> none  [the longest x2 24.6 us: per_device(): exp_rollout = masked(jnp.take(whole_values, picked, axis=0), filled)]
    psum x1 -> x4, blocking collectives: 68.7 us -> 31.6 us  [per_device(): scales = lax.psum(scales, axis)]
    unnamed x7 -> x21, local copies, waits for them, and re-layouts: 2.84 us -> 24.9 us
    ppermute x0 -> x9, starting transfers between devices: none -> 16 us  [the longest x6 10.2 us: sum_over_devices(): others = [lax.ppermute(v, axis, ring(4, k)) for k in (1, 2, 3)]]
    select_n x4 -> x1, other arithmetic: 13.4 us -> 0.01 us  [per_device(): rows.append(jnp.where(occupied > 0, row, 0.0))]
    all_to_all x0 -> x1, blocking collectives: none -> 11.7 us  [per_device(): arrived = lax.all_to_all(routed, 'z', 0, 0, tiled=True)]
    convert_element_type x6 -> x0, other arithmetic: 7.53 us -> none  [the longest x2 5.25 us: quantize(): master.astype(jnp.bfloat16)]
  transfers between devices with their start and end apart: 2 -> 11, of which waited for: 1 -> 8; matrix products, arithmetic and copies ran while one was open for 2% -> 2% of each run, Pallas kernels for 0% -> 0%
where the time goes in v1:
time: 198 us; the launch traced here: 197 us
  waiting for transfers between devices  70 us (35%)
  blocking collectives  53.4 us (27%)
  local copies, waits for them, and re-layouts  28.1 us (14%)
  between operations  24.2 us (12%)
  starting transfers between devices  16.1 us (8%)
  Pallas kernels  4.57 us (2%)
    all_gather x1, waiting for transfers between devices, per_device(): exp_rollout = lax.all_gather(arrived, REPLICA, axis=2, tiled=True)  63.5 us
    psum x4, blocking collectives, per_device(): scales = lax.psum(scales, axis)  31.6 us
    unnamed x21, local copies, waits for them, and re-layouts  24.9 us
    all_to_all x1, blocking collectives, per_device(): arrived = lax.all_to_all(routed, 'z', 0, 0, tiled=True)  11.7 us
    ppermute x6, starting transfers between devices, sum_over_devices(): others = [lax.ppermute(v, axis, ring(4, k)) for k in (1, 2, 3)]  10.2 us
    all_gather x1, blocking collectives, per_device(): kv_plane = lax.all_gather(kv_val, 'z', axis=1, tiled=True)  10.1 us
    ppermute x3, starting transfers between devices, sum_over_devices(): v = v + lax.ppermute(v, axis, ring(2, 1))  5.8 us
  transfers between devices with their start and end apart: 11, of which 8 were waited for; matrix products, arithmetic and copies ran while one was open for 2% of the time, Pallas kernels for 0%

profile of v1, /device:TPU:1, one launch (start us, length us, event | category | flops | bytes accessed | tf_op | source)
XLA Modules:
  0.0 197.1 jit_solution(7269520358179918482)
XLA Ops:
  7.2 0.0 all-gather.3.cloned.1.call-start
  7.2 1.9 sum_of_squares.1
  9.1 1.4 collective-permute-start
  10.5 1.0 collective-permute-done
  11.5 0.7 add.93
  12.2 1.4 collective-permute-start.1
  13.6 1.1 collective-permute-done.1
  14.7 3.0 %collective-permute-start.2 = (f32[8,128]{1,0:T(8,128)S(1)}, f32[8,128]{1,0:T(8,128)S(1)}, u32[]{:S(2)}, u32[]{:S(2)}) collective-permute-start(f32[8,128]{1,0:T(8,128)S(1)} %add.94), channel_id=1, source_target_pairs={{0,1},{1,0},{2,3},{3,2},{4,5},{5,4},{6,7},{7,6},{8,9},{9,8},{10,11... | collective-permute-start | bytes 12296 | tf_op jit(solution)/shard_map/ppermute | solution.py:55
  17.7 1.0 collective-permute-done.2
  18.7 1.3 collective-permute-start.3
  20.0 2.5 %collective-permute-start.4 = (f32[8,128]{1,0:T(8,128)S(1)}, f32[8,128]{1,0:T(8,128)S(1)}, u32[]{:S(2)}, u32[]{:S(2)}) collective-permute-start(f32[8,128]{1,0:T(8,128)S(1)} %add.95), channel_id=1, source_target_pairs={{0,64},{32,96},{64,0},{96,32},{1,65},{33,97},{65,1},{97,33},{2,66}... | collective-permute-start | bytes 12296 | tf_op jit(solution)/shard_map/ppermute | solution.py:57
  22.4 1.2 collective-permute-start.5
  23.6 0.0 collective-permute-done.3
  23.6 0.4 collective-permute-done.4
  23.9 1.2 collective-permute-done.5
  25.2 1.3 collective-permute-start.6
  26.5 3.3 %collective-permute-start.7 = (f32[8,128]{1,0:T(8,128)S(1)}, f32[8,128]{1,0:T(8,128)S(1)}, u32[]{:S(2)}, u32[]{:S(2)}) collective-permute-start(f32[8,128]{1,0:T(8,128)S(1)} %add_add_fusion.1), channel_id=1, source_target_pairs={{0,4},{2,6},{4,0},{6,2},{1,5},{3,7},{5,1},{7,3},{8,12},{10,14},{12... | collective-permute-start | bytes 12296 | tf_op jit(solution)/shard_map/ppermute | solution.py:57
  29.8 0.7 collective-permute-start.8
  30.5 0.0 collective-permute-done.6
  30.5 0.3 collective-permute-done.7
  30.8 1.4 collective-permute-done.8
  32.3 0.0 copy-start
  32.3 1.1 copy-done
  33.4 0.0 copy-start.1
  33.4 1.1 copy-done.1
  34.5 0.0 copy-start.2
  34.5 1.1 copy-done.2
  35.7 0.0 copy-start.3
  35.7 1.1 copy-done.3
  36.8 0.0 copy-start.4
  36.8 0.9 copy-done.4
  37.7 0.0 copy-start.5
  37.7 0.9 copy-done.5
  38.6 0.0 copy-start.6
  38.6 0.9 copy-done.6
  39.5 0.0 copy-start.7
  39.5 0.9 copy-done.7
  40.4 0.0 copy-start.8
  40.4 0.7 copy-done.8
  41.1 2.7 %update.1 = (f32[2,1,128,128]{3,2,1,0:T(8,128)}, f32[4,1,3,128,128]{4,3,2,1,0:T(8,128)}, bf16[2,1,128,128]{3,2,1,0:T(8,128)(2,1)S(1)}, bf16[4,2,3,128,128]{4,3,2,1,0:T(8,128)(2,1)S(1)}, f32[16,128]{1,0:T(8,128)S(1)}) custom-call(s32[1]{0:T(128)} %bitcast.place_ref, s32[4]{0:T(128)S(1)} %copy-done.8, f32[8,128]{1,0:T(8,128)S(1)} %add_add_fusion.total_ref, ...), custom_call_target="tpu_custom_call" | custom-call | tf_op jit(solution)/shard_map/update/pallas_call | solution.py:116
  43.8 10.1 %all_gather.9 = bf16[2,4,128,128]{3,2,1,0:T(8,128)(2,1)} all-gather(bf16[2,1,128,128]{3,2,1,0:T(8,128)(2,1)S(1)} %get-tuple-element.13), channel_id=1, replica_groups=mesh['x'=4,'yl'=2,'c'=2,'z'=4,'yh'=2] {'z'}, dimensions={1}, use_global_device_ids=true | all-gather | bytes 327680 | tf_op jit(solution)/shard_map/all_gather | solution.py:148
  53.9 0.0 all-gather.3.cloned.1.call-update
  53.9 0.0 all-gather.5.cloned.1.call-start
  53.9 11.7 %all_to_all.5 = bf16[4,2,3,128,128]{4,3,2,1,0:T(8,128)(2,1)S(1)} all-to-all(bf16[4,2,3,128,128]{4,3,2,1,0:T(8,128)(2,1)S(1)} %get-tuple-element.15), channel_id=1, replica_groups=mesh['x'=4,'yl'=2,'c'=2,'z'=4,'yh'=2] {'z'}, dimensions={0} | all-to-all | bytes 1572864 | tf_op jit(solution)/shard_map/all_to_all | solution.py:145
  65.7 1.0 copy.16
  66.6 0.0 all-gather.5.cloned.1.call-update
  66.6 1.4 fusion
  78.1 12.3 %psum.28 = f32[16,128]{1,0:T(8,128)S(1)} all-reduce(f32[16,128]{1,0:T(8,128)S(1)} %get-tuple-element.14), channel_id=1, replica_groups=mesh['x'=4,'yl'=2,'c'=2,'z'=4,'yh'=2] {'c'}, use_global_device_ids=true, to_apply=%region_0.0 | all-reduce | flops 2048 | bytes 16384 | tf_op jit(solution)/shard_map/psum | solution.py:151
  90.4 8.4 %psum.29 = f32[16,128]{1,0:T(8,128)S(1)} all-reduce(f32[16,128]{1,0:T(8,128)S(1)} %psum.28), channel_id=1, replica_groups=mesh['x'=4,'yl'=2,'c'=2,'z'=4,'yh'=2] {'x'}, use_global_device_ids=true, to_apply=%region_1.0 | all-reduce | flops 2048 | bytes 16384 | tf_op jit(solution)/shard_map/psum | solution.py:151
  98.9 3.9 %psum.30 = f32[16,128]{1,0:T(8,128)S(1)} all-reduce(f32[16,128]{1,0:T(8,128)S(1)} %psum.29), channel_id=1, replica_groups=mesh['x'=4,'yl'=2,'c'=2,'z'=4,'yh'=2] {'yl'}, use_global_device_ids=true, to_apply=%region_2.0 | all-reduce | flops 2048 | bytes 16384 | tf_op jit(solution)/shard_map/psum | solution.py:151
  102.7 7.0 %psum.31 = f32[16,128]{1,0:T(8,128)S(1)} all-reduce(f32[16,128]{1,0:T(8,128)S(1)} %psum.30), channel_id=1, replica_groups=mesh['x'=4,'yl'=2,'c'=2,'z'=4,'yh'=2] {'z'}, use_global_device_ids=true, to_apply=%region_3.0 | all-reduce | flops 2048 | bytes 16384 | tf_op jit(solution)/shard_map/psum | solution.py:151
  109.7 0.6 slice.18
  110.3 0.1 copy.17
  110.4 0.1 reshape.30
  110.6 0.6 copy.19
  111.2 0.0 all-gather.3.cloned.1.call-done
  111.2 63.5 %all-gather.5.cloned.1.call-done = bf16[2,1,192,128,128]{4,3,2,0,1:T(8,128)(2,1)} async-done(((bf16[2,1,12,128,128]{4,3,2,0,1:T(8,128)(2,1)}), bf16[2,1,192,128,128]{4,3,2,0,1:T(8,128)(2,1)}) %all-gather.5.cloned.1.call-update) | async-done | bytes 12582928 | tf_op jit(solution)/shard_map/all_gather | solution.py:147
  174.7 4.8 %copy.22 = bf16[2,64,128,128]{3,2,1,0:T(8,128)(2,1)} copy(bf16[2,64,128,128]{3,2,1,0:T(8,128)(2,1)} %all-gather.3.cloned.1.call-done) | data formatting | bytes 8388608
  179.5 10.7 %copy.23 = bf16[2,1,192,128,128]{4,3,2,1,0:T(8,128)(2,1)} copy(bf16[2,1,192,128,128]{4,3,2,1,0:T(8,128)(2,1)} %bitcast.11) | data formatting | bytes 25165824
  (8 shorter events, 0.1 us)
Async XLA Ops:
  7.2 104.0 %all-gather.3.cloned.1.call-start = ((), (), s32[]{:S(2)}) async-start(), calls=%async_computation.1 | async-start | bytes 4456448 | tf_op jit(solution)/shard_map/all_gather | solution.py:149
  9.1 2.5 %collective-permute-start = (f32[8,128]{1,0:T(8,128)}, f32[8,128]{1,0:T(8,128)S(1)}, u32[]{:S(2)}, u32[]{:S(2)}) collective-permute-start(f32[8,128]{1,0:T(8,128)} %sum_of_squares.1), channel_id=1, source_target_pairs={{0,8},{8,0},{1,9},{9,1},{2,10},{10,2},{3,11},{11,3},{4,12},{12,4},... | collective-permute-start | bytes 12296 | tf_op jit(solution)/shard_map/ppermute | solution.py:55
  12.2 2.5 %collective-permute-start.1 = (f32[8,128]{1,0:T(8,128)S(1)}, f32[8,128]{1,0:T(8,128)S(1)}, u32[]{:S(2)}, u32[]{:S(2)}) collective-permute-start(f32[8,128]{1,0:T(8,128)S(1)} %add.93), channel_id=1, source_target_pairs={{0,16},{16,0},{1,17},{17,1},{2,18},{18,2},{3,19},{19,3},{4,20},{20... | collective-permute-start | bytes 12296 | tf_op jit(solution)/shard_map/ppermute | solution.py:55
  14.7 4.0 %collective-permute-start.2 = (f32[8,128]{1,0:T(8,128)S(1)}, f32[8,128]{1,0:T(8,128)S(1)}, u32[]{:S(2)}, u32[]{:S(2)}) collective-permute-start(f32[8,128]{1,0:T(8,128)S(1)} %add.94), channel_id=1, source_target_pairs={{0,1},{1,0},{2,3},{3,2},{4,5},{5,4},{6,7},{7,6},{8,9},{9,8},{10,11... | collective-permute-start | bytes 12296 | tf_op jit(solution)/shard_map/ppermute | solution.py:55
  18.7 4.9 %collective-permute-start.3 = (f32[8,128]{1,0:T(8,128)S(1)}, f32[8,128]{1,0:T(8,128)S(1)}, u32[]{:S(2)}, u32[]{:S(2)}) collective-permute-start(f32[8,128]{1,0:T(8,128)S(1)} %add.95), channel_id=1, source_target_pairs={{0,32},{32,64},{64,96},{96,0},{1,33},{33,65},{65,97},{97,1},{2,34}... | collective-permute-start | bytes 12296 | tf_op jit(solution)/shard_map/ppermute | solution.py:57
  20.0 4.0 %collective-permute-start.4 = (f32[8,128]{1,0:T(8,128)S(1)}, f32[8,128]{1,0:T(8,128)S(1)}, u32[]{:S(2)}, u32[]{:S(2)}) collective-permute-start(f32[8,128]{1,0:T(8,128)S(1)} %add.95), channel_id=1, source_target_pairs={{0,64},{32,96},{64,0},{96,32},{1,65},{33,97},{65,1},{97,33},{2,66}... | collective-permute-start | bytes 12296 | tf_op jit(solution)/shard_map/ppermute | solution.py:57
  22.4 2.8 %collective-permute-start.5 = (f32[8,128]{1,0:T(8,128)S(1)}, f32[8,128]{1,0:T(8,128)S(1)}, u32[]{:S(2)}, u32[]{:S(2)}) collective-permute-start(f32[8,128]{1,0:T(8,128)S(1)} %add.95), channel_id=1, source_target_pairs={{0,96},{32,0},{64,32},{96,64},{1,97},{33,1},{65,33},{97,65},{2,98}... | collective-permute-start | bytes 12296 | tf_op jit(solution)/shard_map/ppermute | solution.py:57
  25.2 5.4 %collective-permute-start.6 = (f32[8,128]{1,0:T(8,128)S(1)}, f32[8,128]{1,0:T(8,128)S(1)}, u32[]{:S(2)}, u32[]{:S(2)}) collective-permute-start(f32[8,128]{1,0:T(8,128)S(1)} %add_add_fusion.1), channel_id=1, source_target_pairs={{0,2},{2,4},{4,6},{6,0},{1,3},{3,5},{5,7},{7,1},{8,10},{10,12},{12... | collective-permute-start | bytes 12296 | tf_op jit(solution)/shard_map/ppermute | solution.py:57
  26.5 4.3 %collective-permute-start.7 = (f32[8,128]{1,0:T(8,128)S(1)}, f32[8,128]{1,0:T(8,128)S(1)}, u32[]{:S(2)}, u32[]{:S(2)}) collective-permute-start(f32[8,128]{1,0:T(8,128)S(1)} %add_add_fusion.1), channel_id=1, source_target_pairs={{0,4},{2,6},{4,0},{6,2},{1,5},{3,7},{5,1},{7,3},{8,12},{10,14},{12... | collective-permute-start | bytes 12296 | tf_op jit(solution)/shard_map/ppermute | solution.py:57
  29.8 2.5 %collective-permute-start.8 = (f32[8,128]{1,0:T(8,128)S(1)}, f32[8,128]{1,0:T(8,128)S(1)}, u32[]{:S(2)}, u32[]{:S(2)}) collective-permute-start(f32[8,128]{1,0:T(8,128)S(1)} %add_add_fusion.1), channel_id=1, source_target_pairs={{0,6},{2,0},{4,2},{6,4},{1,7},{3,1},{5,3},{7,5},{8,14},{10,8},{12,... | collective-permute-start | bytes 12296 | tf_op jit(solution)/shard_map/ppermute | solution.py:57
  32.3 1.1 copy-start
  33.4 1.1 copy-start.1
  34.5 1.1 copy-start.2
  35.7 1.1 copy-start.3
  36.8 0.9 copy-start.4
  37.7 0.9 copy-start.5
  38.6 0.9 copy-start.6
  39.5 0.9 copy-start.7
  40.4 0.7 copy-start.8
  53.9 120.8 %all-gather.5.cloned.1.call-start = ((), (), s32[]{:S(2)}) async-start(), calls=%async_computation.2 | async-start | bytes 13369344 | tf_op jit(solution)/shard_map/all_gather | solution.py:147
Sparse Core Ops, SparseCore 0:
  54.0 46.2 all-gather.2
  102.5 72.1 all-gather.4

commit v2 on v1

--- a/solution.py
+++ b/solution.py
@@ -23,6 +23,11 @@
 SHARD = ("x", "yl", "c", "z")
 VMEM = pltpu.VMEM
 SMEM = pltpu.SMEM
+
+TILE = 16
+EXP_T, KV_T = 24, 8
+PART_T = EXP_T + KV_T + 1
+FULL_T = 4 * (EXP_T + KV_T) + 1
 
 
 def ring(n, k):
@@ -84,33 +89,69 @@
 
 def update(place, owner, total, kv, exp):
     def kernel(place_ref, owner_ref, total_ref, *refs):
-        kv_in, exp_in = refs[0:4], refs[4:8]
-        kv_new, exp_new, kv_val, routed, scales, values = refs[8:]
+        kv_hbm, exp_hbm = refs[0:4], refs[4:8]
+        kv_new, exp_new = refs[8:10]
+        parts = refs[10:14]
+        kv_in, exp_in, kv_val, values, sems = refs[14:]
+        kv_copies = [
+            pltpu.make_async_copy(kv_hbm[a], kv_in.at[a], sems.at[EXPERTS, a]) for a in range(4)
+        ]
+        exp_copies = [
+            [
+                pltpu.make_async_copy(exp_hbm[a].at[e, 0], exp_in.at[a, e], sems.at[e, a])
+                for a in range(4)
+            ]
+            for e in range(EXPERTS)
+        ]
+        for copies in [kv_copies] + exp_copies:
+            for copy in copies:
+                copy.start()
         norm = jnp.sqrt(jnp.sum(total_ref[...], keepdims=True)) + 1e-06
         factor = jnp.minimum(1.0, clip_norm / norm)
-        lane = lax.broadcasted_iota(jnp.int32, (1, LANES), 1)
-        mine = lane == place_ref[0]
-        scales[...] = jnp.zeros_like(scales)
-
-        def block(ins, out, val, at, to, row):
-            new = adam(ins[0][at], ins[1][at], ins[2][at], ins[3][at], factor)
-            out[at] = new
+        row = lax.broadcasted_iota(jnp.int32, (TILE, LANES), 0)
+        flat = row * LANES + lax.broadcasted_iota(jnp.int32, (TILE, LANES), 1)
+
+        def block(ins, at):
+            new = adam(ins[0, *at], ins[1, *at], ins[2, *at], ins[3, *at], factor)
             weights = new.astype(jnp.bfloat16).astype(jnp.float32)
             magnitude = jnp.max(jnp.abs(weights), keepdims=True)
-            val[to] = (weights / (magnitude + scale_eps)).astype(jnp.bfloat16)
-            scales[pl.ds(row, 1), :] = jnp.where(mine, magnitude, 0.0)
-
+            scaled = weights / (magnitude + scale_eps)
+            return new, scaled.reshape(BLK // TILE, TILE, LANES).astype(jnp.bfloat16), magnitude
+
+        for copy in kv_copies:
+            copy.wait()
+        kv_mag = []
         for i in range(2):
-            block(kv_in, kv_new, kv_val, (i, 0), (i, 0), i)
+            new, val, magnitude = block(kv_in, (i, 0))
+            kv_new[i, 0] = new
+            kv_val[i] = val
+            kv_mag.append(magnitude)
+        exp_mag = []
         for e in range(EXPERTS):
+            for copy in exp_copies[e]:
+                copy.wait()
             for j in range(3):
-                block(exp_in, exp_new, values, (e, 0, j), (e, j), 2 + 3 * e + j)
+                new, val, magnitude = block(exp_in, (e, j))
+                exp_new[e, 0, j] = new
+                values[e, 8 * j : 8 * j + 8] = val
+                exp_mag.append(magnitude)
+        place = place_ref[0]
+        shard = lax.rem(place, 4)
         owners = [owner_ref[e] for e in range(EXPERTS)]
-        for z in range(4):
-            for s in range(SLOTS):
-                chosen, occupied = slot_of(owners, z, s)
+        for k in range(4):
+            for h in range(SLOTS):
+                chosen, occupied = slot_of(owners, lax.rem(shard + k, 4), h)
                 picked = values[chosen]
-                routed[z, s] = jnp.where(occupied > 0, picked, jnp.zeros_like(picked))
+                parts[k][h, 0:EXP_T] = jnp.where(occupied > 0, picked, jnp.zeros_like(picked))
+                parts[k][h, EXP_T : EXP_T + KV_T] = kv_val[h]
+                tile = jnp.where(flat == 2 * LANES + place, kv_mag[h], 0.0)
+                for j in range(3):
+                    magnitude = jnp.zeros((1, 1), jnp.float32)
+                    for e in range(EXPERTS):
+                        held = jnp.logical_and(chosen == e, occupied > 0)
+                        magnitude = jnp.where(held, exp_mag[3 * e + j], magnitude)
+                    tile = jnp.where(flat == place * 3 + j, magnitude, tile)
+                parts[k][h, EXP_T + KV_T] = tile.astype(jnp.bfloat16)
 
     f32, bf16 = jnp.float32, jnp.bfloat16
     return pl.pallas_call(
@@ -118,16 +159,168 @@
         out_shape=(
             jax.ShapeDtypeStruct((2, 1, BLK, BLK), f32),
             jax.ShapeDtypeStruct((EXPERTS, 1, 3, BLK, BLK), f32),
-            jax.ShapeDtypeStruct((2, 1, BLK, BLK), bf16),
-            jax.ShapeDtypeStruct((4, SLOTS, 3, BLK, BLK), bf16),
-            jax.ShapeDtypeStruct((16, LANES), f32),
-        ),
-        in_specs=[pl.BlockSpec(memory_space=SMEM)] * 2 + [pl.BlockSpec(memory_space=VMEM)] * 9,
-        out_specs=[pl.BlockSpec(memory_space=VMEM)] * 5,
-        scratch_shapes=[pltpu.VMEM((EXPERTS, 3, BLK, BLK), bf16)],
-        compiler_params=pltpu.CompilerParams(vmem_limit_bytes=32 * 1024 * 1024),
+        )
+        + (jax.ShapeDtypeStruct((SLOTS, PART_T, TILE, LANES), bf16),) * 4,
+        in_specs=[pl.BlockSpec(memory_space=SMEM)] * 2
+        + [pl.BlockSpec(memory_space=VMEM)]
+        + [pl.BlockSpec(memory_space=pl.ANY)] * 8,
+        out_specs=[pl.BlockSpec(memory_space=VMEM)] * 6,
+        scratch_shapes=[
+            pltpu.VMEM((4, 2, 1, BLK, BLK), f32),
+            pltpu.VMEM((4, EXPERTS, 3, BLK, BLK), f32),
+            pltpu.VMEM((2, KV_T, TILE, LANES), bf16),
+            pltpu.VMEM((EXPERTS, EXP_T, TILE, LANES), bf16),
+            pltpu.SemaphoreType.DMA((EXPERTS + 1, 4)),
+        ],
+        compiler_params=pltpu.CompilerParams(vmem_limit_bytes=48 * 1024 * 1024),
         name="update",
     )(place, owner, total, *kv, *exp)
+
+
+def join(place, parts):
+    def kernel(place_ref, *refs):
+        out = refs[4]
+        shard = lax.rem(place_ref[0], 4)
+        for h in range(SLOTS):
+            tile = jnp.zeros((TILE, LANES), jnp.float32)
+            for k in range(4):
+                z = lax.rem(shard - k + 4, 4)
+                out[h, pl.ds(z * EXP_T, EXP_T)] = refs[k][h, 0:EXP_T]
+                out[h, pl.ds(4 * EXP_T + z * KV_T, KV_T)] = refs[k][h, EXP_T : EXP_T + KV_T]
+                tile += refs[k][h, EXP_T + KV_T].astype(jnp.float32)
+            out[h, FULL_T - 1] = tile.astype(jnp.bfloat16)
+
+    return pl.pallas_call(
+        kernel,
+        out_shape=jax.ShapeDtypeStruct((SLOTS, FULL_T, TILE, LANES), jnp.bfloat16),
+        in_specs=[pl.BlockSpec(memory_space=SMEM)] + [pl.BlockSpec(memory_space=VMEM)] * 4,
+        out_specs=pl.BlockSpec(memory_space=VMEM),
+        compiler_params=pltpu.CompilerParams(vmem_limit_bytes=16 * 1024 * 1024),
+        name="join",
+    )(place, *parts)
+
+
+def source(place, steps, over_y, over_c):
+    replica = lax.div(place, 4)
+    x, y, c = lax.div(replica, 4), lax.rem(lax.div(replica, 2), 2), lax.rem(replica, 2)
+    c = 1 - c if over_c else c
+    y = 1 - y if over_y else y
+    x = lax.rem(x + 4 + jnp.where(c == 0, -steps, steps), 4)
+    return x * 4 + y * 2 + c
+
+
+EXP_OUT = jax.ShapeDtypeStruct((SLOTS, 16 * 4 * EXP_T, TILE, LANES), jnp.bfloat16)
+KV_OUT = jax.ShapeDtypeStruct((SLOTS, 16 * 4 * KV_T, TILE, LANES), jnp.bfloat16)
+
+
+def lay(place, pieces, outs=None, tiles=None):
+    arrays = [p[0] for p in pieces]
+    more = [p[0] for p in tiles] if tiles else []
+    count = sum(2 if p[1] is None else 1 for p in pieces)
+
+    def views(p, ref):
+        if p[1] is None:
+            return [(h, ref.at[h]) for h in range(SLOTS)]
+        return [(p[1], ref)]
+
+    every = (pieces + tiles) if tiles else []
+    seen = sum(2 if p[1] is None else 1 for p in every)
+
+    def kernel(place_ref, *refs):
+        n, m, o = len(arrays), len(more), 2 if outs else 0
+        ins, late = refs[:n], refs[n : n + m]
+        rest = refs[n + m + o :]
+        exp_out, kv_out = rest[0], rest[1]
+        sems = rest[-1]
+        here = place_ref[0]
+        copies = []
+        gets = []
+        if tiles:
+            exp_scales, kv_scales, held, tile_sems = rest[2], rest[3], rest[4], rest[5]
+            i = 0
+            slots = []
+            for p, ref in zip(every, ins + late):
+                for h, view in views(p, ref):
+                    gets.append(pltpu.make_async_copy(view.at[FULL_T - 1], held.at[i], tile_sems.at[i]))
+                    slots.append(h)
+                    i += 1
+        i = 0
+        for p, ref in zip(pieces, ins):
+            at = source(here, *p[2:])
+            for h, view in views(p, ref):
+                n_exp, n_kv = 4 * EXP_T, 4 * KV_T
+                copies.append(
+                    pltpu.make_async_copy(
+                        view.at[pl.ds(0, n_exp)],
+                        exp_out.at[h, pl.ds(at * n_exp, n_exp)],
+                        sems.at[i, 0],
+                    )
+                )
+                copies.append(
+                    pltpu.make_async_copy(
+                        view.at[pl.ds(n_exp, n_kv)],
+                        kv_out.at[h, pl.ds(at * n_kv, n_kv)],
+                        sems.at[i, 1],
+                    )
+                )
+                i += 1
+        for copy in gets + copies:
+            copy.start()
+        if tiles:
+            for get in gets:
+                get.wait()
+            for h in range(SLOTS):
+                total = jnp.zeros((TILE, LANES), jnp.float32)
+                for i, slot in enumerate(slots):
+                    if slot == h:
+                        total += held[i].astype(jnp.float32)
+                exp_scales[h, 0:1, :] = total[0:1, :]
+                exp_scales[h, 1:2, :] = total[1:2, :]
+                kv_scales[h : h + 1, :] = total[2:3, :]
+        for copy in copies:
+            copy.wait()
+
+    out_shape = [EXP_OUT, KV_OUT]
+    out_specs = [pl.BlockSpec(memory_space=pl.ANY)] * 2
+    scratch = []
+    if tiles:
+        out_shape += [
+            jax.ShapeDtypeStruct((SLOTS, 2, LANES), jnp.float32),
+            jax.ShapeDtypeStruct((SLOTS, LANES), jnp.float32),
+        ]
+        out_specs += [pl.BlockSpec(memory_space=VMEM)] * 2
+        scratch += [
+            pltpu.VMEM((seen, TILE, LANES), jnp.bfloat16),
+            pltpu.SemaphoreType.DMA((seen,)),
+        ]
+    scratch.append(pltpu.SemaphoreType.DMA((count, 2)))
+    operands = arrays + more + (list(outs) if outs else [])
+    first = 1 + len(arrays) + len(more)
+    return pl.pallas_call(
+        kernel,
+        out_shape=tuple(out_shape),
+        in_specs=[pl.BlockSpec(memory_space=SMEM)]
+        + [pl.BlockSpec(memory_space=pl.ANY)] * len(operands),
+        out_specs=tuple(out_specs),
+        scratch_shapes=scratch,
+        input_output_aliases={first: 0, first + 1: 1} if outs else {},
+        compiler_params=pltpu.CompilerParams(vmem_limit_bytes=4 * 1024 * 1024),
+        cost_estimate=pl.CostEstimate(flops=0, transcendentals=0, bytes_accessed=count * 2**20),
+        name="lay",
+    )(place, *operands)
+
+
+def swap_core(v):
+    return lax.ppermute(v, "c", ring(2, 1))
+
+
+def swap_y(v):
+    return lax.ppermute(v, "yl", ring(2, 1))
+
+
+def along_x(v):
+    pairs = [(2 * x + c, 2 * ((x + (3 if c else 1)) % 4) + c) for x in range(4) for c in range(2)]
+    return lax.ppermute(v, ("x", "c"), pairs)
 
 
 def per_device(
@@ -135,30 +328,51 @@
 ):
     total = sum_over_devices(sum_of_squares(kv_grad, exp_grad))
     place = lax.axis_index(SHARD).astype(jnp.int32).reshape(1)
-    kv_new, exp_new, kv_val, routed, scales = update(
+    kv_new, exp_new, *parts = update(
         place,
         expert_owner,
         total,
         (kv_param, kv_grad, kv_mean, kv_square),
         (exp_param, exp_grad, exp_mean, exp_square),
     )
-    arrived = lax.all_to_all(routed, "z", 0, 0, tiled=True)
-    arrived = arrived.transpose(1, 0, 2, 3, 4).reshape(SLOTS, 1, 12, BLK, BLK)
-    exp_rollout = lax.all_gather(arrived, REPLICA, axis=2, tiled=True)
-    kv_plane = lax.all_gather(kv_val, "z", axis=1, tiled=True)
-    kv_rollout = lax.all_gather(kv_plane, REPLICA, axis=1, tiled=True)
-    for axis in ("c", "x", "yl", "z"):
-        scales = lax.psum(scales, axis)
-    kv_scales = scales[0:2, 0:64]
-    by_expert = scales[2:14, 0:64].reshape(EXPERTS, 3, 64).transpose(0, 2, 1).reshape(EXPERTS, 192)
-    shard = lax.axis_index("z").astype(jnp.int32)
-    rows = []
-    for s in range(SLOTS):
-        chosen, occupied = slot_of(expert_owner, shard, s)
-        row = lax.dynamic_index_in_dim(by_expert, chosen, 0, keepdims=False)
-        rows.append(jnp.where(occupied > 0, row, 0.0))
-    exp_scales = jnp.stack(rows).reshape(SLOTS, 1, 192)
-    return kv_new, exp_new, kv_rollout, kv_scales, exp_rollout, exp_scales
+    parts = [parts[0]] + [lax.ppermute(parts[k], "z", ring(4, k)) for k in (1, 2, 3)]
+    p0 = join(place, parts)
+    q0 = swap_y(p0)
+    p1 = along_x(p0)
+    p2 = along_x(p1)
+    p3 = along_x(p2)
+    a1 = along_x(q0[0])
+    a2 = along_x(a1)
+    a3 = along_x(a2)
+    b1, b2, b3 = swap_y(p1[1]), swap_y(p2[1]), swap_y(p3[1])
+    own = [
+        (p0, None, 0, False),
+        (p1, None, 1, False),
+        (p2, None, 2, False),
+        (q0, None, 0, True),
+        (p3, None, 3, False),
+        (b1, 1, 1, True),
+        (a1, 0, 1, True),
+        (b2, 1, 2, True),
+        (a2, 0, 2, True),
+        (b3, 1, 3, True),
+        (a3, 0, 3, True),
+    ]
+    pieces = []
+    for p in own:
+        pieces.append((*p, False))
+        pieces.append((swap_core(p[0]), *p[1:], True))
+    outs = lay(place, pieces[:8])
+    outs = lay(place, pieces[8:16], outs)
+    exp_rollout, kv_rollout, exp_scales, kv_scales = lay(place, pieces[16:], outs, pieces[:16])
+    return (
+        kv_new,
+        exp_new,
+        kv_rollout.reshape(2, 64, BLK, BLK),
+        kv_scales[:, 0:64],
+        exp_rollout.reshape(SLOTS, 1, 192, BLK, BLK),
+        exp_scales.reshape(SLOTS, 1, 2 * LANES)[:, :, 0:192],
+    )
 
 
 def solution(mesh):

time: 198 us -> 138 us (0.70)
  blocking collectives: 53.4 us -> 0 us
  starting transfers between devices: 16.1 us -> 53.4 us
  between operations: 24.2 us -> 0.82 us
  local copies, waits for them, and re-layouts: 28.1 us -> 6.91 us
  Pallas kernels: 4.57 us -> 19.2 us
  waiting for transfers between devices: 70 us -> 56.5 us
    all_gather x2 -> x0, waiting for transfers between devices: 63.5 us -> none  [the longest x1 63.5 us: per_device(): exp_rollout = lax.all_gather(arrived, REPLICA, axis=2, tiled=True)]
    ppermute x0 -> x24, waiting for transfers between devices: none -> 47.1 us  [the longest x6 26.6 us: along_x(): return lax.ppermute(v, ('x', 'c'), pairs)]
    ppermute x0 -> x24, starting transfers between devices: none -> 39.5 us  [the longest x11 19.7 us: swap_core(): return lax.ppermute(v, 'c', ring(2, 1))]
    psum x4 -> x0, blocking collectives: 31.6 us -> none  [per_device(): scales = lax.psum(scales, axis)]
    unnamed x21 -> x18, local copies, waits for them, and re-layouts: 24.9 us -> 6.77 us
    all_to_all x1 -> x0, blocking collectives: 11.7 us -> none  [per_device(): arrived = lax.all_to_all(routed, 'z', 0, 0, tiled=True)]
    all_gather x1 -> x0, blocking collectives: 10.1 us -> none  [per_device(): kv_plane = lax.all_gather(kv_val, 'z', axis=1, tiled=True)]
    pallas_call x0 -> x4, Pallas kernels: none -> 9.02 us  [the longest x3 8.94 us: lay(): pl.pallas_call(kernel, out_shape=tuple(out_shape), in_specs=[pl.BlockSpec...]
  transfers between devices with their start and end apart: 11 -> 33, of which waited for: 8 -> 15; matrix products, arithmetic and copies ran while one was open for 2% -> 0% of each run, Pallas kernels for 0% -> 4%
where the time goes in v2:
time: 138 us
  waiting for transfers between devices  56.5 us (41%)
  starting transfers between devices  53.4 us (39%)
  Pallas kernels  19.2 us (14%)
  local copies, waits for them, and re-layouts  6.91 us (5%)
    ppermute x6, waiting for transfers between devices, along_x(): return lax.ppermute(v, ('x', 'c'), pairs)  26.6 us
    ppermute x11, starting transfers between devices, swap_core(): return lax.ppermute(v, 'c', ring(2, 1))  19.7 us
    ppermute x4, waiting for transfers between devices, swap_y(): return lax.ppermute(v, 'yl', ring(2, 1))  12.3 us
    ppermute x6, starting transfers between devices, along_x(): return lax.ppermute(v, ('x', 'c'), pairs)  10.9 us
    pallas_call x3, Pallas kernels, lay(): pl.pallas_call(kernel, out_shape=tuple(out_shape), in_specs=[pl.BlockSpec...  8.94 us
    pallas_call x1, Pallas kernels, update(): pl.pallas_call(kernel, out_shape=(jax.ShapeDtypeStruct((2, 1, BLK, BLK),...  8.25 us
    ppermute x6, starting transfers between devices, sum_over_devices(): others = [lax.ppermute(v, axis, ring(4, k)) for k in (1, 2, 3)]  8.11 us
    ppermute x3, waiting for transfers between devices, per_device(): lax.ppermute(parts[k], 'z', ring(4, k))  6.81 us
  transfers between devices with their start and end apart: 33, of which 15 were waited for; matrix products, arithmetic and copies ran while one was open for 0% of the time, Pallas kernels for 4%

profile of v2, /device:TPU:1, one launch (start us, length us, event | category | flops | bytes accessed | tf_op | source)
XLA Modules:
  0.0 137.6 jit_solution(15724569841414850207)
XLA Ops:
  0.7 1.9 %sum_of_squares.1 = f32[8,128]{1,0:T(8,128)} custom-call(f32[2,1,128,128]{3,2,1,0:T(8,128)} %refs_1_.1, f32[4,1,3,128,128]{4,3,2,1,0:T(8,128)} %refs_5_.1), custom_call_target="tpu_custom_call" | custom-call | tf_op jit(solution)/shard_map/sum_of_squares/pallas_call | solution.py:49
  2.6 1.4 %collective-permute-start = (f32[8,128]{1,0:T(8,128)}, f32[8,128]{1,0:T(8,128)S(1)}, u32[]{:S(2)}, u32[]{:S(2)}) collective-permute-start(f32[8,128]{1,0:T(8,128)} %sum_of_squares.1), channel_id=1, source_target_pairs={{0,8},{8,0},{1,9},{9,1},{2,10},{10,2},{3,11},{11,3},{4,12},{12,4},... | collective-permute-start | bytes 12296 | tf_op jit(solution)/shard_map/ppermute | solution.py:60
  4.0 1.0 collective-permute-done
  5.0 0.7 add.39
  5.7 1.4 %collective-permute-start.1 = (f32[8,128]{1,0:T(8,128)S(1)}, f32[8,128]{1,0:T(8,128)S(1)}, u32[]{:S(2)}, u32[]{:S(2)}) collective-permute-start(f32[8,128]{1,0:T(8,128)S(1)} %add.39), channel_id=1, source_target_pairs={{0,16},{16,0},{1,17},{17,1},{2,18},{18,2},{3,19},{19,3},{4,20},{20... | collective-permute-start | bytes 12296 | tf_op jit(solution)/shard_map/ppermute | solution.py:60
  7.1 1.1 collective-permute-done.1
  8.2 3.0 %collective-permute-start.2 = (f32[8,128]{1,0:T(8,128)S(1)}, f32[8,128]{1,0:T(8,128)S(1)}, u32[]{:S(2)}, u32[]{:S(2)}) collective-permute-start(f32[8,128]{1,0:T(8,128)S(1)} %add.40), channel_id=1, source_target_pairs={{0,1},{1,0},{2,3},{3,2},{4,5},{5,4},{6,7},{7,6},{8,9},{9,8},{10,11... | collective-permute-start | bytes 12296 | tf_op jit(solution)/shard_map/ppermute | solution.py:60
  11.2 1.0 collective-permute-done.2
  12.2 2.5 %collective-permute-start.5 = (f32[8,128]{1,0:T(8,128)S(1)}, f32[8,128]{1,0:T(8,128)S(1)}, u32[]{:S(2)}, u32[]{:S(2)}) collective-permute-start(f32[8,128]{1,0:T(8,128)S(1)} %add.41), channel_id=1, source_target_pairs={{0,96},{32,0},{64,32},{96,64},{1,97},{33,1},{65,33},{97,65},{2,98}... | collective-permute-start | bytes 12296 | tf_op jit(solution)/shard_map/ppermute | solution.py:62
  14.7 0.5 collective-permute-start.4
  15.2 0.6 collective-permute-start.3
  15.9 2.8 %collective-permute-done.4 = f32[8,128]{1,0:T(8,128)S(1)} collective-permute-done((f32[8,128]{1,0:T(8,128)S(1)}, f32[8,128]{1,0:T(8,128)S(1)}, u32[]{:S(2)}, u32[]{:S(2)}) %collective-permute-start.4) | collective-permute-done | bytes 4128 | tf_op jit(solution)/shard_map/ppermute | solution.py:62
  18.7 0.2 collective-permute-done.3
  18.9 3.8 %collective-permute-start.8 = (f32[8,128]{1,0:T(8,128)S(1)}, f32[8,128]{1,0:T(8,128)S(1)}, u32[]{:S(2)}, u32[]{:S(2)}) collective-permute-start(f32[8,128]{1,0:T(8,128)S(1)} %add_add_fusion.1), channel_id=1, source_target_pairs={{0,6},{2,0},{4,2},{6,4},{1,7},{3,1},{5,3},{7,5},{8,14},{10,8},{12,... | collective-permute-start | bytes 12296 | tf_op jit(solution)/shard_map/ppermute | solution.py:62
  22.7 0.7 collective-permute-start.6
  23.4 0.1 collective-permute-done.8
  23.4 3.2 %collective-permute-done.7 = f32[8,128]{1,0:T(8,128)S(1)} collective-permute-done((f32[8,128]{1,0:T(8,128)S(1)}, f32[8,128]{1,0:T(8,128)S(1)}, u32[]{:S(2)}, u32[]{:S(2)}) %collective-permute-start.7) | collective-permute-done | bytes 4128 | tf_op jit(solution)/shard_map/ppermute | solution.py:62
  26.6 0.0 collective-permute-done.6
  26.7 0.0 copy-start.1
  26.7 1.1 copy-done.1
  27.8 1.1 copy-done.2
  28.9 1.1 copy-done.3
  30.1 0.9 copy-done.5
  31.0 0.9 copy-done.6
  31.9 0.9 copy-done.7
  32.8 0.7 copy-done.8
  33.4 8.2 %update.1 = (f32[2,1,128,128]{3,2,1,0:T(8,128)}, f32[4,1,3,128,128]{4,3,2,1,0:T(8,128)}, bf16[2,33,16,128]{3,2,1,0:T(8,128)(2,1)S(1)}, bf16[2,33,16,128]{3,2,1,0...) custom-call(s32[1]{0:T(128)} %bitcast.place_ref, s32[4]{0:T(128)S(1)} %copy-done.8, ...), custom_call_target="tpu_custom_call" | custom-call | tf_op jit(solution)/shard_map/update/pallas_call | solution.py:157
  41.7 0.1 collective-permute-start.9
  41.8 1.5 %collective-permute-start.10 = (bf16[2,33,16,128]{3,2,1,0:T(8,128)(2,1)S(1)}, bf16[2,33,16,128]{3,2,1,0:T(8,128)(2,1)S(1)}, u32[]{:S(2)}, u32[]{:S(2)}) collective-permute-start(bf16[2,33,16,128]{3,2,1,0:T(8,128)(2,1)S(1)} %get-tuple-element.24), channel_id=1, source_target_pairs={{0,4},{2,6},{4,0},{6,2},{1,5},{3,7},{5,1},{7,3},{8,12},{10,14},{12... | collective-permute-start | bytes 811016 | tf_op jit(solution)/shard_map/ppermute | solution.py:338
  43.3 2.0 %collective-permute-start.11 = (bf16[2,33,16,128]{3,2,1,0:T(8,128)(2,1)S(1)}, bf16[2,33,16,128]{3,2,1,0:T(8,128)(2,1)S(1)}, u32[]{:S(2)}, u32[]{:S(2)}) collective-permute-start(bf16[2,33,16,128]{3,2,1,0:T(8,128)(2,1)S(1)} %get-tuple-element.25), channel_id=1, source_target_pairs={{0,6},{2,0},{4,2},{6,4},{1,7},{3,1},{5,3},{7,5},{8,14},{10,8},{12,... | collective-permute-start | bytes 811016 | tf_op jit(solution)/shard_map/ppermute | solution.py:338
  45.3 5.9 %collective-permute-done.9.refs_1_ = bf16[2,33,16,128]{3,2,1,0:T(8,128)(2,1)S(1)} collective-permute-done((bf16[2,33,16,128]{3,2,1,0:T(8,128)(2,1)S(1)}, bf16[2,33,16,128]{3,2,1,0:T(8,128)(2,1)S(1)}, u32[]{:S(2)}, u32[]{:S(2)}) %collective-permute-start.9) | collective-permute-done | bytes 270368 | tf_op jit(solution)/shard_map/ppermute | solution.py:338
  51.2 0.0 collective-permute-done.10.refs_2_
  51.2 0.9 collective-permute-done.11.refs_3_
  52.1 0.1 join.1.refs_0_.refs_6_
  52.2 0.5 collective-permute-start.16
  52.7 1.3 collective-permute-start.12
  53.9 12.3 %collective-permute-done.16.refs_2_.refs_8_ = bf16[2,129,16,128]{3,2,1,0:T(8,128)(2,1)S(1)} collective-permute-done((bf16[2,129,16,128]{3,2,1,0:T(8,128)(2,1)S(1)}, bf16[2,129,16,128]{3,2,1,0:T(8,128)(2,1)S(1)}, u32[]{:S(2)}, u32[]{:S(2)}) %collective-permute-start.16) | collective-permute-done | bytes 1056800 | tf_op jit(solution)/shard_map/ppermute | solution.py:323
  66.3 1.3 collective-permute-start.17
  67.6 7.7 %collective-permute-start.23 = (bf16[2,129,16,128]{3,2,1,0:T(8,128)(2,1)S(1)}, bf16[2,129,16,128]{3,2,1,0:T(8,128)(2,1)S(1)}, u32[]{:S(2)}, u32[]{:S(2)}) collective-permute-start(bf16[2,129,16,128]{3,2,1,0:T(8,128)(2,1)S(1)} %join.1.refs_0_.refs_6_), channel_id=1, source_target_pairs={{0,8},{8,0},{1,9},{9,1},{2,10},{10,2},{3,11},{11,3},{4,12},{12,4},... | collective-permute-start | bytes 3170312 | tf_op jit(solution)/shard_map/ppermute | solution.py:314
  75.3 1.4 collective-permute-start.28
  76.7 0.3 collective-permute-start.24
  77.0 3.0 %collective-permute-start.13 = (bf16[129,16,128]{2,1,0:T(8,128)(2,1)S(1)}, bf16[129,16,128]{2,1,0:T(8,128)(2,1)S(1)}, u32[]{:S(2)}, u32[]{:S(2)}) collective-permute-start(bf16[129,16,128]{2,1,0:T(8,128)(2,1)S(1)} %slice_bitcast_fusion.3), channel_id=1, source_target_pairs={{0,32},{8,104},{32,64},{40,8},{64,96},{72,40},{96,0},{104,72},{1,3... | collective-permute-start | bytes 1585160 | tf_op jit(solution)/shard_map/ppermute | solution.py:323
  80.0 9.0 %collective-permute-done.28.refs_2_.refs_16_ = bf16[129,16,128]{2,1,0:T(8,128)(2,1)S(1)} collective-permute-done((bf16[129,16,128]{2,1,0:T(8,128)(2,1)S(1)}, bf16[129,16,128]{2,1,0:T(8,128)(2,1)S(1)}, u32[]{:S(2)}, u32[]{:S(2)}) %collective-permute-start.28) | collective-permute-done | bytes 528416 | tf_op jit(solution)/shard_map/ppermute | solution.py:318
  89.0 0.8 collective-permute-start.29
  89.8 3.0 %collective-permute-start.18 = (bf16[2,129,16,128]{3,2,1,0:T(8,128)(2,1)S(1)}, bf16[2,129,16,128]{3,2,1,0:T(8,128)(2,1)S(1)}, u32[]{:S(2)}, u32[]{:S(2)}) collective-permute-start(bf16[2,129,16,128]{3,2,1,0:T(8,128)(2,1)S(1)} %collective-permute-done.17.refs_4_.refs_10_), channel_id=1, source_target_pairs={{0,32},{8,104},{32,64},{40,8},{64,96},{72,40},{96,0},{104,72},{1,3... | collective-permute-start | bytes 3170312 | tf_op jit(solution)/shard_map/ppermute | solution.py:323
  92.8 0.0 collective-permute-done.23.refs_1_.refs_7_
  92.8 0.0 collective-permute-start.26
  92.8 4.2 %collective-permute-start.30 = (bf16[129,16,128]{2,1,0:T(8,128)(2,1)S(1)}, bf16[129,16,128]{2,1,0:T(8,128)(2,1)S(1)}, u32[]{:S(2)}, u32[]{:S(2)}) collective-permute-start(bf16[129,16,128]{2,1,0:T(8,128)(2,1)S(1)} %collective-permute-done.13.refs_4_.refs_18_), channel_id=1, source_target_pairs={{0,8},{8,0},{1,9},{9,1},{2,10},{10,2},{3,11},{11,3},{4,12},{12,4},... | collective-permute-start | bytes 1585160 | tf_op jit(solution)/shard_map/ppermute | solution.py:314
  97.0 0.1 collective-permute-start.25
  97.2 1.4 %collective-permute-done.30.refs_5_.refs_19_ = bf16[129,16,128]{2,1,0:T(8,128)(2,1)S(1)} collective-permute-done((bf16[129,16,128]{2,1,0:T(8,128)(2,1)S(1)}, bf16[129,16,128]{2,1,0:T(8,128)(2,1)S(1)}, u32[]{:S(2)}, u32[]{:S(2)}) %collective-permute-start.30) | collective-permute-done | bytes 528416 | tf_op jit(solution)/shard_map/ppermute | solution.py:314
  98.6 1.3 collective-permute-start.31
  99.9 10.4 %collective-permute-done.14.refs_0_ = bf16[129,16,128]{2,1,0:T(8,128)(2,1)S(1)} collective-permute-done((bf16[129,16,128]{2,1,0:T(8,128)(2,1)S(1)}, bf16[129,16,128]{2,1,0:T(8,128)(2,1)S(1)}, u32[]{:S(2)}, u32[]{:S(2)}) %collective-permute-start.14) | collective-permute-done | bytes 528416 | tf_op jit(solution)/shard_map/ppermute | solution.py:323
  110.3 3.1 %collective-permute-start.21 = (bf16[129,16,128]{2,1,0:T(8,128)(2,1)S(1)}, bf16[129,16,128]{2,1,0:T(8,128)(2,1)S(1)}, u32[]{:S(2)}, u32[]{:S(2)}) collective-permute-start(bf16[129,16,128]{2,1,0:T(8,128)(2,1)S(1)} %collective-permute-done.14.refs_0_), channel_id=1, source_target_pairs={{0,32},{8,104},{32,64},{40,8},{64,96},{72,40},{96,0},{104,72},{1,3... | collective-permute-start | bytes 1585160 | tf_op jit(solution)/shard_map/ppermute | solution.py:323
  113.4 0.6 collective-permute-start.27
  114.1 1.4 collective-permute-start.19
  115.4 0.3 collective-permute-start.32
  115.7 3.8 %collective-permute-done.21.refs_4_ = bf16[129,16,128]{2,1,0:T(8,128)(2,1)S(1)} collective-permute-done((bf16[129,16,128]{2,1,0:T(8,128)(2,1)S(1)}, bf16[129,16,128]{2,1,0:T(8,128)(2,1)S(1)}, u32[]{:S(2)}, u32[]{:S(2)}) %collective-permute-start.21) | collective-permute-done | bytes 528416 | tf_op jit(solution)/shard_map/ppermute | solution.py:323
  119.5 4.9 %collective-permute-start.15 = (bf16[129,16,128]{2,1,0:T(8,128)(2,1)S(1)}, bf16[129,16,128]{2,1,0:T(8,128)(2,1)S(1)}, u32[]{:S(2)}, u32[]{:S(2)}) collective-permute-start(bf16[129,16,128]{2,1,0:T(8,128)(2,1)S(1)} %collective-permute-done.14.refs_0_), channel_id=1, source_target_pairs={{0,8},{8,0},{1,9},{9,1},{2,10},{10,2},{3,11},{11,3},{4,12},{12,4},... | collective-permute-start | bytes 1585160 | tf_op jit(solution)/shard_map/ppermute | solution.py:314
  124.4 0.0 collective-permute-start.22
  124.4 3.3 %collective-permute-done.19.refs_2_ = bf16[129,16,128]{2,1,0:T(8,128)(2,1)S(1)} collective-permute-done((bf16[129,16,128]{2,1,0:T(8,128)(2,1)S(1)}, bf16[129,16,128]{2,1,0:T(8,128)(2,1)S(1)}, u32[]{:S(2)}, u32[]{:S(2)}) %collective-permute-start.19) | collective-permute-done | bytes 528416 | tf_op jit(solution)/shard_map/ppermute | solution.py:318
  127.8 0.8 collective-permute-start.20
  128.6 3.5 %lay.3 = (bf16[2,1536,16,128]{3,2,1,0:T(8,128)(2,1)}, bf16[2,512,16,128]{3,2,1,0:T(8,128)(2,1)}) custom-call(s32[1]{0:T(128)} %bitcast.place_ref, bf16[2,129,16,128]{3,2,1,0:T(8,128)(2,1)S(1)} %join.1.refs_0_.refs_6_, bf16[2,129,16,128]{3,2,1,0:T(8,128)(2,1)S(1)} %collective-permute-done.23.refs_1_.refs_7_, ...), custom_call_target="tpu_custom_call" | custom-call | bytes 16777216 | tf_op jit(solution)/shard_map/lay/pallas_call | solution.py:299
  132.1 2.5 %lay.4 = (bf16[2,1536,16,128]{3,2,1,0:T(8,128)(2,1)}, bf16[2,512,16,128]{3,2,1,0:T(8,128)(2,1)}) custom-call(s32[1]{0:T(128)} %bitcast.place_ref, bf16[2,129,16,128]{3,2,1,0:T(8,128)(2,1)S(1)} %collective-permute-done.18.refs_0_.refs_14_, ...), custom_call_target="tpu_custom_call", output_to_operand_aliasing={{0}: (9, {}), {1}: (10, {})} | custom-call | bytes 10485760 | tf_op jit(solution)/shard_map/lay/pallas_call | solution.py:299
  134.7 2.9 %lay.5 = (bf16[2,1536,16,128]{3,2,1,0:T(8,128)(2,1)}, bf16[2,512,16,128]{3,2,1,0:T(8,128)(2,1)}, f32[2,2,128]{2,1,0:T(2,128)}, f32[2,128]{1,0:T(2,128)}) custom-call(s32[1]{0:T(128)} %bitcast.place_ref, bf16[129,16,128]{2,1,0:T(8,128)(2,1)S(1)} %collective-permute-done.14.refs_0_, ...), custom_call_target="tpu_custom_call", output_to_operand_aliasing={{0}: (23, {}), {1}: (24, {})} | custom-call | bytes 6291456 | tf_op jit(solution)/shard_map/lay/pallas_call | solution.py:299
  (35 shorter events, 0.2 us)
Async XLA Ops:
  0.6 26.0 %copy-start = (f32[4,1,3,128,128]{4,3,2,1,0:T(8,128)S(1)}, f32[4,1,3,128,128]{4,3,2,1,0:T(8,128)}, u32[]{:S(2)}) copy-start(f32[4,1,3,128,128]{4,3,2,1,0:T(8,128)} %refs_5_.1) | copy-start | bytes 2359300
  0.6 26.0 %copy-start.4 = (f32[2,1,128,128]{3,2,1,0:T(8,128)S(1)}, f32[2,1,128,128]{3,2,1,0:T(8,128)}, u32[]{:S(2)}) copy-start(f32[2,1,128,128]{3,2,1,0:T(8,128)} %refs_1_.1) | copy-start | bytes 393220
  2.6 2.5 %collective-permute-start = (f32[8,128]{1,0:T(8,128)}, f32[8,128]{1,0:T(8,128)S(1)}, u32[]{:S(2)}, u32[]{:S(2)}) collective-permute-start(f32[8,128]{1,0:T(8,128)} %sum_of_squares.1), channel_id=1, source_target_pairs={{0,8},{8,0},{1,9},{9,1},{2,10},{10,2},{3,11},{11,3},{4,12},{12,4},... | collective-permute-start | bytes 12296 | tf_op jit(solution)/shard_map/ppermute | solution.py:60
  5.7 2.5 %collective-permute-start.1 = (f32[8,128]{1,0:T(8,128)S(1)}, f32[8,128]{1,0:T(8,128)S(1)}, u32[]{:S(2)}, u32[]{:S(2)}) collective-permute-start(f32[8,128]{1,0:T(8,128)S(1)} %add.39), channel_id=1, source_target_pairs={{0,16},{16,0},{1,17},{17,1},{2,18},{18,2},{3,19},{19,3},{4,20},{20... | collective-permute-start | bytes 12296 | tf_op jit(solution)/shard_map/ppermute | solution.py:60
  8.2 4.0 %collective-permute-start.2 = (f32[8,128]{1,0:T(8,128)S(1)}, f32[8,128]{1,0:T(8,128)S(1)}, u32[]{:S(2)}, u32[]{:S(2)}) collective-permute-start(f32[8,128]{1,0:T(8,128)S(1)} %add.40), channel_id=1, source_target_pairs={{0,1},{1,0},{2,3},{3,2},{4,5},{5,4},{6,7},{7,6},{8,9},{9,8},{10,11... | collective-permute-start | bytes 12296 | tf_op jit(solution)/shard_map/ppermute | solution.py:60
  12.2 3.7 %collective-permute-start.5 = (f32[8,128]{1,0:T(8,128)S(1)}, f32[8,128]{1,0:T(8,128)S(1)}, u32[]{:S(2)}, u32[]{:S(2)}) collective-permute-start(f32[8,128]{1,0:T(8,128)S(1)} %add.41), channel_id=1, source_target_pairs={{0,96},{32,0},{64,32},{96,64},{1,97},{33,1},{65,33},{97,65},{2,98}... | collective-permute-start | bytes 12296 | tf_op jit(solution)/shard_map/ppermute | solution.py:62
  14.7 4.0 %collective-permute-start.4 = (f32[8,128]{1,0:T(8,128)S(1)}, f32[8,128]{1,0:T(8,128)S(1)}, u32[]{:S(2)}, u32[]{:S(2)}) collective-permute-start(f32[8,128]{1,0:T(8,128)S(1)} %add.41), channel_id=1, source_target_pairs={{0,64},{32,96},{64,0},{96,32},{1,65},{33,97},{65,1},{97,33},{2,66}... | collective-permute-start | bytes 12296 | tf_op jit(solution)/shard_map/ppermute | solution.py:62
  15.2 3.7 %collective-permute-start.3 = (f32[8,128]{1,0:T(8,128)S(1)}, f32[8,128]{1,0:T(8,128)S(1)}, u32[]{:S(2)}, u32[]{:S(2)}) collective-permute-start(f32[8,128]{1,0:T(8,128)S(1)} %add.41), channel_id=1, source_target_pairs={{0,32},{32,64},{64,96},{96,0},{1,33},{33,65},{65,97},{97,1},{2,34}... | collective-permute-start | bytes 12296 | tf_op jit(solution)/shard_map/ppermute | solution.py:62
  18.9 4.5 %collective-permute-start.8 = (f32[8,128]{1,0:T(8,128)S(1)}, f32[8,128]{1,0:T(8,128)S(1)}, u32[]{:S(2)}, u32[]{:S(2)}) collective-permute-start(f32[8,128]{1,0:T(8,128)S(1)} %add_add_fusion.1), channel_id=1, source_target_pairs={{0,6},{2,0},{4,2},{6,4},{1,7},{3,1},{5,3},{7,5},{8,14},{10,8},{12,... | collective-permute-start | bytes 12296 | tf_op jit(solution)/shard_map/ppermute | solution.py:62
  22.7 4.0 %collective-permute-start.7 = (f32[8,128]{1,0:T(8,128)S(1)}, f32[8,128]{1,0:T(8,128)S(1)}, u32[]{:S(2)}, u32[]{:S(2)}) collective-permute-start(f32[8,128]{1,0:T(8,128)S(1)} %add_add_fusion.1), channel_id=1, source_target_pairs={{0,4},{2,6},{4,0},{6,2},{1,5},{3,7},{5,1},{7,3},{8,12},{10,14},{12... | collective-permute-start | bytes 12296 | tf_op jit(solution)/shard_map/ppermute | solution.py:62
  22.7 4.0 %collective-permute-start.6 = (f32[8,128]{1,0:T(8,128)S(1)}, f32[8,128]{1,0:T(8,128)S(1)}, u32[]{:S(2)}, u32[]{:S(2)}) collective-permute-start(f32[8,128]{1,0:T(8,128)S(1)} %add_add_fusion.1), channel_id=1, source_target_pairs={{0,2},{2,4},{4,6},{6,0},{1,3},{3,5},{5,7},{7,1},{8,10},{10,12},{12... | collective-permute-start | bytes 12296 | tf_op jit(solution)/shard_map/ppermute | solution.py:62
  26.7 1.1 copy-start.1
  27.8 1.1 copy-start.2
  28.9 1.1 copy-start.3
  30.1 0.9 copy-start.5
  31.0 0.9 copy-start.6
  31.9 0.9 copy-start.7
  32.8 0.7 copy-start.8
  41.7 9.5 %collective-permute-start.9 = (bf16[2,33,16,128]{3,2,1,0:T(8,128)(2,1)S(1)}, bf16[2,33,16,128]{3,2,1,0:T(8,128)(2,1)S(1)}, u32[]{:S(2)}, u32[]{:S(2)}) collective-permute-start(bf16[2,33,16,128]{3,2,1,0:T(8,128)(2,1)S(1)} %get-tuple-element.23), channel_id=1, source_target_pairs={{0,2},{2,4},{4,6},{6,0},{1,3},{3,5},{5,7},{7,1},{8,10},{10,12},{12... | collective-permute-start | bytes 811016 | tf_op jit(solution)/shard_map/ppermute | solution.py:338
  41.8 9.4 %collective-permute-start.10 = (bf16[2,33,16,128]{3,2,1,0:T(8,128)(2,1)S(1)}, bf16[2,33,16,128]{3,2,1,0:T(8,128)(2,1)S(1)}, u32[]{:S(2)}, u32[]{:S(2)}) collective-permute-start(bf16[2,33,16,128]{3,2,1,0:T(8,128)(2,1)S(1)} %get-tuple-element.24), channel_id=1, source_target_pairs={{0,4},{2,6},{4,0},{6,2},{1,5},{3,7},{5,1},{7,3},{8,12},{10,14},{12... | collective-permute-start | bytes 811016 | tf_op jit(solution)/shard_map/ppermute | solution.py:338
  43.3 8.8 %collective-permute-start.11 = (bf16[2,33,16,128]{3,2,1,0:T(8,128)(2,1)S(1)}, bf16[2,33,16,128]{3,2,1,0:T(8,128)(2,1)S(1)}, u32[]{:S(2)}, u32[]{:S(2)}) collective-permute-start(bf16[2,33,16,128]{3,2,1,0:T(8,128)(2,1)S(1)} %get-tuple-element.25), channel_id=1, source_target_pairs={{0,6},{2,0},{4,2},{6,4},{1,7},{3,1},{5,3},{7,5},{8,14},{10,8},{12,... | collective-permute-start | bytes 811016 | tf_op jit(solution)/shard_map/ppermute | solution.py:338
  52.2 14.1 %collective-permute-start.16 = (bf16[2,129,16,128]{3,2,1,0:T(8,128)(2,1)S(1)}, bf16[2,129,16,128]{3,2,1,0:T(8,128)(2,1)S(1)}, u32[]{:S(2)}, u32[]{:S(2)}) collective-permute-start(bf16[2,129,16,128]{3,2,1,0:T(8,128)(2,1)S(1)} %join.1.refs_0_.refs_6_), channel_id=1, source_target_pairs={{0,32},{8,104},{32,64},{40,8},{64,96},{72,40},{96,0},{104,72},{1,3... | collective-permute-start | bytes 3170312 | tf_op jit(solution)/shard_map/ppermute | solution.py:323
  52.7 24.3 %collective-permute-start.12 = (bf16[2,129,16,128]{3,2,1,0:T(8,128)(2,1)S(1)}, bf16[2,129,16,128]{3,2,1,0:T(8,128)(2,1)S(1)}, u32[]{:S(2)}, u32[]{:S(2)}) collective-permute-start(bf16[2,129,16,128]{3,2,1,0:T(8,128)(2,1)S(1)} %join.1.refs_0_.refs_6_), channel_id=1, source_target_pairs={{0,16},{16,0},{1,17},{17,1},{2,18},{18,2},{3,19},{19,3},{4,20},{20... | collective-permute-start | bytes 3170312 | tf_op jit(solution)/shard_map/ppermute | solution.py:318
  66.3 23.5 %collective-permute-start.17 = (bf16[2,129,16,128]{3,2,1,0:T(8,128)(2,1)S(1)}, bf16[2,129,16,128]{3,2,1,0:T(8,128)(2,1)S(1)}, u32[]{:S(2)}, u32[]{:S(2)}) collective-permute-start(bf16[2,129,16,128]{3,2,1,0:T(8,128)(2,1)S(1)} %collective-permute-done.16.refs_2_.refs_8_), channel_id=1, source_target_pairs={{0,32},{8,104},{32,64},{40,8},{64,96},{72,40},{96,0},{104,72},{1,3... | collective-permute-start | bytes 3170312 | tf_op jit(solution)/shard_map/ppermute | solution.py:323
  67.6 25.2 %collective-permute-start.23 = (bf16[2,129,16,128]{3,2,1,0:T(8,128)(2,1)S(1)}, bf16[2,129,16,128]{3,2,1,0:T(8,128)(2,1)S(1)}, u32[]{:S(2)}, u32[]{:S(2)}) collective-permute-start(bf16[2,129,16,128]{3,2,1,0:T(8,128)(2,1)S(1)} %join.1.refs_0_.refs_6_), channel_id=1, source_target_pairs={{0,8},{8,0},{1,9},{9,1},{2,10},{10,2},{3,11},{11,3},{4,12},{12,4},... | collective-permute-start | bytes 3170312 | tf_op jit(solution)/shard_map/ppermute | solution.py:314
  75.3 13.7 %collective-permute-start.28 = (bf16[129,16,128]{2,1,0:T(8,128)(2,1)S(1)}, bf16[129,16,128]{2,1,0:T(8,128)(2,1)S(1)}, u32[]{:S(2)}, u32[]{:S(2)}) collective-permute-start(bf16[129,16,128]{2,1,0:T(8,128)(2,1)S(1)} %slice_bitcast_fusion.1), channel_id=1, source_target_pairs={{0,16},{16,0},{1,17},{17,1},{2,18},{18,2},{3,19},{19,3},{4,20},{20... | collective-permute-start | bytes 1585160 | tf_op jit(solution)/shard_map/ppermute | solution.py:318
  76.7 20.4 %collective-permute-start.24 = (bf16[2,129,16,128]{3,2,1,0:T(8,128)(2,1)S(1)}, bf16[2,129,16,128]{3,2,1,0:T(8,128)(2,1)S(1)}, u32[]{:S(2)}, u32[]{:S(2)}) collective-permute-start(bf16[2,129,16,128]{3,2,1,0:T(8,128)(2,1)S(1)} %collective-permute-done.16.refs_2_.refs_8_), channel_id=1, source_target_pairs={{0,8},{8,0},{1,9},{9,1},{2,10},{10,2},{3,11},{11,3},{4,12},{12,4},... | collective-permute-start | bytes 3170312 | tf_op jit(solution)/shard_map/ppermute | solution.py:314
  77.0 15.8 %collective-permute-start.13 = (bf16[129,16,128]{2,1,0:T(8,128)(2,1)S(1)}, bf16[129,16,128]{2,1,0:T(8,128)(2,1)S(1)}, u32[]{:S(2)}, u32[]{:S(2)}) collective-permute-start(bf16[129,16,128]{2,1,0:T(8,128)(2,1)S(1)} %slice_bitcast_fusion.3), channel_id=1, source_target_pairs={{0,32},{8,104},{32,64},{40,8},{64,96},{72,40},{96,0},{104,72},{1,3... | collective-permute-start | bytes 1585160 | tf_op jit(solution)/shard_map/ppermute | solution.py:323
  89.0 8.0 %collective-permute-start.29 = (bf16[129,16,128]{2,1,0:T(8,128)(2,1)S(1)}, bf16[129,16,128]{2,1,0:T(8,128)(2,1)S(1)}, u32[]{:S(2)}, u32[]{:S(2)}) collective-permute-start(bf16[129,16,128]{2,1,0:T(8,128)(2,1)S(1)} %collective-permute-done.28.refs_2_.refs_16_), channel_id=1, source_target_pairs={{0,8},{8,0},{1,9},{9,1},{2,10},{10,2},{3,11},{11,3},{4,12},{12,4},... | collective-permute-start | bytes 1585160 | tf_op jit(solution)/shard_map/ppermute | solution.py:314
  89.8 23.6 %collective-permute-start.18 = (bf16[2,129,16,128]{3,2,1,0:T(8,128)(2,1)S(1)}, bf16[2,129,16,128]{3,2,1,0:T(8,128)(2,1)S(1)}, u32[]{:S(2)}, u32[]{:S(2)}) collective-permute-start(bf16[2,129,16,128]{3,2,1,0:T(8,128)(2,1)S(1)} %collective-permute-done.17.refs_4_.refs_10_), channel_id=1, source_target_pairs={{0,32},{8,104},{32,64},{40,8},{64,96},{72,40},{96,0},{104,72},{1,3... | collective-permute-start | bytes 3170312 | tf_op jit(solution)/shard_map/ppermute | solution.py:323
  92.8 21.3 %collective-permute-start.26 = (bf16[2,129,16,128]{3,2,1,0:T(8,128)(2,1)S(1)}, bf16[2,129,16,128]{3,2,1,0:T(8,128)(2,1)S(1)}, u32[]{:S(2)}, u32[]{:S(2)}) collective-permute-start(bf16[2,129,16,128]{3,2,1,0:T(8,128)(2,1)S(1)} %collective-permute-done.12.refs_6_.refs_12_), channel_id=1, source_target_pairs={{0,8},{8,0},{1,9},{9,1},{2,10},{10,2},{3,11},{11,3},{4,12},{12,4},... | collective-permute-start | bytes 3170312 | tf_op jit(solution)/shard_map/ppermute | solution.py:314
  92.8 5.8 %collective-permute-start.30 = (bf16[129,16,128]{2,1,0:T(8,128)(2,1)S(1)}, bf16[129,16,128]{2,1,0:T(8,128)(2,1)S(1)}, u32[]{:S(2)}, u32[]{:S(2)}) collective-permute-start(bf16[129,16,128]{2,1,0:T(8,128)(2,1)S(1)} %collective-permute-done.13.refs_4_.refs_18_), channel_id=1, source_target_pairs={{0,8},{8,0},{1,9},{9,1},{2,10},{10,2},{3,11},{11,3},{4,12},{12,4},... | collective-permute-start | bytes 1585160 | tf_op jit(solution)/shard_map/ppermute | solution.py:314
  97.0 13.2 %collective-permute-start.14 = (bf16[129,16,128]{2,1,0:T(8,128)(2,1)S(1)}, bf16[129,16,128]{2,1,0:T(8,128)(2,1)S(1)}, u32[]{:S(2)}, u32[]{:S(2)}) collective-permute-start(bf16[129,16,128]{2,1,0:T(8,128)(2,1)S(1)} %collective-permute-done.13.refs_4_.refs_18_), channel_id=1, source_target_pairs={{0,32},{8,104},{32,64},{40,8},{64,96},{72,40},{96,0},{104,72},{1,3... | collective-permute-start | bytes 1585160 | tf_op jit(solution)/shard_map/ppermute | solution.py:323
  97.0 27.4 %collective-permute-start.25 = (bf16[2,129,16,128]{3,2,1,0:T(8,128)(2,1)S(1)}, bf16[2,129,16,128]{3,2,1,0:T(8,128)(2,1)S(1)}, u32[]{:S(2)}, u32[]{:S(2)}) collective-permute-start(bf16[2,129,16,128]{3,2,1,0:T(8,128)(2,1)S(1)} %collective-permute-done.17.refs_4_.refs_10_), channel_id=1, source_target_pairs={{0,8},{8,0},{1,9},{9,1},{2,10},{10,2},{3,11},{11,3},{4,12},{12,4},... | collective-permute-start | bytes 3170312 | tf_op jit(solution)/shard_map/ppermute | solution.py:314
  98.6 16.9 %collective-permute-start.31 = (bf16[129,16,128]{2,1,0:T(8,128)(2,1)S(1)}, bf16[129,16,128]{2,1,0:T(8,128)(2,1)S(1)}, u32[]{:S(2)}, u32[]{:S(2)}) collective-permute-start(bf16[129,16,128]{2,1,0:T(8,128)(2,1)S(1)} %slice_bitcast_fusion), channel_id=1, source_target_pairs={{0,16},{16,0},{1,17},{17,1},{2,18},{18,2},{3,19},{19,3},{4,20},{20... | collective-permute-start | bytes 1585160 | tf_op jit(solution)/shard_map/ppermute | solution.py:318
  110.3 9.3 %collective-permute-start.21 = (bf16[129,16,128]{2,1,0:T(8,128)(2,1)S(1)}, bf16[129,16,128]{2,1,0:T(8,128)(2,1)S(1)}, u32[]{:S(2)}, u32[]{:S(2)}) collective-permute-start(bf16[129,16,128]{2,1,0:T(8,128)(2,1)S(1)} %collective-permute-done.14.refs_0_), channel_id=1, source_target_pairs={{0,32},{8,104},{32,64},{40,8},{64,96},{72,40},{96,0},{104,72},{1,3... | collective-permute-start | bytes 1585160 | tf_op jit(solution)/shard_map/ppermute | solution.py:323
  113.4 18.7 %collective-permute-start.27 = (bf16[2,129,16,128]{3,2,1,0:T(8,128)(2,1)S(1)}, bf16[2,129,16,128]{3,2,1,0:T(8,128)(2,1)S(1)}, u32[]{:S(2)}, u32[]{:S(2)}) collective-permute-start(bf16[2,129,16,128]{3,2,1,0:T(8,128)(2,1)S(1)} %collective-permute-done.18.refs_0_.refs_14_), channel_id=1, source_target_pairs={{0,8},{8,0},{1,9},{9,1},{2,10},{10,2},{3,11},{11,3},{4,12},{12,4},... | collective-permute-start | bytes 3170312 | tf_op jit(solution)/shard_map/ppermute | solution.py:314
  114.1 13.7 %collective-permute-start.19 = (bf16[129,16,128]{2,1,0:T(8,128)(2,1)S(1)}, bf16[129,16,128]{2,1,0:T(8,128)(2,1)S(1)}, u32[]{:S(2)}, u32[]{:S(2)}) collective-permute-start(bf16[129,16,128]{2,1,0:T(8,128)(2,1)S(1)} %slice_bitcast_fusion.2), channel_id=1, source_target_pairs={{0,16},{16,0},{1,17},{17,1},{2,18},{18,2},{3,19},{19,3},{4,20},{20... | collective-permute-start | bytes 1585160 | tf_op jit(solution)/shard_map/ppermute | solution.py:318
  115.4 16.7 %collective-permute-start.32 = (bf16[129,16,128]{2,1,0:T(8,128)(2,1)S(1)}, bf16[129,16,128]{2,1,0:T(8,128)(2,1)S(1)}, u32[]{:S(2)}, u32[]{:S(2)}) collective-permute-start(bf16[129,16,128]{2,1,0:T(8,128)(2,1)S(1)} %collective-permute-done.31.refs_6_.refs_20_), channel_id=1, source_target_pairs={{0,8},{8,0},{1,9},{9,1},{2,10},{10,2},{3,11},{11,3},{4,12},{12,4},... | collective-permute-start | bytes 1585160 | tf_op jit(solution)/shard_map/ppermute | solution.py:314
  119.5 15.1 %collective-permute-start.15 = (bf16[129,16,128]{2,1,0:T(8,128)(2,1)S(1)}, bf16[129,16,128]{2,1,0:T(8,128)(2,1)S(1)}, u32[]{:S(2)}, u32[]{:S(2)}) collective-permute-start(bf16[129,16,128]{2,1,0:T(8,128)(2,1)S(1)} %collective-permute-done.14.refs_0_), channel_id=1, source_target_pairs={{0,8},{8,0},{1,9},{9,1},{2,10},{10,2},{3,11},{11,3},{4,12},{12,4},... | collective-permute-start | bytes 1585160 | tf_op jit(solution)/shard_map/ppermute | solution.py:314
  124.4 10.2 %collective-permute-start.22 = (bf16[129,16,128]{2,1,0:T(8,128)(2,1)S(1)}, bf16[129,16,128]{2,1,0:T(8,128)(2,1)S(1)}, u32[]{:S(2)}, u32[]{:S(2)}) collective-permute-start(bf16[129,16,128]{2,1,0:T(8,128)(2,1)S(1)} %collective-permute-done.21.refs_4_), channel_id=1, source_target_pairs={{0,8},{8,0},{1,9},{9,1},{2,10},{10,2},{3,11},{11,3},{4,12},{12,4},... | collective-permute-start | bytes 1585160 | tf_op jit(solution)/shard_map/ppermute | solution.py:314
  127.8 6.9 %collective-permute-start.20 = (bf16[129,16,128]{2,1,0:T(8,128)(2,1)S(1)}, bf16[129,16,128]{2,1,0:T(8,128)(2,1)S(1)}, u32[]{:S(2)}, u32[]{:S(2)}) collective-permute-start(bf16[129,16,128]{2,1,0:T(8,128)(2,1)S(1)} %collective-permute-done.19.refs_2_), channel_id=1, source_target_pairs={{0,8},{8,0},{1,9},{9,1},{2,10},{10,2},{3,11},{11,3},{4,12},{12,4},... | collective-permute-start | bytes 1585160 | tf_op jit(solution)/shard_map/ppermute | solution.py:314

commit v3 on v1

v3 whole, which is shorter than its diff:
```python
import jax
import jax.numpy as jnp
from jax import lax
from jax.experimental import pallas as pl
from jax.experimental.pallas import tpu as pltpu
from jax.sharding import Mesh, PartitionSpec as P

SLOTS = 2
EXPERTS = 4
BLK = 128
LANES = 128

beta_one = 0.9
beta_two = 0.95
learn_rate = 0.25
decay_rate = 0.01
adam_eps = 1e-08
step_count = 20.0
clip_norm = 1.0
scale_eps = 1e-06

REPLICA = ("x", "yl", "c")
SHARD = ("x", "yl", "c", "z")
VMEM = pltpu.VMEM
SMEM = pltpu.SMEM

TILE = 16
SLOT_T = 24
PART_T = 1 + 2 * SLOT_T
FULL_T = 1 + 8 * SLOT_T
A_T = 129
KV_T = 8
PLANE_T = 2 * 8 * KV_T + 1


def ring(n, k):
    return [(i, (i + k) % n) for i in range(n)]


def sum_of_squares(kv_grad, exp_grad):
    def kernel(kv_ref, exp_ref, out_ref):
        total = jnp.zeros((8, LANES), jnp.float32)
        for i in range(2):
            g = kv_ref[i, 0]
            total += jnp.sum((g * g).reshape(BLK // 8, 8, LANES), axis=0)
        for e in range(EXPERTS):
            for j in range(3):
                g = exp_ref[e, 0, j]
                total += jnp.sum((g * g).reshape(BLK // 8, 8, LANES), axis=0)
        out_ref[...] = total

    return pl.pallas_call(
        kernel,
        out_shape=jax.ShapeDtypeStruct((8, LANES), jnp.float32),
        in_specs=[pl.BlockSpec(memory_space=VMEM)] * 2,
        out_specs=pl.BlockSpec(memory_space=VMEM),
        name="sum_of_squares",
    )(kv_grad, exp_grad)


def sum_over_devices(v):
    for axis in ("x", "z"):
        others = [lax.ppermute(v, axis, ring(4, k)) for k in (1, 2, 3)]
        v = v + others[0] + others[1] + others[2]
    for axis in ("yl", "yh", "c"):
        v = v + lax.ppermute(v, axis, ring(2, 1))
    return v


def adam(master, gradient, moment_one, moment_two, factor):
    scaled = factor * gradient
    mean_new = beta_one * moment_one + (1.0 - beta_one) * scaled
    square_new = beta_two * moment_two + (1.0 - beta_two) * scaled * scaled
    corr_one = 1.0 - beta_one**step_count
    corr_two = 1.0 - beta_two**step_count
    update = mean_new / corr_one / (jnp.sqrt(square_new / corr_two) + adam_eps)
    return master - learn_rate * (update + decay_rate * master)


def slot_of(owner, shard, slot):
    chosen = jnp.int32(0)
    occupied = jnp.int32(0)
    for e in range(EXPERTS):
        rank = jnp.int32(0)
        for f in range(e):
            rank += (owner[f] == owner[e]).astype(jnp.int32)
        matched = jnp.logical_and(owner[e] == shard, rank == slot).astype(jnp.int32)
        chosen += matched * e
        occupied += matched
    return chosen, occupied


def update(place, owner, total, kv, exp):
    def kernel(place_ref, owner_ref, total_ref, *refs):
        kv_hbm, exp_hbm = refs[0:4], refs[4:8]
        kv_new, exp_new = refs[8:10]
        parts, kv_part = refs[10:14], refs[14]
        kv_in, exp_in, values, tiles, sems = refs[15:]
        kv_copies = [
            pltpu.make_async_copy(kv_hbm[a], kv_in.at[a], sems.at[EXPERTS, a]) for a in range(4)
        ]
        exp_copies = [
            [
                pltpu.make_async_copy(exp_hbm[a].at[e, 0], exp_in.at[a, e], sems.at[e, a])
                for a in range(4)
            ]
            for e in range(EXPERTS)
        ]
        for copies in [kv_copies] + exp_copies:
            for copy in copies:
                copy.start()
        norm = jnp.sqrt(jnp.sum(total_ref[...], keepdims=True)) + 1e-06
        factor = jnp.minimum(1.0, clip_norm / norm)
        row = lax.broadcasted_iota(jnp.int32, (TILE, LANES), 0)
        flat = row * LANES + lax.broadcasted_iota(jnp.int32, (TILE, LANES), 1)

        def block(ins, at):
            new = adam(ins[0, *at], ins[1, *at], ins[2, *at], ins[3, *at], factor)
            weights = new.astype(jnp.bfloat16).astype(jnp.float32)
            magnitude = jnp.max(jnp.abs(weights), keepdims=True)
            scaled = weights / (magnitude + scale_eps)
            return new, scaled.reshape(BLK // TILE, TILE, LANES).astype(jnp.bfloat16), magnitude

        for copy in kv_copies:
            copy.wait()
        place = place_ref[0]
        shard = lax.rem(place, 4)
        kv_tile = jnp.zeros((TILE, LANES), jnp.float32)
        for i in range(2):
            new, val, magnitude = block(kv_in, (i, 0))
            kv_new[i, 0] = new
            kv_part[8 * i : 8 * i + 8] = val
            kv_tile = jnp.where(flat == i * LANES + place, magnitude, kv_tile)
        kv_part[16] = kv_tile.astype(jnp.bfloat16)
        for e in range(EXPERTS):
            for copy in exp_copies[e]:
                copy.wait()
            tile = jnp.zeros((TILE, LANES), jnp.float32)
            for j in range(3):
                new, val, magnitude = block(exp_in, (e, j))
                exp_new[e, 0, j] = new
                values[e, 8 * j : 8 * j + 8] = val
                at = place * 3 + j
                here = jnp.logical_or(flat == at, flat == at + 2 * LANES)
                tile = jnp.where(here, magnitude, tile)
            tiles[e] = tile
        owners = [owner_ref[e] for e in range(EXPERTS)]
        for k in range(4):
            scales = jnp.zeros((TILE, LANES), jnp.float32)
            for h in range(SLOTS):
                chosen, occupied = slot_of(owners, lax.rem(shard + k, 4), h)
                picked = values[chosen]
                at = 1 + h * SLOT_T
                parts[k][at : at + SLOT_T] = jnp.where(
                    occupied > 0, picked, jnp.zeros_like(picked)
                )
                held = jnp.logical_and(lax.div(row, 2) == h, occupied > 0)
                scales = jnp.where(held, tiles[chosen], scales)
            parts[k][0] = scales.astype(jnp.bfloat16)

    f32, bf16 = jnp.float32, jnp.bfloat16
    return pl.pallas_call(
        kernel,
        out_shape=(
            jax.ShapeDtypeStruct((2, 1, BLK, BLK), f32),
            jax.ShapeDtypeStruct((EXPERTS, 1, 3, BLK, BLK), f32),
        )
        + (jax.ShapeDtypeStruct((PART_T, TILE, LANES), bf16),) * 4
        + (jax.ShapeDtypeStruct((17, TILE, LANES), bf16),),
        in_specs=[pl.BlockSpec(memory_space=SMEM)] * 2
        + [pl.BlockSpec(memory_space=VMEM)]
        + [pl.BlockSpec(memory_space=pltpu.HBM)] * 8,
        out_specs=[pl.BlockSpec(memory_space=VMEM)] * 7,
        scratch_shapes=[
            pltpu.VMEM((4, 2, 1, BLK, BLK), f32),
            pltpu.VMEM((4, EXPERTS, 3, BLK, BLK), f32),
            pltpu.VMEM((EXPERTS, SLOT_T, TILE, LANES), bf16),
            pltpu.VMEM((EXPERTS, TILE, LANES), f32),
            pltpu.SemaphoreType.DMA((EXPERTS + 1, 4)),
        ],
        compiler_params=pltpu.CompilerParams(vmem_limit_bytes=60 * 1024 * 1024),
        name="update",
    )(place, owner, total, *kv, *exp)


def join(place, parts):
    def kernel(place_ref, *refs):
        out, out_a, out_b = refs[4:]
        shard = lax.rem(place_ref[0], 4)
        tile = jnp.zeros((TILE, LANES), jnp.float32)
        for k in range(4):
            z = lax.rem(shard - k + 4, 4)
            tile += refs[k][0].astype(jnp.float32)
            for h in range(SLOTS):
                got = refs[k][1 + h * SLOT_T : 1 + (h + 1) * SLOT_T]
                out[pl.ds(1 + 4 * h * SLOT_T + z * SLOT_T, SLOT_T)] = got
        out[0] = tile.astype(jnp.bfloat16)
        out_a[...] = out[0:A_T]
        out_b[...] = out[A_T:FULL_T]

    return pl.pallas_call(
        kernel,
        out_shape=tuple(
            jax.ShapeDtypeStruct((n, TILE, LANES), jnp.bfloat16) for n in (FULL_T, A_T, FULL_T - A_T)
        ),
        in_specs=[pl.BlockSpec(memory_space=SMEM)] + [pl.BlockSpec(memory_space=VMEM)] * 4,
        out_specs=[pl.BlockSpec(memory_space=VMEM)] * 3,
        compiler_params=pltpu.CompilerParams(vmem_limit_bytes=16 * 1024 * 1024),
        name="join",
    )(place, *parts)


def join_kv(place, parts):
    def kernel(place_ref, *refs):
        out = refs[5]
        replica = lax.div(place_ref[0], 4)
        y = lax.rem(lax.div(replica, 2), 2)
        views = [(refs[0], 0, y), (refs[1], 0, 1 - y)]
        for k in (1, 2, 3):
            views += [(refs[k + 1].at[0], k, y), (refs[k + 1].at[1], k, 1 - y)]
        tile = jnp.zeros((TILE, LANES), jnp.float32)
        for ref, steps, at_y in views:
            chip = chip_along(replica, steps) * 2 + at_y
            for h in range(2):
                out[pl.ds(KV_T * (8 * h + chip), KV_T)] = ref[KV_T * h : KV_T * (h + 1)]
            tile += ref[16].astype(jnp.float32)
        out[PLANE_T - 1] = tile.astype(jnp.bfloat16)

    return pl.pallas_call(
        kernel,
        out_shape=jax.ShapeDtypeStruct((PLANE_T, TILE, LANES), jnp.bfloat16),
        in_specs=[pl.BlockSpec(memory_space=SMEM)] + [pl.BlockSpec(memory_space=VMEM)] * 5,
        out_specs=pl.BlockSpec(memory_space=VMEM),
        compiler_params=pltpu.CompilerParams(vmem_limit_bytes=16 * 1024 * 1024),
        name="join_kv",
    )(place, *parts)


def chip_along(replica, steps):
    x, c = lax.div(replica, 4), lax.rem(replica, 2)
    return lax.rem(x + 4 + jnp.where(c == 0, -steps, steps), 4)


EXP_OUT = jax.ShapeDtypeStruct((SLOTS, 16 * 4 * SLOT_T, TILE, LANES), jnp.bfloat16)
KV_OUT = jax.ShapeDtypeStruct((2, 8, 2, 4, KV_T, TILE, LANES), jnp.bfloat16)


SIZE = {"P": FULL_T, "A": A_T, "B": FULL_T - A_T, "K": PLANE_T}
SCALES = {"P": 0, "A": 0, "K": PLANE_T - 1}


def lay(place, own, got, outs=None, pack=False, last=False):
    views = [(n, 0, piece, False) for n, (_, piece) in enumerate(own)]
    for n, (_, held) in enumerate(got):
        at = 0
        for piece in held:
            views.append((len(own) + n, at, piece, True))
            at += SIZE[piece[0]]
    arrays = [array for array, _ in own + got]
    total = sum(SIZE[piece[0]] for _, piece in own)
    with_scales = [view for view in views if view[2][0] != "B"]
    count = 2 * len(views) + (len(own) if pack else 0)

    def kernel(place_ref, *refs):
        ins = refs[: len(arrays)]
        sum_in = refs[len(arrays) + 2] if outs else None
        rest = refs[len(arrays) + (3 if outs else 0) :]
        exp_out, kv_out, results = rest[0], rest[1], rest[2:-3]
        tiles, tile_sems, sems = rest[-3:]
        here = place_ref[0]
        replica, shard = lax.div(here, 4), lax.rem(here, 4)
        copies, gets = [], []

        def copy(src, dst):
            copies.append(pltpu.make_async_copy(src, dst, sems.at[len(copies)]))
            copies[-1].start()

        for i, (n, at, piece, _) in enumerate(with_scales):
            src = ins[n].at[at + SCALES[piece[0]]]
            gets.append(pltpu.make_async_copy(src, tiles.at[i], tile_sems.at[i]))
            gets[-1].start()
        if pack:
            at = 0
            for n, (_, piece) in enumerate(own):
                copy(ins[n], results[1].at[pl.ds(at, SIZE[piece[0]])])
                at += SIZE[piece[0]]
        for n, base, (kind, steps, over_y), over_c in views:
            ref = ins[n]
            c = lax.rem(replica, 2)
            if over_c:
                c = 1 - c
            forward = jnp.where(c == 0, -steps, steps)
            if kind == "K":
                z = lax.rem(shard + 4 + forward, 4)
                for h in range(2):
                    blocks = ref.at[pl.ds(base + 8 * KV_T * h, 8 * KV_T)]
                    copy(blocks.reshape(8, KV_T, TILE, LANES), kv_out.at[h, :, c, z])
                continue
            y = lax.rem(lax.div(replica, 2), 2)
            if over_y:
                y = 1 - y
            x = lax.rem(lax.div(replica, 4) + 4 + forward, 4)
            n = 4 * SLOT_T
            to = (x * 4 + y * 2 + c) * n
            first = A_T - 1 - n
            if kind in "PA":
                copy(ref.at[pl.ds(base + 1, n)], exp_out.at[0, pl.ds(to, n)])
            if kind == "P":
                copy(ref.at[pl.ds(base + 1 + n, n)], exp_out.at[1, pl.ds(to, n)])
            if kind == "A":
                copy(ref.at[pl.ds(base + 1 + n, first)], exp_out.at[1, pl.ds(to, first)])
            if kind == "B":
                copy(ref.at[pl.ds(base, n - first)], exp_out.at[1, pl.ds(to + first, n - first)])
        for get in gets:
            get.wait()
        sums = [jnp.zeros((TILE, LANES), jnp.float32) for _ in range(2)]
        if outs:
            sums = [sum_in[0], sum_in[1]]
        for i, (_, _, piece, _) in enumerate(with_scales):
            sums[piece[0] == "K"] += tiles[i].astype(jnp.float32)
        if last:
            results[0][0] = sums[0][0:2]
            results[0][1] = sums[0][2:4]
            results[1][...] = sums[1][0:2]
        else:
            results[0][0] = sums[0]
            results[0][1] = sums[1]
        for c in copies:
            c.wait()

    out_shape = [EXP_OUT, KV_OUT]
    out_specs = [pl.BlockSpec(memory_space=pl.ANY)] * 2
    if last:
        out_shape += [
            jax.ShapeDtypeStruct((SLOTS, 2, LANES), jnp.float32),
            jax.ShapeDtypeStruct((2, LANES), jnp.float32),
        ]
        out_specs += [pl.BlockSpec(memory_space=VMEM)] * 2
    else:
        out_shape += [jax.ShapeDtypeStruct((2, TILE, LANES), jnp.float32)]
        out_specs += [pl.BlockSpec(memory_space=VMEM)]
    if pack:
        out_shape += [jax.ShapeDtypeStruct((total, TILE, LANES), jnp.bfloat16)]
        out_specs += [pl.BlockSpec(memory_space=pltpu.HBM)]
    first_out = 1 + len(arrays)
    return pl.pallas_call(
        kernel,
        out_shape=tuple(out_shape),
        in_specs=[pl.BlockSpec(memory_space=SMEM)]
        + [pl.BlockSpec(memory_space=pl.ANY)] * (len(arrays) + (2 if outs else 0))
        + [pl.BlockSpec(memory_space=VMEM)] * (1 if outs else 0),
        out_specs=tuple(out_specs),
        scratch_shapes=[
            pltpu.VMEM((len(with_scales), TILE, LANES), jnp.bfloat16),
            pltpu.SemaphoreType.DMA((len(with_scales),)),
            pltpu.SemaphoreType.DMA((count,)),
        ],
        input_output_aliases={first_out: 0, first_out + 1: 1} if outs else {},
        compiler_params=pltpu.CompilerParams(vmem_limit_bytes=4 * 1024 * 1024),
        cost_estimate=pl.CostEstimate(flops=0, transcendentals=0, bytes_accessed=count * 2**19),
        name="lay",
    )(place, *arrays, *(outs or []))


def after(*values):
    return lax.optimization_barrier(values)


def swap_core(v):
    return lax.ppermute(v, "c", ring(2, 1))


def swap_y(v):
    return lax.ppermute(v, "yl", ring(2, 1))


def along_x(v, k=1):
    step = (k, 4 - k)
    pairs = [(2 * x + c, 2 * ((x + step[c]) % 4) + c) for x in range(4) for c in range(2)]
    return lax.ppermute(v, ("x", "c"), pairs)


def along_z(v):
    pairs = [(4 * c + z, 4 * c + (z + (3 if c else 1)) % 4) for c in range(2) for z in range(4)]
    return lax.ppermute(v, ("c", "z"), pairs)


def per_device(
    kv_param, kv_grad, kv_mean, kv_square, exp_param, exp_grad, exp_mean, exp_square, expert_owner
):
    total = sum_over_devices(sum_of_squares(kv_grad, exp_grad))
    place = lax.axis_index(SHARD).astype(jnp.int32).reshape(1)
    kv_new, exp_new, *parts, kv_part = update(
        place,
        expert_owner,
        total,
        (kv_param, kv_grad, kv_mean, kv_square),
        (exp_param, exp_grad, exp_mean, exp_square),
    )
    parts = [parts[0]] + [lax.ppermute(parts[k], "z", ring(4, k)) for k in (1, 2, 3)]
    kv_across = swap_y(kv_part)
    *parts, kv_part, kv_across = after(*parts, kv_part, kv_across)

    p0, a_own, b_own = join(place, parts)
    p1, qa = along_x(p0), swap_y(a_own)
    kv_two = jnp.stack([kv_part, kv_across])
    k1, k2, k3 = (along_x(kv_two, k) for k in (1, 2, 3))
    p1, qa, b_own, k1, k2, k3 = after(p1, qa, b_own, k1, k2, k3)

    w0 = join_kv(place, (kv_part, kv_across, k1, k2, k3))
    p2, a1, qb, b1, w1 = along_x(p1), along_x(qa), swap_y(b_own), swap_y(p1[A_T:FULL_T]), along_z(w0)
    held1 = [("P", 0, False), ("P", 1, False), ("A", 0, True)]
    *outs, pack1 = lay(place, list(zip([p0, p1, qa], held1)), [], pack=True)
    p2, a1, qb, b1, w1, pack1, *outs = after(p2, a1, qb, b1, w1, pack1, *outs)

    p3, a2, b2, w2 = along_x(p2), along_x(a1), swap_y(p2[A_T:FULL_T]), along_z(w1)
    got1 = swap_core(pack1)
    held2 = [("P", 2, False), ("A", 1, True), ("B", 0, True), ("B", 1, True)]
    held2 += [("K", 0, False), ("K", 1, False)]
    own = [p2, a1, qb, b1, w0, w1]
    *outs, pack2 = lay(place, list(zip(own, held2)), [], outs, pack=True)
    p3, a2, b2, w2, got1, pack2, *outs = after(p3, a2, b2, w2, got1, pack2, *outs)

    a3, b3, w3 = along_x(a2), swap_y(p3[A_T:FULL_T]), along_z(w2)
    got2, got3 = swap_core(pack2), swap_core(p3)
    held3 = [("A", 2, True), ("B", 2, True), ("K", 2, False)]
    own = list(zip([a2, b2, w2], held3))
    *outs, pack3 = lay(place, own, [(got1, held1)], outs, pack=True)
    a3, b3, w3, got2, got3, pack3, *outs = after(a3, b3, w3, got2, got3, pack3, *outs)

    held4 = [("A", 3, True), ("B", 3, True), ("K", 3, False)]
    got4 = [(swap_core(v), [p]) for v, p in zip((a3, b3, w3), held4)]
    got4.append((swap_core(pack3), held3))
    own = list(zip([p3, a3, b3, w3], [("P", 3, False)] + held4))
    outs = lay(place, own, [(got2, held2), (got3, [("P", 3, False)])], outs)
    exp_rollout, kv_rollout, exp_scales, kv_scales = lay(place, [], got4, outs, last=True)
    return (
        kv_new,
        exp_new,
        kv_rollout.reshape(2, 64, BLK, BLK),
        kv_scales[:, 0:64],
        exp_rollout.reshape(SLOTS, 1, 192, BLK, BLK),
        exp_scales.reshape(SLOTS, 1, 2 * LANES)[:, :, 0:192],
    )


def solution(mesh):
    fine = Mesh(mesh.devices.reshape(4, 2, 2, 4, 2), ("x", "yl", "c", "z", "yh"))
    kv = P("yh", SHARD, None, None)
    exp = P(None, "yh", SHARD, None, None)
    return jax.shard_map(
        per_device,
        mesh=fine,
        in_specs=(kv, kv, kv, kv, exp, exp, exp, exp, P()),
        out_specs=(
            kv,
            exp,
            P("yh", None, None, None),
            P("yh", None),
            P("z", "yh", None, None, None),
            P("z", "yh", None),
        ),
        check_vma=False,
    )
```

time: 198 us -> 128 us (0.65)
  blocking collectives: 53.4 us -> 0 us
  starting transfers between devices: 16.1 us -> 51.4 us
  local copies, waits for them, and re-layouts: 28.1 us -> 1.86 us
  between operations: 24.2 us -> 0.92 us
  waiting for transfers between devices: 70 us -> 53.7 us
  Pallas kernels: 4.57 us -> 17.3 us
    all_gather x2 -> x0, waiting for transfers between devices: 63.5 us -> none  [the longest x1 63.5 us: per_device(): exp_rollout = lax.all_gather(arrived, REPLICA, axis=2, tiled=True)]
    ppermute x0 -> x28, waiting for transfers between devices: none -> 47.1 us  [the longest x6 20.5 us: swap_y(): return lax.ppermute(v, 'yl', ring(2, 1))]
    psum x4 -> x0, blocking collectives: 31.6 us -> none  [per_device(): scales = lax.psum(scales, axis)]
    ppermute x0 -> x28, starting transfers between devices: none -> 29.8 us  [the longest x7 7.78 us: swap_core(): return lax.ppermute(v, 'c', ring(2, 1))]
    unnamed x21 -> x4, local copies, waits for them, and re-layouts: 24.9 us -> 1.81 us
    all_to_all x1 -> x0, blocking collectives: 11.7 us -> none  [per_device(): arrived = lax.all_to_all(routed, 'z', 0, 0, tiled=True)]
    pallas_call x0 -> x7, Pallas kernels: none -> 10.8 us  [the longest x5 10.6 us: lay(): pl.pallas_call(kernel, out_shape=tuple(out_shape), in_specs=[pl.BlockSpec...]
    all_gather x1 -> x0, blocking collectives: 10.1 us -> none  [per_device(): kv_plane = lax.all_gather(kv_val, 'z', axis=1, tiled=True)]
  transfers between devices with their start and end apart: 11 -> 37, of which waited for: 8 -> 18; matrix products, arithmetic and copies ran while one was open for 2% -> 1% of each run, Pallas kernels for 0% -> 7%
where the time goes in v3:
time: 128 us; the launch traced here: 127 us
  waiting for transfers between devices  53.7 us (42%)
  starting transfers between devices  51.4 us (40%)
  Pallas kernels  17.3 us (14%)
  other arithmetic  2.19 us (2%)
  local copies, waits for them, and re-layouts  1.86 us (1%)
    ppermute x6, waiting for transfers between devices, swap_y(): return lax.ppermute(v, 'yl', ring(2, 1))  20.5 us
    ppermute x9, waiting for transfers between devices, along_x(): return lax.ppermute(v, ('x', 'c'), pairs)  18.9 us
    ppermute x6, starting transfers between devices, sum_over_devices(): others = [lax.ppermute(v, axis, ring(4, k)) for k in (1, 2, 3)]  11.3 us
    pallas_call x5, Pallas kernels, lay(): pl.pallas_call(kernel, out_shape=tuple(out_shape), in_specs=[pl.BlockSpec...  10.6 us
    ppermute x3, starting transfers between devices, sum_over_devices(): v = v + lax.ppermute(v, axis, ring(2, 1))  10.3 us
    ppermute x7, starting transfers between devices, swap_core(): return lax.ppermute(v, 'c', ring(2, 1))  7.78 us
    ppermute x9, starting transfers between devices, along_x(): return lax.ppermute(v, ('x', 'c'), pairs)  7.19 us
    ppermute x6, starting transfers between devices, swap_y(): return lax.ppermute(v, 'yl', ring(2, 1))  6.87 us
  transfers between devices with their start and end apart: 37, of which 18 were waited for; matrix products, arithmetic and copies ran while one was open for 1% of the time, Pallas kernels for 7%

profile of v3, /device:TPU:1, one launch (start us, length us, event | category | flops | bytes accessed | tf_op | source)
XLA Modules:
  0.0 127.4 jit_solution(11825037642968842357)
XLA Ops:
  0.6 1.9 %sum_of_squares.1 = f32[8,128]{1,0:T(8,128)} custom-call(f32[2,1,128,128]{3,2,1,0:T(8,128)} %refs_1_.1, f32[4,1,3,128,128]{4,3,2,1,0:T(8,128)} %refs_5_.1), custom_call_target="tpu_custom_call" | custom-call | tf_op jit(solution)/shard_map/sum_of_squares/pallas_call | solution.py:52
  2.5 2.0 %collective-permute-start = (f32[8,128]{1,0:T(8,128)}, f32[8,128]{1,0:T(8,128)S(1)}, u32[]{:S(2)}, u32[]{:S(2)}) collective-permute-start(f32[8,128]{1,0:T(8,128)} %sum_of_squares.1), channel_id=1, source_target_pairs={{0,32},{32,64},{64,96},{96,0},{1,33},{33,65},{65,97},{97,1},{2,34}... | collective-permute-start | bytes 12296 | tf_op jit(solution)/shard_map/ppermute | solution.py:63
  4.5 2.5 %collective-permute-start.1 = (f32[8,128]{1,0:T(8,128)}, f32[8,128]{1,0:T(8,128)S(1)}, u32[]{:S(2)}, u32[]{:S(2)}) collective-permute-start(f32[8,128]{1,0:T(8,128)} %sum_of_squares.1), channel_id=1, source_target_pairs={{0,64},{32,96},{64,0},{96,32},{1,65},{33,97},{65,1},{97,33},{2,66}... | collective-permute-start | bytes 12296 | tf_op jit(solution)/shard_map/ppermute | solution.py:63
  7.0 1.2 collective-permute-start.2
  8.2 0.6 collective-permute-done.1
  8.7 1.2 collective-permute-done.2
  10.0 0.7 add_add_fusion.1
  10.7 1.6 %collective-permute-start.3 = (f32[8,128]{1,0:T(8,128)S(1)}, f32[8,128]{1,0:T(8,128)S(1)}, u32[]{:S(2)}, u32[]{:S(2)}) collective-permute-start(f32[8,128]{1,0:T(8,128)S(1)} %add_add_fusion.1), channel_id=1, source_target_pairs={{0,2},{2,4},{4,6},{6,0},{1,3},{3,5},{5,7},{7,1},{8,10},{10,12},{12... | collective-permute-start | bytes 12296 | tf_op jit(solution)/shard_map/ppermute | solution.py:63
  12.3 3.3 %collective-permute-start.4 = (f32[8,128]{1,0:T(8,128)S(1)}, f32[8,128]{1,0:T(8,128)S(1)}, u32[]{:S(2)}, u32[]{:S(2)}) collective-permute-start(f32[8,128]{1,0:T(8,128)S(1)} %add_add_fusion.1), channel_id=1, source_target_pairs={{0,4},{2,6},{4,0},{6,2},{1,5},{3,7},{5,1},{7,3},{8,12},{10,14},{12... | collective-permute-start | bytes 12296 | tf_op jit(solution)/shard_map/ppermute | solution.py:63
  15.6 0.7 collective-permute-start.5
  16.3 0.3 collective-permute-done.4
  16.6 1.4 %collective-permute-done.5 = f32[8,128]{1,0:T(8,128)S(1)} collective-permute-done((f32[8,128]{1,0:T(8,128)S(1)}, f32[8,128]{1,0:T(8,128)S(1)}, u32[]{:S(2)}, u32[]{:S(2)}) %collective-permute-start.5) | collective-permute-done | bytes 4128 | tf_op jit(solution)/shard_map/ppermute | solution.py:63
  18.1 1.3 %collective-permute-start.6 = (f32[8,128]{1,0:T(8,128)S(1)}, f32[8,128]{1,0:T(8,128)S(1)}, u32[]{:S(2)}, u32[]{:S(2)}) collective-permute-start(f32[8,128]{1,0:T(8,128)S(1)} %add_add_fusion), channel_id=1, source_target_pairs={{0,16},{16,0},{1,17},{17,1},{2,18},{18,2},{3,19},{19,3},{4,20},{20... | collective-permute-start | bytes 12296 | tf_op jit(solution)/shard_map/ppermute | solution.py:66
  19.4 1.2 collective-permute-done.6
  20.5 2.9 %collective-permute-start.7 = (f32[8,128]{1,0:T(8,128)S(1)}, f32[8,128]{1,0:T(8,128)S(1)}, u32[]{:S(2)}, u32[]{:S(2)}) collective-permute-start(f32[8,128]{1,0:T(8,128)S(1)} %add.45), channel_id=1, source_target_pairs={{0,1},{1,0},{2,3},{3,2},{4,5},{5,4},{6,7},{7,6},{8,9},{9,8},{10,11... | collective-permute-start | bytes 12296 | tf_op jit(solution)/shard_map/ppermute | solution.py:66
  23.4 1.0 collective-permute-done.7
  24.5 6.1 %collective-permute-start.8 = (f32[8,128]{1,0:T(8,128)S(1)}, f32[8,128]{1,0:T(8,128)S(1)}, u32[]{:S(2)}, u32[]{:S(2)}) collective-permute-start(f32[8,128]{1,0:T(8,128)S(1)} %add.46), channel_id=1, source_target_pairs={{0,8},{8,0},{1,9},{9,1},{2,10},{10,2},{3,11},{11,3},{4,12},{12,4},... | collective-permute-start | bytes 12296 | tf_op jit(solution)/shard_map/ppermute | solution.py:66
  30.6 0.8 collective-permute-done.8
  31.4 0.6 add.47.total_ref
  32.0 4.7 %update.1 = (f32[2,1,128,128]{3,2,1,0:T(8,128)}, f32[4,1,3,128,128]{4,3,2,1,0:T(8,128)}, bf16[49,16,128]{2,1,0:T(8,128)(2,1)}, bf16[49,16,128]{2,1,0:T(8,128)(2,...) custom-call(s32[1]{0:T(128)} %bitcast.place_ref, s32[4]{0:T(128)} %owner_ref.1, ...), custom_call_target="tpu_custom_call" | custom-call | tf_op jit(solution)/shard_map/update/pallas_call | solution.py:162
  36.7 1.4 %collective-permute-start.10 = (bf16[49,16,128]{2,1,0:T(8,128)(2,1)}, bf16[49,16,128]{2,1,0:T(8,128)(2,1)S(1)}, u32[]{:S(2)}, u32[]{:S(2)}) collective-permute-start(bf16[49,16,128]{2,1,0:T(8,128)(2,1)} %get-tuple-element.78), channel_id=1, source_target_pairs={{0,4},{2,6},{4,0},{6,2},{1,5},{3,7},{5,1},{7,3},{8,12},{10,14},{12... | collective-permute-start | bytes 602120 | tf_op jit(solution)/shard_map/ppermute | solution.py:400
  38.1 0.7 collective-permute-start.11
  38.8 0.7 collective-permute-start.9
  39.6 1.3 %collective-permute-start.12 = (bf16[17,16,128]{2,1,0:T(8,128)(2,1)}, bf16[17,16,128]{2,1,0:T(8,128)(2,1)S(1)}, u32[]{:S(2)}, u32[]{:S(2)}) collective-permute-start(bf16[17,16,128]{2,1,0:T(8,128)(2,1)} %get-tuple-element.88.refs_0_), channel_id=1, source_target_pairs={{0,16},{16,0},{1,17},{17,1},{2,18},{18,2},{3,19},{19,3},{4,20},{20... | collective-permute-start | bytes 208904 | tf_op jit(solution)/shard_map/ppermute | solution.py:374
  40.9 2.4 %collective-permute-done.12.refs_1_ = bf16[17,16,128]{2,1,0:T(8,128)(2,1)S(1)} collective-permute-done((bf16[17,16,128]{2,1,0:T(8,128)(2,1)}, bf16[17,16,128]{2,1,0:T(8,128)(2,1)S(1)}, u32[]{:S(2)}, u32[]{:S(2)}) %collective-permute-start.12) | collective-permute-done | bytes 69664 | tf_op jit(solution)/shard_map/ppermute | solution.py:374
  43.2 1.5 %collective-permute-done.10.refs_2_ = bf16[49,16,128]{2,1,0:T(8,128)(2,1)S(1)} collective-permute-done((bf16[49,16,128]{2,1,0:T(8,128)(2,1)}, bf16[49,16,128]{2,1,0:T(8,128)(2,1)S(1)}, u32[]{:S(2)}, u32[]{:S(2)}) %collective-permute-start.10) | collective-permute-done | bytes 200736 | tf_op jit(solution)/shard_map/ppermute | solution.py:400
  44.8 3.9 %collective-permute-done.11.refs_3_ = bf16[49,16,128]{2,1,0:T(8,128)(2,1)S(1)} collective-permute-done((bf16[49,16,128]{2,1,0:T(8,128)(2,1)}, bf16[49,16,128]{2,1,0:T(8,128)(2,1)S(1)}, u32[]{:S(2)}, u32[]{:S(2)}) %collective-permute-start.11) | collective-permute-done | bytes 200736 | tf_op jit(solution)/shard_map/ppermute | solution.py:400
  48.6 1.1 collective-permute-done.9.refs_1_
  49.7 0.9 copy-done.1
  50.6 0.1 join.1
  50.8 2.4 %collective-permute-start.13 = (bf16[193,16,128]{2,1,0:T(8,128)(2,1)S(1)}, bf16[193,16,128]{2,1,0:T(8,128)(2,1)S(1)}, u32[]{:S(2)}, u32[]{:S(2)}) collective-permute-start(bf16[193,16,128]{2,1,0:T(8,128)(2,1)S(1)} %get-tuple-element.85.refs_0_), channel_id=1, source_target_pairs={{0,32},{8,104},{32,64},{40,8},{64,96},{72,40},{96,0},{104,72},{1,3... | collective-permute-start | bytes 2371592 | tf_op jit(solution)/shard_map/ppermute | solution.py:380
  53.2 1.3 %collective-permute-start.14 = (bf16[129,16,128]{2,1,0:T(8,128)(2,1)S(1)}, bf16[129,16,128]{2,1,0:T(8,128)(2,1)S(1)}, u32[]{:S(2)}, u32[]{:S(2)}) collective-permute-start(bf16[129,16,128]{2,1,0:T(8,128)(2,1)S(1)} %get-tuple-element.86), channel_id=1, source_target_pairs={{0,16},{16,0},{1,17},{17,1},{2,18},{18,2},{3,19},{19,3},{4,20},{20... | collective-permute-start | bytes 1585160 | tf_op jit(solution)/shard_map/ppermute | solution.py:374
  54.5 0.9 pad_maximum_fusion
  55.4 0.2 collective-permute-start.15
  55.6 0.8 collective-permute-start.16
  56.4 0.6 collective-permute-start.17
  56.9 11.2 %collective-permute-done.15.refs_2_ = bf16[2,17,16,128]{3,2,1,0:T(8,128)(2,1)S(1)} collective-permute-done((bf16[2,17,16,128]{3,2,1,0:T(8,128)(2,1)S(1)}, bf16[2,17,16,128]{3,2,1,0:T(8,128)(2,1)S(1)}, u32[]{:S(2)}, u32[]{:S(2)}) %collective-permute-start.15) | collective-permute-done | bytes 139296 | tf_op jit(solution)/shard_map/ppermute | solution.py:380
  68.2 3.2 %collective-permute-start.18 = (bf16[193,16,128]{2,1,0:T(8,128)(2,1)S(1)}, bf16[193,16,128]{2,1,0:T(8,128)(2,1)S(1)}, u32[]{:S(2)}, u32[]{:S(2)}) collective-permute-start(bf16[193,16,128]{2,1,0:T(8,128)(2,1)S(1)} %collective-permute-done.13.refs_1_), channel_id=1, source_target_pairs={{0,32},{8,104},{32,64},{40,8},{64,96},{72,40},{96,0},{104,72},{1,3... | collective-permute-start | bytes 2371592 | tf_op jit(solution)/shard_map/ppermute | solution.py:380
  71.4 0.9 copy-done
  72.3 1.6 %collective-permute-start.22 = (bf16[129,16,128]{2,1,0:T(8,128)(2,1)S(1)}, bf16[129,16,128]{2,1,0:T(8,128)(2,1)S(1)}, u32[]{:S(2)}, u32[]{:S(2)}) collective-permute-start(bf16[129,16,128]{2,1,0:T(8,128)(2,1)S(1)} %join_kv.1.refs_4_), channel_id=1, source_target_pairs={{0,2},{2,4},{4,6},{6,0},{8,14},{10,8},{12,10},{14,12},{1,3},{3,5},... | collective-permute-start | bytes 1585160 | tf_op jit(solution)/shard_map/ppermute | solution.py:385
  74.0 1.4 %collective-permute-start.21 = (bf16[64,16,128]{2,1,0:T(8,128)(2,1)S(1)}, bf16[64,16,128]{2,1,0:T(8,128)(2,1)S(1)}, u32[]{:S(2)}, u32[]{:S(2)}) collective-permute-start(bf16[64,16,128]{2,1,0:T(8,128)(2,1)S(1)} %slice.15), channel_id=1, source_target_pairs={{0,16},{16,0},{1,17},{17,1},{2,18},{18,2},{3,19},{19,3},{4,20},{20... | collective-permute-start | bytes 786440 | tf_op jit(solution)/shard_map/ppermute | solution.py:374
  75.3 0.2 collective-permute-start.20
  75.5 1.6 %lay.5 = (bf16[2,1536,16,128]{3,2,1,0:T(8,128)(2,1)}, bf16[2,8,2,4,8,16,128]{6,5,4,3,2,1,0:T(8,128)(2,1)}, f32[2,16,128]{2,1,0:T(8,128)S(1)}, bf16[515,16,128]{2,1,0:T(8,128)(2,1)S(1)}) custom-call(s32[1]{0:T(128)} %bitcast.place_ref, bf16[193,16,128]{2,1,0:T(8,128)(2,1)S(1)} %get-tuple-element.85.refs_0_, ...), custom_call_target="tpu_custom_call" | custom-call | bytes 4718592 | tf_op jit(solution)/shard_map/lay/pallas_call | solution.py:346
  77.1 5.2 %collective-permute-done.21.refs_3_ = bf16[64,16,128]{2,1,0:T(8,128)(2,1)S(1)} collective-permute-done((bf16[64,16,128]{2,1,0:T(8,128)(2,1)S(1)}, bf16[64,16,128]{2,1,0:T(8,128)(2,1)S(1)}, u32[]{:S(2)}, u32[]{:S(2)}) %collective-permute-start.21) | collective-permute-done | bytes 262176 | tf_op jit(solution)/shard_map/ppermute | solution.py:374
  82.3 4.8 %collective-permute-done.20.refs_2_ = bf16[64,16,128]{2,1,0:T(8,128)(2,1)S(1)} collective-permute-done((bf16[64,16,128]{2,1,0:T(8,128)(2,1)S(1)}, bf16[64,16,128]{2,1,0:T(8,128)(2,1)S(1)}, u32[]{:S(2)}, u32[]{:S(2)}) %collective-permute-start.20) | collective-permute-done | bytes 262176 | tf_op jit(solution)/shard_map/ppermute | solution.py:374
  87.2 3.3 %collective-permute-start.27 = (bf16[515,16,128]{2,1,0:T(8,128)(2,1)S(1)}, bf16[515,16,128]{2,1,0:T(8,128)(2,1)S(1)}, u32[]{:S(2)}, u32[]{:S(2)}) collective-permute-start(bf16[515,16,128]{2,1,0:T(8,128)(2,1)S(1)} %get-tuple-element.103), channel_id=1, source_target_pairs={{0,8},{8,0},{1,9},{9,1},{2,10},{10,2},{3,11},{11,3},{4,12},{12,4},... | collective-permute-start | bytes 6328328 | tf_op jit(solution)/shard_map/ppermute | solution.py:370
  90.4 1.7 %collective-permute-start.26 = (bf16[129,16,128]{2,1,0:T(8,128)(2,1)S(1)}, bf16[129,16,128]{2,1,0:T(8,128)(2,1)S(1)}, u32[]{:S(2)}, u32[]{:S(2)}) collective-permute-start(bf16[129,16,128]{2,1,0:T(8,128)(2,1)S(1)} %collective-permute-done.22.refs_5_), channel_id=1, source_target_pairs={{0,2},{2,4},{4,6},{6,0},{8,14},{10,8},{12,10},{14,12},{1,3},{3,5},... | collective-permute-start | bytes 1585160 | tf_op jit(solution)/shard_map/ppermute | solution.py:385
  92.2 1.4 %collective-permute-start.25 = (bf16[64,16,128]{2,1,0:T(8,128)(2,1)S(1)}, bf16[64,16,128]{2,1,0:T(8,128)(2,1)S(1)}, u32[]{:S(2)}, u32[]{:S(2)}) collective-permute-start(bf16[64,16,128]{2,1,0:T(8,128)(2,1)S(1)} %slice.16), channel_id=1, source_target_pairs={{0,16},{16,0},{1,17},{17,1},{2,18},{18,2},{3,19},{19,3},{4,20},{20... | collective-permute-start | bytes 786440 | tf_op jit(solution)/shard_map/ppermute | solution.py:374
  93.6 2.0 %lay.6 = (bf16[2,1536,16,128]{3,2,1,0:T(8,128)(2,1)}, bf16[2,8,2,4,8,16,128]{6,5,4,3,2,1,0:T(8,128)(2,1)}, f32[2,16,128]{2,1,0:T(8,128)S(1)}, bf16[708,16,128]{2,1,0:T(8,128)(2,1)S(1)}) custom-call(s32[1]{0:T(128)} %bitcast.place_ref, bf16[193,16,128]{2,1,0:T(8,128)(2,1)S(1)} %collective-permute-done.18.refs_0_, ...), custom_call_target="tpu_custom_call", output_to_operand_aliasing={{0}: (7, {}), {1}: (8, {})} | custom-call | bytes 9437184 | tf_op jit(solution)/shard_map/lay/pallas_call | solution.py:346
  95.6 4.0 %collective-permute-done.25.refs_1_ = bf16[64,16,128]{2,1,0:T(8,128)(2,1)S(1)} collective-permute-done((bf16[64,16,128]{2,1,0:T(8,128)(2,1)S(1)}, bf16[64,16,128]{2,1,0:T(8,128)(2,1)S(1)}, u32[]{:S(2)}, u32[]{:S(2)}) %collective-permute-start.25) | collective-permute-done | bytes 262176 | tf_op jit(solution)/shard_map/ppermute | solution.py:374
  99.6 7.7 %collective-permute-done.24.refs_0_ = bf16[129,16,128]{2,1,0:T(8,128)(2,1)S(1)} collective-permute-done((bf16[129,16,128]{2,1,0:T(8,128)(2,1)S(1)}, bf16[129,16,128]{2,1,0:T(8,128)(2,1)S(1)}, u32[]{:S(2)}, u32[]{:S(2)}) %collective-permute-start.24) | collective-permute-done | bytes 528416 | tf_op jit(solution)/shard_map/ppermute | solution.py:380
  107.3 2.1 %collective-permute-start.31 = (bf16[708,16,128]{2,1,0:T(8,128)(2,1)S(1)}, bf16[708,16,128]{2,1,0:T(8,128)(2,1)S(1)}, u32[]{:S(2)}, u32[]{:S(2)}) collective-permute-start(bf16[708,16,128]{2,1,0:T(8,128)(2,1)S(1)} %get-tuple-element.116), channel_id=1, source_target_pairs={{0,8},{8,0},{1,9},{9,1},{2,10},{10,2},{3,11},{11,3},{4,12},{12,4},... | collective-permute-start | bytes 8699912 | tf_op jit(solution)/shard_map/ppermute | solution.py:370
  109.4 0.3 collective-permute-start.32
  109.7 1.7 %collective-permute-start.30 = (bf16[129,16,128]{2,1,0:T(8,128)(2,1)S(1)}, bf16[129,16,128]{2,1,0:T(8,128)(2,1)S(1)}, u32[]{:S(2)}, u32[]{:S(2)}) collective-permute-start(bf16[129,16,128]{2,1,0:T(8,128)(2,1)S(1)} %collective-permute-done.26.refs_2_), channel_id=1, source_target_pairs={{0,2},{2,4},{4,6},{6,0},{8,14},{10,8},{12,10},{14,12},{1,3},{3,5},... | collective-permute-start | bytes 1585160 | tf_op jit(solution)/shard_map/ppermute | solution.py:385
  111.5 1.4 %collective-permute-start.29 = (bf16[64,16,128]{2,1,0:T(8,128)(2,1)S(1)}, bf16[64,16,128]{2,1,0:T(8,128)(2,1)S(1)}, u32[]{:S(2)}, u32[]{:S(2)}) collective-permute-start(bf16[64,16,128]{2,1,0:T(8,128)(2,1)S(1)} %slice.17), channel_id=1, source_target_pairs={{0,16},{16,0},{1,17},{17,1},{2,18},{18,2},{3,19},{19,3},{4,20},{20... | collective-permute-start | bytes 786440 | tf_op jit(solution)/shard_map/ppermute | solution.py:374
  112.8 2.0 %lay.7 = (bf16[2,1536,16,128]{3,2,1,0:T(8,128)(2,1)}, bf16[2,8,2,4,8,16,128]{6,5,4,3,2,1,0:T(8,128)(2,1)}, f32[2,16,128]{2,1,0:T(8,128)S(1)}, bf16[322,16,128]{2,1,0:T(8,128)(2,1)S(1)}) custom-call(s32[1]{0:T(128)} %bitcast.place_ref, bf16[129,16,128]{2,1,0:T(8,128)(2,1)S(1)} %collective-permute-done.24.refs_0_, ...), custom_call_target="tpu_custom_call", output_to_operand_aliasing={{0}: (5, {}), {1}: (6, {})} | custom-call | bytes 7864320 | tf_op jit(solution)/shard_map/lay/pallas_call | solution.py:346
  114.9 4.1 %collective-permute-done.29.refs_2_ = bf16[64,16,128]{2,1,0:T(8,128)(2,1)S(1)} collective-permute-done((bf16[64,16,128]{2,1,0:T(8,128)(2,1)S(1)}, bf16[64,16,128]{2,1,0:T(8,128)(2,1)S(1)}, u32[]{:S(2)}, u32[]{:S(2)}) %collective-permute-start.29) | collective-permute-done | bytes 262176 | tf_op jit(solution)/shard_map/ppermute | solution.py:374
  119.0 1.5 %collective-permute-start.36 = (bf16[322,16,128]{2,1,0:T(8,128)(2,1)S(1)}, bf16[322,16,128]{2,1,0:T(8,128)(2,1)S(1)}, u32[]{:S(2)}, u32[]{:S(2)}) collective-permute-start(bf16[322,16,128]{2,1,0:T(8,128)(2,1)S(1)} %get-tuple-element.129), channel_id=1, source_target_pairs={{0,8},{8,0},{1,9},{9,1},{2,10},{10,2},{3,11},{11,3},{4,12},{12,4},... | collective-permute-start | bytes 3956744 | tf_op jit(solution)/shard_map/ppermute | solution.py:370
  120.5 0.1 collective-permute-start.33
  120.5 0.4 collective-permute-start.35
  121.0 0.1 collective-permute-start.34
  121.1 2.8 %lay.8 = (bf16[2,1536,16,128]{3,2,1,0:T(8,128)(2,1)}, bf16[2,8,2,4,8,16,128]{6,5,4,3,2,1,0:T(8,128)(2,1)}, f32[2,16,128]{2,1,0:T(8,128)S(1)}) custom-call(s32[1]{0:T(128)} %bitcast.place_ref, bf16[193,16,128]{2,1,0:T(8,128)(2,1)S(1)} %collective-permute-done.23.refs_0_, ...), custom_call_target="tpu_custom_call", output_to_operand_aliasing={{0}: (7, {}), {1}: (8, {})} | custom-call | bytes 11534336 | tf_op jit(solution)/shard_map/lay/pallas_call | solution.py:346
  123.8 1.2 collective-permute-done.34.refs_1_
  125.0 2.2 %lay.9 = (bf16[2,1536,16,128]{3,2,1,0:T(8,128)(2,1)}, bf16[2,8,2,4,8,16,128]{6,5,4,3,2,1,0:T(8,128)(2,1)}, f32[2,2,128]{2,1,0:T(2,128)}, f32[2,128]{1,0:T(2,128)}) custom-call(s32[1]{0:T(128)} %bitcast.place_ref, bf16[129,16,128]{2,1,0:T(8,128)(2,1)S(1)} %collective-permute-done.33.refs_0_, ...), custom_call_target="tpu_custom_call", output_to_operand_aliasing={{0}: (5, {}), {1}: (6, {})} | custom-call | bytes 6291456 | tf_op jit(solution)/shard_map/lay/pallas_call | solution.py:346
  (32 shorter events, 0.2 us)
Async XLA Ops:
  2.5 5.6 %collective-permute-start = (f32[8,128]{1,0:T(8,128)}, f32[8,128]{1,0:T(8,128)S(1)}, u32[]{:S(2)}, u32[]{:S(2)}) collective-permute-start(f32[8,128]{1,0:T(8,128)} %sum_of_squares.1), channel_id=1, source_target_pairs={{0,32},{32,64},{64,96},{96,0},{1,33},{33,65},{65,97},{97,1},{2,34}... | collective-permute-start | bytes 12296 | tf_op jit(solution)/shard_map/ppermute | solution.py:63
  4.5 4.2 %collective-permute-start.1 = (f32[8,128]{1,0:T(8,128)}, f32[8,128]{1,0:T(8,128)S(1)}, u32[]{:S(2)}, u32[]{:S(2)}) collective-permute-start(f32[8,128]{1,0:T(8,128)} %sum_of_squares.1), channel_id=1, source_target_pairs={{0,64},{32,96},{64,0},{96,32},{1,65},{33,97},{65,1},{97,33},{2,66}... | collective-permute-start | bytes 12296 | tf_op jit(solution)/shard_map/ppermute | solution.py:63
  7.0 3.0 %collective-permute-start.2 = (f32[8,128]{1,0:T(8,128)}, f32[8,128]{1,0:T(8,128)S(1)}, u32[]{:S(2)}, u32[]{:S(2)}) collective-permute-start(f32[8,128]{1,0:T(8,128)} %sum_of_squares.1), channel_id=1, source_target_pairs={{0,96},{32,0},{64,32},{96,64},{1,97},{33,1},{65,33},{97,65},{2,98}... | collective-permute-start | bytes 12296 | tf_op jit(solution)/shard_map/ppermute | solution.py:63
  10.7 5.7 %collective-permute-start.3 = (f32[8,128]{1,0:T(8,128)S(1)}, f32[8,128]{1,0:T(8,128)S(1)}, u32[]{:S(2)}, u32[]{:S(2)}) collective-permute-start(f32[8,128]{1,0:T(8,128)S(1)} %add_add_fusion.1), channel_id=1, source_target_pairs={{0,2},{2,4},{4,6},{6,0},{1,3},{3,5},{5,7},{7,1},{8,10},{10,12},{12... | collective-permute-start | bytes 12296 | tf_op jit(solution)/shard_map/ppermute | solution.py:63
  12.3 4.3 %collective-permute-start.4 = (f32[8,128]{1,0:T(8,128)S(1)}, f32[8,128]{1,0:T(8,128)S(1)}, u32[]{:S(2)}, u32[]{:S(2)}) collective-permute-start(f32[8,128]{1,0:T(8,128)S(1)} %add_add_fusion.1), channel_id=1, source_target_pairs={{0,4},{2,6},{4,0},{6,2},{1,5},{3,7},{5,1},{7,3},{8,12},{10,14},{12... | collective-permute-start | bytes 12296 | tf_op jit(solution)/shard_map/ppermute | solution.py:63
  15.6 2.5 %collective-permute-start.5 = (f32[8,128]{1,0:T(8,128)S(1)}, f32[8,128]{1,0:T(8,128)S(1)}, u32[]{:S(2)}, u32[]{:S(2)}) collective-permute-start(f32[8,128]{1,0:T(8,128)S(1)} %add_add_fusion.1), channel_id=1, source_target_pairs={{0,6},{2,0},{4,2},{6,4},{1,7},{3,1},{5,3},{7,5},{8,14},{10,8},{12,... | collective-permute-start | bytes 12296 | tf_op jit(solution)/shard_map/ppermute | solution.py:63
  18.1 2.5 %collective-permute-start.6 = (f32[8,128]{1,0:T(8,128)S(1)}, f32[8,128]{1,0:T(8,128)S(1)}, u32[]{:S(2)}, u32[]{:S(2)}) collective-permute-start(f32[8,128]{1,0:T(8,128)S(1)} %add_add_fusion), channel_id=1, source_target_pairs={{0,16},{16,0},{1,17},{17,1},{2,18},{18,2},{3,19},{19,3},{4,20},{20... | collective-permute-start | bytes 12296 | tf_op jit(solution)/shard_map/ppermute | solution.py:66
  20.5 4.0 %collective-permute-start.7 = (f32[8,128]{1,0:T(8,128)S(1)}, f32[8,128]{1,0:T(8,128)S(1)}, u32[]{:S(2)}, u32[]{:S(2)}) collective-permute-start(f32[8,128]{1,0:T(8,128)S(1)} %add.45), channel_id=1, source_target_pairs={{0,1},{1,0},{2,3},{3,2},{4,5},{5,4},{6,7},{7,6},{8,9},{9,8},{10,11... | collective-permute-start | bytes 12296 | tf_op jit(solution)/shard_map/ppermute | solution.py:66
  24.5 6.9 %collective-permute-start.8 = (f32[8,128]{1,0:T(8,128)S(1)}, f32[8,128]{1,0:T(8,128)S(1)}, u32[]{:S(2)}, u32[]{:S(2)}) collective-permute-start(f32[8,128]{1,0:T(8,128)S(1)} %add.46), channel_id=1, source_target_pairs={{0,8},{8,0},{1,9},{9,1},{2,10},{10,2},{3,11},{11,3},{4,12},{12,4},... | collective-permute-start | bytes 12296 | tf_op jit(solution)/shard_map/ppermute | solution.py:66
  36.7 8.1 %collective-permute-start.10 = (bf16[49,16,128]{2,1,0:T(8,128)(2,1)}, bf16[49,16,128]{2,1,0:T(8,128)(2,1)S(1)}, u32[]{:S(2)}, u32[]{:S(2)}) collective-permute-start(bf16[49,16,128]{2,1,0:T(8,128)(2,1)} %get-tuple-element.78), channel_id=1, source_target_pairs={{0,4},{2,6},{4,0},{6,2},{1,5},{3,7},{5,1},{7,3},{8,12},{10,14},{12... | collective-permute-start | bytes 602120 | tf_op jit(solution)/shard_map/ppermute | solution.py:400
  38.1 10.5 %collective-permute-start.11 = (bf16[49,16,128]{2,1,0:T(8,128)(2,1)}, bf16[49,16,128]{2,1,0:T(8,128)(2,1)S(1)}, u32[]{:S(2)}, u32[]{:S(2)}) collective-permute-start(bf16[49,16,128]{2,1,0:T(8,128)(2,1)} %get-tuple-element.79), channel_id=1, source_target_pairs={{0,6},{2,0},{4,2},{6,4},{1,7},{3,1},{5,3},{7,5},{8,14},{10,8},{12,... | collective-permute-start | bytes 602120 | tf_op jit(solution)/shard_map/ppermute | solution.py:400
  38.8 10.9 %collective-permute-start.9 = (bf16[49,16,128]{2,1,0:T(8,128)(2,1)}, bf16[49,16,128]{2,1,0:T(8,128)(2,1)S(1)}, u32[]{:S(2)}, u32[]{:S(2)}) collective-permute-start(bf16[49,16,128]{2,1,0:T(8,128)(2,1)} %get-tuple-element.77), channel_id=1, source_target_pairs={{0,2},{2,4},{4,6},{6,0},{1,3},{3,5},{5,7},{7,1},{8,10},{10,12},{12... | collective-permute-start | bytes 602120 | tf_op jit(solution)/shard_map/ppermute | solution.py:400
  39.6 3.7 %collective-permute-start.12 = (bf16[17,16,128]{2,1,0:T(8,128)(2,1)}, bf16[17,16,128]{2,1,0:T(8,128)(2,1)S(1)}, u32[]{:S(2)}, u32[]{:S(2)}) collective-permute-start(bf16[17,16,128]{2,1,0:T(8,128)(2,1)} %get-tuple-element.88.refs_0_), channel_id=1, source_target_pairs={{0,16},{16,0},{1,17},{17,1},{2,18},{18,2},{3,19},{19,3},{4,20},{20... | collective-permute-start | bytes 208904 | tf_op jit(solution)/shard_map/ppermute | solution.py:374
  49.7 0.9 copy-start.1
  50.8 17.4 %collective-permute-start.13 = (bf16[193,16,128]{2,1,0:T(8,128)(2,1)S(1)}, bf16[193,16,128]{2,1,0:T(8,128)(2,1)S(1)}, u32[]{:S(2)}, u32[]{:S(2)}) collective-permute-start(bf16[193,16,128]{2,1,0:T(8,128)(2,1)S(1)} %get-tuple-element.85.refs_0_), channel_id=1, source_target_pairs={{0,32},{8,104},{32,64},{40,8},{64,96},{72,40},{96,0},{104,72},{1,3... | collective-permute-start | bytes 2371592 | tf_op jit(solution)/shard_map/ppermute | solution.py:380
  53.2 15.0 %collective-permute-start.14 = (bf16[129,16,128]{2,1,0:T(8,128)(2,1)S(1)}, bf16[129,16,128]{2,1,0:T(8,128)(2,1)S(1)}, u32[]{:S(2)}, u32[]{:S(2)}) collective-permute-start(bf16[129,16,128]{2,1,0:T(8,128)(2,1)S(1)} %get-tuple-element.86), channel_id=1, source_target_pairs={{0,16},{16,0},{1,17},{17,1},{2,18},{18,2},{3,19},{19,3},{4,20},{20... | collective-permute-start | bytes 1585160 | tf_op jit(solution)/shard_map/ppermute | solution.py:374
  55.4 12.8 %collective-permute-start.15 = (bf16[2,17,16,128]{3,2,1,0:T(8,128)(2,1)S(1)}, bf16[2,17,16,128]{3,2,1,0:T(8,128)(2,1)S(1)}, u32[]{:S(2)}, u32[]{:S(2)}) collective-permute-start(bf16[2,17,16,128]{3,2,1,0:T(8,128)(2,1)S(1)} %pad_maximum_fusion), channel_id=1, source_target_pairs={{0,32},{8,104},{32,64},{40,8},{64,96},{72,40},{96,0},{104,72},{1,3... | collective-permute-start | bytes 417800 | tf_op jit(solution)/shard_map/ppermute | solution.py:380
  55.6 12.6 %collective-permute-start.16 = (bf16[2,17,16,128]{3,2,1,0:T(8,128)(2,1)S(1)}, bf16[2,17,16,128]{3,2,1,0:T(8,128)(2,1)S(1)}, u32[]{:S(2)}, u32[]{:S(2)}) collective-permute-start(bf16[2,17,16,128]{3,2,1,0:T(8,128)(2,1)S(1)} %pad_maximum_fusion), channel_id=1, source_target_pairs={{0,64},{8,72},{32,96},{40,104},{64,0},{72,8},{96,32},{104,40},{1,6... | collective-permute-start | bytes 417800 | tf_op jit(solution)/shard_map/ppermute | solution.py:380
  56.4 11.8 %collective-permute-start.17 = (bf16[2,17,16,128]{3,2,1,0:T(8,128)(2,1)S(1)}, bf16[2,17,16,128]{3,2,1,0:T(8,128)(2,1)S(1)}, u32[]{:S(2)}, u32[]{:S(2)}) collective-permute-start(bf16[2,17,16,128]{3,2,1,0:T(8,128)(2,1)S(1)} %pad_maximum_fusion), channel_id=1, source_target_pairs={{0,96},{8,40},{32,0},{40,72},{64,32},{72,104},{96,64},{104,8},{1,9... | collective-permute-start | bytes 417800 | tf_op jit(solution)/shard_map/ppermute | solution.py:380
  68.2 19.0 %collective-permute-start.18 = (bf16[193,16,128]{2,1,0:T(8,128)(2,1)S(1)}, bf16[193,16,128]{2,1,0:T(8,128)(2,1)S(1)}, u32[]{:S(2)}, u32[]{:S(2)}) collective-permute-start(bf16[193,16,128]{2,1,0:T(8,128)(2,1)S(1)} %collective-permute-done.13.refs_1_), channel_id=1, source_target_pairs={{0,32},{8,104},{32,64},{40,8},{64,96},{72,40},{96,0},{104,72},{1,3... | collective-permute-start | bytes 2371592 | tf_op jit(solution)/shard_map/ppermute | solution.py:380
  71.4 0.9 copy-start
  72.3 14.8 %collective-permute-start.22 = (bf16[129,16,128]{2,1,0:T(8,128)(2,1)S(1)}, bf16[129,16,128]{2,1,0:T(8,128)(2,1)S(1)}, u32[]{:S(2)}, u32[]{:S(2)}) collective-permute-start(bf16[129,16,128]{2,1,0:T(8,128)(2,1)S(1)} %join_kv.1.refs_4_), channel_id=1, source_target_pairs={{0,2},{2,4},{4,6},{6,0},{8,14},{10,8},{12,10},{14,12},{1,3},{3,5},... | collective-permute-start | bytes 1585160 | tf_op jit(solution)/shard_map/ppermute | solution.py:385
  73.9 13.2 %collective-permute-start.19 = (bf16[129,16,128]{2,1,0:T(8,128)(2,1)S(1)}, bf16[129,16,128]{2,1,0:T(8,128)(2,1)S(1)}, u32[]{:S(2)}, u32[]{:S(2)}) collective-permute-start(bf16[129,16,128]{2,1,0:T(8,128)(2,1)S(1)} %collective-permute-done.14.refs_2_), channel_id=1, source_target_pairs={{0,32},{8,104},{32,64},{40,8},{64,96},{72,40},{96,0},{104,72},{1,3... | collective-permute-start | bytes 1585160 | tf_op jit(solution)/shard_map/ppermute | solution.py:380
  74.0 8.4 %collective-permute-start.21 = (bf16[64,16,128]{2,1,0:T(8,128)(2,1)S(1)}, bf16[64,16,128]{2,1,0:T(8,128)(2,1)S(1)}, u32[]{:S(2)}, u32[]{:S(2)}) collective-permute-start(bf16[64,16,128]{2,1,0:T(8,128)(2,1)S(1)} %slice.15), channel_id=1, source_target_pairs={{0,16},{16,0},{1,17},{17,1},{2,18},{18,2},{3,19},{19,3},{4,20},{20... | collective-permute-start | bytes 786440 | tf_op jit(solution)/shard_map/ppermute | solution.py:374
  75.3 11.8 %collective-permute-start.20 = (bf16[64,16,128]{2,1,0:T(8,128)(2,1)S(1)}, bf16[64,16,128]{2,1,0:T(8,128)(2,1)S(1)}, u32[]{:S(2)}, u32[]{:S(2)}) collective-permute-start(bf16[64,16,128]{2,1,0:T(8,128)(2,1)S(1)} %get-tuple-element.92), channel_id=1, source_target_pairs={{0,16},{16,0},{1,17},{17,1},{2,18},{18,2},{3,19},{19,3},{4,20},{20... | collective-permute-start | bytes 786440 | tf_op jit(solution)/shard_map/ppermute | solution.py:374
  87.2 20.1 %collective-permute-start.27 = (bf16[515,16,128]{2,1,0:T(8,128)(2,1)S(1)}, bf16[515,16,128]{2,1,0:T(8,128)(2,1)S(1)}, u32[]{:S(2)}, u32[]{:S(2)}) collective-permute-start(bf16[515,16,128]{2,1,0:T(8,128)(2,1)S(1)} %get-tuple-element.103), channel_id=1, source_target_pairs={{0,8},{8,0},{1,9},{9,1},{2,10},{10,2},{3,11},{11,3},{4,12},{12,4},... | collective-permute-start | bytes 6328328 | tf_op jit(solution)/shard_map/ppermute | solution.py:370
  90.4 16.8 %collective-permute-start.23 = (bf16[193,16,128]{2,1,0:T(8,128)(2,1)S(1)}, bf16[193,16,128]{2,1,0:T(8,128)(2,1)S(1)}, u32[]{:S(2)}, u32[]{:S(2)}) collective-permute-start(bf16[193,16,128]{2,1,0:T(8,128)(2,1)S(1)} %collective-permute-done.18.refs_0_), channel_id=1, source_target_pairs={{0,32},{8,104},{32,64},{40,8},{64,96},{72,40},{96,0},{104,72},{1,3... | collective-permute-start | bytes 2371592 | tf_op jit(solution)/shard_map/ppermute | solution.py:380
  90.4 16.8 %collective-permute-start.24 = (bf16[129,16,128]{2,1,0:T(8,128)(2,1)S(1)}, bf16[129,16,128]{2,1,0:T(8,128)(2,1)S(1)}, u32[]{:S(2)}, u32[]{:S(2)}) collective-permute-start(bf16[129,16,128]{2,1,0:T(8,128)(2,1)S(1)} %collective-permute-done.19.refs_1_), channel_id=1, source_target_pairs={{0,32},{8,104},{32,64},{40,8},{64,96},{72,40},{96,0},{104,72},{1,3... | collective-permute-start | bytes 1585160 | tf_op jit(solution)/shard_map/ppermute | solution.py:380
  90.4 16.8 %collective-permute-start.26 = (bf16[129,16,128]{2,1,0:T(8,128)(2,1)S(1)}, bf16[129,16,128]{2,1,0:T(8,128)(2,1)S(1)}, u32[]{:S(2)}, u32[]{:S(2)}) collective-permute-start(bf16[129,16,128]{2,1,0:T(8,128)(2,1)S(1)} %collective-permute-done.22.refs_5_), channel_id=1, source_target_pairs={{0,2},{2,4},{4,6},{6,0},{8,14},{10,8},{12,10},{14,12},{1,3},{3,5},... | collective-permute-start | bytes 1585160 | tf_op jit(solution)/shard_map/ppermute | solution.py:385
  92.2 7.4 %collective-permute-start.25 = (bf16[64,16,128]{2,1,0:T(8,128)(2,1)S(1)}, bf16[64,16,128]{2,1,0:T(8,128)(2,1)S(1)}, u32[]{:S(2)}, u32[]{:S(2)}) collective-permute-start(bf16[64,16,128]{2,1,0:T(8,128)(2,1)S(1)} %slice.16), channel_id=1, source_target_pairs={{0,16},{16,0},{1,17},{17,1},{2,18},{18,2},{3,19},{19,3},{4,20},{20... | collective-permute-start | bytes 786440 | tf_op jit(solution)/shard_map/ppermute | solution.py:374
  107.3 11.7 %collective-permute-start.31 = (bf16[708,16,128]{2,1,0:T(8,128)(2,1)S(1)}, bf16[708,16,128]{2,1,0:T(8,128)(2,1)S(1)}, u32[]{:S(2)}, u32[]{:S(2)}) collective-permute-start(bf16[708,16,128]{2,1,0:T(8,128)(2,1)S(1)} %get-tuple-element.116), channel_id=1, source_target_pairs={{0,8},{8,0},{1,9},{9,1},{2,10},{10,2},{3,11},{11,3},{4,12},{12,4},... | collective-permute-start | bytes 8699912 | tf_op jit(solution)/shard_map/ppermute | solution.py:370
  109.4 9.5 %collective-permute-start.32 = (bf16[193,16,128]{2,1,0:T(8,128)(2,1)S(1)}, bf16[193,16,128]{2,1,0:T(8,128)(2,1)S(1)}, u32[]{:S(2)}, u32[]{:S(2)}) collective-permute-start(bf16[193,16,128]{2,1,0:T(8,128)(2,1)S(1)} %collective-permute-done.23.refs_0_), channel_id=1, source_target_pairs={{0,8},{8,0},{1,9},{9,1},{2,10},{10,2},{3,11},{11,3},{4,12},{12,4},... | collective-permute-start | bytes 2371592 | tf_op jit(solution)/shard_map/ppermute | solution.py:370
  109.7 9.2 %collective-permute-start.28 = (bf16[129,16,128]{2,1,0:T(8,128)(2,1)S(1)}, bf16[129,16,128]{2,1,0:T(8,128)(2,1)S(1)}, u32[]{:S(2)}, u32[]{:S(2)}) collective-permute-start(bf16[129,16,128]{2,1,0:T(8,128)(2,1)S(1)} %collective-permute-done.24.refs_0_), channel_id=1, source_target_pairs={{0,32},{8,104},{32,64},{40,8},{64,96},{72,40},{96,0},{104,72},{1,3... | collective-permute-start | bytes 1585160 | tf_op jit(solution)/shard_map/ppermute | solution.py:380
  109.7 9.2 %collective-permute-start.30 = (bf16[129,16,128]{2,1,0:T(8,128)(2,1)S(1)}, bf16[129,16,128]{2,1,0:T(8,128)(2,1)S(1)}, u32[]{:S(2)}, u32[]{:S(2)}) collective-permute-start(bf16[129,16,128]{2,1,0:T(8,128)(2,1)S(1)} %collective-permute-done.26.refs_2_), channel_id=1, source_target_pairs={{0,2},{2,4},{4,6},{6,0},{8,14},{10,8},{12,10},{14,12},{1,3},{3,5},... | collective-permute-start | bytes 1585160 | tf_op jit(solution)/shard_map/ppermute | solution.py:385
  111.5 7.5 %collective-permute-start.29 = (bf16[64,16,128]{2,1,0:T(8,128)(2,1)S(1)}, bf16[64,16,128]{2,1,0:T(8,128)(2,1)S(1)}, u32[]{:S(2)}, u32[]{:S(2)}) collective-permute-start(bf16[64,16,128]{2,1,0:T(8,128)(2,1)S(1)} %slice.17), channel_id=1, source_target_pairs={{0,16},{16,0},{1,17},{17,1},{2,18},{18,2},{3,19},{19,3},{4,20},{20... | collective-permute-start | bytes 786440 | tf_op jit(solution)/shard_map/ppermute | solution.py:374
  119.0 6.1 %collective-permute-start.36 = (bf16[322,16,128]{2,1,0:T(8,128)(2,1)S(1)}, bf16[322,16,128]{2,1,0:T(8,128)(2,1)S(1)}, u32[]{:S(2)}, u32[]{:S(2)}) collective-permute-start(bf16[322,16,128]{2,1,0:T(8,128)(2,1)S(1)} %get-tuple-element.129), channel_id=1, source_target_pairs={{0,8},{8,0},{1,9},{9,1},{2,10},{10,2},{3,11},{11,3},{4,12},{12,4},... | collective-permute-start | bytes 3956744 | tf_op jit(solution)/shard_map/ppermute | solution.py:370
  120.5 4.6 %collective-permute-start.33 = (bf16[129,16,128]{2,1,0:T(8,128)(2,1)S(1)}, bf16[129,16,128]{2,1,0:T(8,128)(2,1)S(1)}, u32[]{:S(2)}, u32[]{:S(2)}) collective-permute-start(bf16[129,16,128]{2,1,0:T(8,128)(2,1)S(1)} %collective-permute-done.28.refs_1_), channel_id=1, source_target_pairs={{0,8},{8,0},{1,9},{9,1},{2,10},{10,2},{3,11},{11,3},{4,12},{12,4},... | collective-permute-start | bytes 1585160 | tf_op jit(solution)/shard_map/ppermute | solution.py:370
  120.5 4.5 %collective-permute-start.35 = (bf16[129,16,128]{2,1,0:T(8,128)(2,1)S(1)}, bf16[129,16,128]{2,1,0:T(8,128)(2,1)S(1)}, u32[]{:S(2)}, u32[]{:S(2)}) collective-permute-start(bf16[129,16,128]{2,1,0:T(8,128)(2,1)S(1)} %collective-permute-done.30.refs_3_), channel_id=1, source_target_pairs={{0,8},{8,0},{1,9},{9,1},{2,10},{10,2},{3,11},{11,3},{4,12},{12,4},... | collective-permute-start | bytes 1585160 | tf_op jit(solution)/shard_map/ppermute | solution.py:370
  121.0 4.0 %collective-permute-start.34 = (bf16[64,16,128]{2,1,0:T(8,128)(2,1)S(1)}, bf16[64,16,128]{2,1,0:T(8,128)(2,1)S(1)}, u32[]{:S(2)}, u32[]{:S(2)}) collective-permute-start(bf16[64,16,128]{2,1,0:T(8,128)(2,1)S(1)} %collective-permute-done.29.refs_2_), channel_id=1, source_target_pairs={{0,8},{8,0},{1,9},{9,1},{2,10},{10,2},{3,11},{11,3},{4,12},{12,4},... | collective-permute-start | bytes 786440 | tf_op jit(solution)/shard_map/ppermute | solution.py:370

commit v4 on v3

--- a/solution.py
+++ b/solution.py
@@ -62,8 +62,9 @@
     for axis in ("x", "z"):
         others = [lax.ppermute(v, axis, ring(4, k)) for k in (1, 2, 3)]
         v = v + others[0] + others[1] + others[2]
-    for axis in ("yl", "yh", "c"):
-        v = v + lax.ppermute(v, axis, ring(2, 1))
+    for pairs in ([(0, 2), (2, 0), (1, 3), (3, 1)], [(2, 1), (1, 2), (3, 0), (0, 3)]):
+        v = v + lax.ppermute(v, ("yl", "yh"), pairs)
+    v = v + lax.ppermute(v, "c", ring(2, 1))
     return v
 
 
@@ -185,7 +186,7 @@
 
 def join(place, parts):
     def kernel(place_ref, *refs):
-        out, out_a, out_b = refs[4:]
+        out = refs[4]
         shard = lax.rem(place_ref[0], 4)
         tile = jnp.zeros((TILE, LANES), jnp.float32)
         for k in range(4):
@@ -195,16 +196,12 @@
                 got = refs[k][1 + h * SLOT_T : 1 + (h + 1) * SLOT_T]
                 out[pl.ds(1 + 4 * h * SLOT_T + z * SLOT_T, SLOT_T)] = got
         out[0] = tile.astype(jnp.bfloat16)
-        out_a[...] = out[0:A_T]
-        out_b[...] = out[A_T:FULL_T]
 
     return pl.pallas_call(
         kernel,
-        out_shape=tuple(
-            jax.ShapeDtypeStruct((n, TILE, LANES), jnp.bfloat16) for n in (FULL_T, A_T, FULL_T - A_T)
-        ),
+        out_shape=jax.ShapeDtypeStruct((FULL_T, TILE, LANES), jnp.bfloat16),
         in_specs=[pl.BlockSpec(memory_space=SMEM)] + [pl.BlockSpec(memory_space=VMEM)] * 4,
-        out_specs=[pl.BlockSpec(memory_space=VMEM)] * 3,
+        out_specs=pl.BlockSpec(memory_space=VMEM),
         compiler_params=pltpu.CompilerParams(vmem_limit_bytes=16 * 1024 * 1024),
         name="join",
     )(place, *parts)
@@ -380,8 +377,9 @@
     return lax.ppermute(v, ("x", "c"), pairs)
 
 
-def along_z(v):
-    pairs = [(4 * c + z, 4 * c + (z + (3 if c else 1)) % 4) for c in range(2) for z in range(4)]
+def along_z(v, k=1):
+    step = (k, 4 - k)
+    pairs = [(4 * c + z, 4 * c + (z + step[c]) % 4) for c in range(2) for z in range(4)]
     return lax.ppermute(v, ("c", "z"), pairs)
 
 
@@ -399,41 +397,34 @@
     )
     parts = [parts[0]] + [lax.ppermute(parts[k], "z", ring(4, k)) for k in (1, 2, 3)]
     kv_across = swap_y(kv_part)
-    *parts, kv_part, kv_across = after(*parts, kv_part, kv_across)
-
-    p0, a_own, b_own = join(place, parts)
-    p1, qa = along_x(p0), swap_y(a_own)
     kv_two = jnp.stack([kv_part, kv_across])
-    k1, k2, k3 = (along_x(kv_two, k) for k in (1, 2, 3))
-    p1, qa, b_own, k1, k2, k3 = after(p1, qa, b_own, k1, k2, k3)
+    kv_far = [along_x(kv_two, k) for k in (1, 2, 3)]
+    *parts, kv_part, kv_across, k1, k2, k3 = after(*parts, kv_part, kv_across, *kv_far)
 
     w0 = join_kv(place, (kv_part, kv_across, k1, k2, k3))
-    p2, a1, qb, b1, w1 = along_x(p1), along_x(qa), swap_y(b_own), swap_y(p1[A_T:FULL_T]), along_z(w0)
-    held1 = [("P", 0, False), ("P", 1, False), ("A", 0, True)]
-    *outs, pack1 = lay(place, list(zip([p0, p1, qa], held1)), [], pack=True)
-    p2, a1, qb, b1, w1, pack1, *outs = after(p2, a1, qb, b1, w1, pack1, *outs)
-
-    p3, a2, b2, w2 = along_x(p2), along_x(a1), swap_y(p2[A_T:FULL_T]), along_z(w1)
+    p0 = join(place, parts)
+    q0, p1, p3, w1, w3 = swap_y(p0), along_x(p0), along_x(p0, 3), along_z(w0), along_z(w0, 3)
+    q0, p1, p3, w1, w3 = after(q0, p1, p3, w1, w3)
+
+    b1, b3, p2 = swap_y(p1[A_T:FULL_T]), swap_y(p3[A_T:FULL_T]), along_x(p1)
+    qa = q0[0:A_T]
+    a1, a3 = along_x(qa), along_x(qa, 3)
+    held1 = [("P", 0, False), ("P", 1, False), ("P", 3, False), ("P", 0, True)]
+    held1 += [("K", 0, False), ("K", 1, False), ("K", 3, False)]
+    *outs, pack1 = lay(place, list(zip([p0, p1, p3, q0, w0, w1, w3], held1)), [], pack=True)
+    a1, a3, b1, b3, p2, pack1, *outs = after(a1, a3, b1, b3, p2, pack1, *outs)
+
+    b2, a2, w2 = swap_y(p2[A_T:FULL_T]), along_x(a1), along_z(w1)
     got1 = swap_core(pack1)
-    held2 = [("P", 2, False), ("A", 1, True), ("B", 0, True), ("B", 1, True)]
-    held2 += [("K", 0, False), ("K", 1, False)]
-    own = [p2, a1, qb, b1, w0, w1]
-    *outs, pack2 = lay(place, list(zip(own, held2)), [], outs, pack=True)
-    p3, a2, b2, w2, got1, pack2, *outs = after(p3, a2, b2, w2, got1, pack2, *outs)
-
-    a3, b3, w3 = along_x(a2), swap_y(p3[A_T:FULL_T]), along_z(w2)
-    got2, got3 = swap_core(pack2), swap_core(p3)
+    held2 = [("A", 1, True), ("A", 3, True), ("B", 1, True), ("B", 3, True), ("P", 2, False)]
+    *outs, pack2 = lay(place, list(zip([a1, a3, b1, b3, p2], held2)), [], outs, pack=True)
+    a2, b2, w2, got1, pack2, *outs = after(a2, b2, w2, got1, pack2, *outs)
+
     held3 = [("A", 2, True), ("B", 2, True), ("K", 2, False)]
-    own = list(zip([a2, b2, w2], held3))
-    *outs, pack3 = lay(place, own, [(got1, held1)], outs, pack=True)
-    a3, b3, w3, got2, got3, pack3, *outs = after(a3, b3, w3, got2, got3, pack3, *outs)
-
-    held4 = [("A", 3, True), ("B", 3, True), ("K", 3, False)]
-    got4 = [(swap_core(v), [p]) for v, p in zip((a3, b3, w3), held4)]
-    got4.append((swap_core(pack3), held3))
-    own = list(zip([p3, a3, b3, w3], [("P", 3, False)] + held4))
-    outs = lay(place, own, [(got2, held2), (got3, [("P", 3, False)])], outs)
-    exp_rollout, kv_rollout, exp_scales, kv_scales = lay(place, [], got4, outs, last=True)
+    own = [a2, b2, w2]
+    got = [(swap_core(pack2), held2)] + [(swap_core(v), [p]) for v, p in zip(own, held3)]
+    outs = lay(place, list(zip(own, held3)), [(got1, held1)], outs)
+    exp_rollout, kv_rollout, exp_scales, kv_scales = lay(place, [], got, outs, last=True)
     return (
         kv_new,
         exp_new,

time: 128 us -> 121 us (0.945)
  starting transfers between devices: 51.4 us -> 41.8 us
  waiting for transfers between devices: 53.7 us -> 57.5 us
    ppermute x3, waiting for transfers between devices: 0.01 us -> 16.8 us  [along_z(): return lax.ppermute(v, ('c', 'z'), pairs)]
    ppermute x6 -> x5, waiting for transfers between devices: 20.5 us -> 10.7 us  [swap_y(): return lax.ppermute(v, 'yl', ring(2, 1))]
    ppermute x6 -> x5, starting transfers between devices: 6.87 us -> 2.41 us  [swap_y(): return lax.ppermute(v, 'yl', ring(2, 1))]
    ppermute x7 -> x5, starting transfers between devices: 7.78 us -> 5.13 us  [swap_core(): return lax.ppermute(v, 'c', ring(2, 1))]
    ppermute x3, starting transfers between devices: 5.1 us -> 2.55 us  [along_z(): return lax.ppermute(v, ('c', 'z'), pairs)]
    ppermute x9, waiting for transfers between devices: 18.9 us -> 16.5 us  [along_x(): return lax.ppermute(v, ('x', 'c'), pairs)]
    ppermute x3, waiting for transfers between devices: 6.48 us -> 4.24 us  [per_device(): lax.ppermute(parts[k], 'z', ring(4, k))]
    ppermute x7 -> x5, waiting for transfers between devices: 1.19 us -> 2.69 us  [swap_core(): return lax.ppermute(v, 'c', ring(2, 1))]
  transfers between devices with their start and end apart: 37 -> 34, of which waited for: 18 -> 22; matrix products, arithmetic and copies ran while one was open for 1% -> 1% of each run, Pallas kernels for 7% -> 6%
where the time goes in v4:
time: 121 us
  waiting for transfers between devices  57.5 us (48%)
  starting transfers between devices  41.8 us (35%)
  Pallas kernels  16.7 us (14%)
  other arithmetic  2.19 us (2%)
  local copies, waits for them, and re-layouts  1.9 us (2%)
    ppermute x3, waiting for transfers between devices, along_z(): return lax.ppermute(v, ('c', 'z'), pairs)  16.8 us
    ppermute x9, waiting for transfers between devices, along_x(): return lax.ppermute(v, ('x', 'c'), pairs)  16.5 us
    ppermute x6, starting transfers between devices, sum_over_devices(): others = [lax.ppermute(v, axis, ring(4, k)) for k in (1, 2, 3)]  11.3 us
    ppermute x5, waiting for transfers between devices, swap_y(): return lax.ppermute(v, 'yl', ring(2, 1))  10.7 us
    pallas_call x4, Pallas kernels, lay(): pl.pallas_call(kernel, out_shape=tuple(out_shape), in_specs=[pl.BlockSpec...  10 us
    ppermute x9, starting transfers between devices, along_x(): return lax.ppermute(v, ('x', 'c'), pairs)  7.44 us
    ppermute x1, starting transfers between devices, sum_over_devices(): v = v + lax.ppermute(v, 'c', ring(2, 1))  6.04 us
    ppermute x5, starting transfers between devices, swap_core(): return lax.ppermute(v, 'c', ring(2, 1))  5.13 us
  transfers between devices with their start and end apart: 34, of which 22 were waited for; matrix products, arithmetic and copies ran while one was open for 1% of the time, Pallas kernels for 6%

profile of v4, /device:TPU:1, one launch (start us, length us, event | category | flops | bytes accessed | tf_op | source)
XLA Modules:
  0.0 120.8 jit_solution(8246139309113529130)
XLA Ops:
  0.6 1.9 %sum_of_squares.1 = f32[8,128]{1,0:T(8,128)} custom-call(f32[2,1,128,128]{3,2,1,0:T(8,128)} %refs_1_.1, f32[4,1,3,128,128]{4,3,2,1,0:T(8,128)} %refs_5_.1), custom_call_target="tpu_custom_call" | custom-call | tf_op jit(solution)/shard_map/sum_of_squares/pallas_call | solution.py:52
  2.5 2.0 %collective-permute-start = (f32[8,128]{1,0:T(8,128)}, f32[8,128]{1,0:T(8,128)S(1)}, u32[]{:S(2)}, u32[]{:S(2)}) collective-permute-start(f32[8,128]{1,0:T(8,128)} %sum_of_squares.1), channel_id=1, source_target_pairs={{0,32},{32,64},{64,96},{96,0},{1,33},{33,65},{65,97},{97,1},{2,34}... | collective-permute-start | bytes 12296 | tf_op jit(solution)/shard_map/ppermute | solution.py:63
  4.5 2.5 %collective-permute-start.1 = (f32[8,128]{1,0:T(8,128)}, f32[8,128]{1,0:T(8,128)S(1)}, u32[]{:S(2)}, u32[]{:S(2)}) collective-permute-start(f32[8,128]{1,0:T(8,128)} %sum_of_squares.1), channel_id=1, source_target_pairs={{0,64},{32,96},{64,0},{96,32},{1,65},{33,97},{65,1},{97,33},{2,66}... | collective-permute-start | bytes 12296 | tf_op jit(solution)/shard_map/ppermute | solution.py:63
  7.0 1.2 collective-permute-start.2
  8.2 0.6 collective-permute-done.1
  8.7 1.2 %collective-permute-done.2 = f32[8,128]{1,0:T(8,128)S(1)} collective-permute-done((f32[8,128]{1,0:T(8,128)}, f32[8,128]{1,0:T(8,128)S(1)}, u32[]{:S(2)}, u32[]{:S(2)}) %collective-permute-start.2) | collective-permute-done | bytes 4128 | tf_op jit(solution)/shard_map/ppermute | solution.py:63
  10.0 0.7 add_add_fusion.1
  10.7 1.6 %collective-permute-start.3 = (f32[8,128]{1,0:T(8,128)S(1)}, f32[8,128]{1,0:T(8,128)S(1)}, u32[]{:S(2)}, u32[]{:S(2)}) collective-permute-start(f32[8,128]{1,0:T(8,128)S(1)} %add_add_fusion.1), channel_id=1, source_target_pairs={{0,2},{2,4},{4,6},{6,0},{1,3},{3,5},{5,7},{7,1},{8,10},{10,12},{12... | collective-permute-start | bytes 12296 | tf_op jit(solution)/shard_map/ppermute | solution.py:63
  12.3 3.3 %collective-permute-start.4 = (f32[8,128]{1,0:T(8,128)S(1)}, f32[8,128]{1,0:T(8,128)S(1)}, u32[]{:S(2)}, u32[]{:S(2)}) collective-permute-start(f32[8,128]{1,0:T(8,128)S(1)} %add_add_fusion.1), channel_id=1, source_target_pairs={{0,4},{2,6},{4,0},{6,2},{1,5},{3,7},{5,1},{7,3},{8,12},{10,14},{12... | collective-permute-start | bytes 12296 | tf_op jit(solution)/shard_map/ppermute | solution.py:63
  15.6 0.7 collective-permute-start.5
  16.3 0.3 collective-permute-done.4
  16.6 1.4 %collective-permute-done.5 = f32[8,128]{1,0:T(8,128)S(1)} collective-permute-done((f32[8,128]{1,0:T(8,128)S(1)}, f32[8,128]{1,0:T(8,128)S(1)}, u32[]{:S(2)}, u32[]{:S(2)}) %collective-permute-start.5) | collective-permute-done | bytes 4128 | tf_op jit(solution)/shard_map/ppermute | solution.py:63
  18.1 1.3 %collective-permute-start.6 = (f32[8,128]{1,0:T(8,128)S(1)}, f32[8,128]{1,0:T(8,128)S(1)}, u32[]{:S(2)}, u32[]{:S(2)}) collective-permute-start(f32[8,128]{1,0:T(8,128)S(1)} %add_add_fusion), channel_id=1, source_target_pairs={{0,16},{16,0},{1,17},{17,1},{2,18},{18,2},{3,19},{19,3},{4,20},{20... | collective-permute-start | bytes 12296 | tf_op jit(solution)/shard_map/ppermute | solution.py:66
  19.4 1.2 collective-permute-done.6
  20.5 2.7 %collective-permute-start.7 = (f32[8,128]{1,0:T(8,128)S(1)}, f32[8,128]{1,0:T(8,128)S(1)}, u32[]{:S(2)}, u32[]{:S(2)}) collective-permute-start(f32[8,128]{1,0:T(8,128)S(1)} %add.45), channel_id=1, source_target_pairs={{16,1},{1,16},{17,0},{0,17},{18,3},{3,18},{19,2},{2,19},{20,5},{5,... | collective-permute-start | bytes 12296 | tf_op jit(solution)/shard_map/ppermute | solution.py:66
  23.3 1.0 collective-permute-done.7
  24.3 6.0 %collective-permute-start.8 = (f32[8,128]{1,0:T(8,128)S(1)}, f32[8,128]{1,0:T(8,128)S(1)}, u32[]{:S(2)}, u32[]{:S(2)}) collective-permute-start(f32[8,128]{1,0:T(8,128)S(1)} %add.46), channel_id=1, source_target_pairs={{0,8},{8,0},{1,9},{9,1},{2,10},{10,2},{3,11},{11,3},{4,12},{12,4},... | collective-permute-start | bytes 12296 | tf_op jit(solution)/shard_map/ppermute | solution.py:67
  30.3 0.8 collective-permute-done.8
  31.1 0.6 add.47.total_ref
  31.7 4.7 %update.1 = (f32[2,1,128,128]{3,2,1,0:T(8,128)}, f32[4,1,3,128,128]{4,3,2,1,0:T(8,128)}, bf16[49,16,128]{2,1,0:T(8,128)(2,1)}, bf16[49,16,128]{2,1,0:T(8,128)(2,...) custom-call(s32[1]{0:T(128)} %bitcast.place_ref, s32[4]{0:T(128)} %owner_ref.1, ...), custom_call_target="tpu_custom_call" | custom-call | tf_op jit(solution)/shard_map/update/pallas_call | solution.py:163
  36.4 1.4 %collective-permute-start.10 = (bf16[49,16,128]{2,1,0:T(8,128)(2,1)}, bf16[49,16,128]{2,1,0:T(8,128)(2,1)S(1)}, u32[]{:S(2)}, u32[]{:S(2)}) collective-permute-start(bf16[49,16,128]{2,1,0:T(8,128)(2,1)} %get-tuple-element.63), channel_id=1, source_target_pairs={{0,4},{2,6},{4,0},{6,2},{1,5},{3,7},{5,1},{7,3},{8,12},{10,14},{12... | collective-permute-start | bytes 602120 | tf_op jit(solution)/shard_map/ppermute | solution.py:398
  37.8 0.1 collective-permute-start.12
  37.9 0.7 collective-permute-start.11
  38.6 0.7 collective-permute-start.9
  39.4 1.8 %collective-permute-done.12.refs_1_ = bf16[17,16,128]{2,1,0:T(8,128)(2,1)S(1)} collective-permute-done((bf16[17,16,128]{2,1,0:T(8,128)(2,1)}, bf16[17,16,128]{2,1,0:T(8,128)(2,1)S(1)}, u32[]{:S(2)}, u32[]{:S(2)}) %collective-permute-start.12) | collective-permute-done | bytes 69664 | tf_op jit(solution)/shard_map/ppermute | solution.py:371
  41.2 0.9 pad_maximum_fusion
  42.1 2.4 %collective-permute-start.13 = (bf16[2,17,16,128]{3,2,1,0:T(8,128)(2,1)S(1)}, bf16[2,17,16,128]{3,2,1,0:T(8,128)(2,1)S(1)}, u32[]{:S(2)}, u32[]{:S(2)}) collective-permute-start(bf16[2,17,16,128]{3,2,1,0:T(8,128)(2,1)S(1)} %pad_maximum_fusion), channel_id=1, source_target_pairs={{0,32},{8,104},{32,64},{40,8},{64,96},{72,40},{96,0},{104,72},{1,3... | collective-permute-start | bytes 417800 | tf_op jit(solution)/shard_map/ppermute | solution.py:377
  44.5 0.7 collective-permute-start.15
  45.2 3.1 %collective-permute-done.11.refs_3_ = bf16[49,16,128]{2,1,0:T(8,128)(2,1)S(1)} collective-permute-done((bf16[49,16,128]{2,1,0:T(8,128)(2,1)}, bf16[49,16,128]{2,1,0:T(8,128)(2,1)S(1)}, u32[]{:S(2)}, u32[]{:S(2)}) %collective-permute-start.11) | collective-permute-done | bytes 200736 | tf_op jit(solution)/shard_map/ppermute | solution.py:398
  48.3 1.1 collective-permute-done.9.refs_1_
  49.4 1.6 %collective-permute-done.14.refs_3_ = bf16[2,17,16,128]{3,2,1,0:T(8,128)(2,1)S(1)} collective-permute-done((bf16[2,17,16,128]{3,2,1,0:T(8,128)(2,1)S(1)}, bf16[2,17,16,128]{3,2,1,0:T(8,128)(2,1)S(1)}, u32[]{:S(2)}, u32[]{:S(2)}) %collective-permute-start.14) | collective-permute-done | bytes 139296 | tf_op jit(solution)/shard_map/ppermute | solution.py:377
  51.1 2.4 %collective-permute-done.15.refs_4_ = bf16[2,17,16,128]{3,2,1,0:T(8,128)(2,1)S(1)} collective-permute-done((bf16[2,17,16,128]{3,2,1,0:T(8,128)(2,1)S(1)}, bf16[2,17,16,128]{3,2,1,0:T(8,128)(2,1)S(1)}, u32[]{:S(2)}, u32[]{:S(2)}) %collective-permute-start.15) | collective-permute-done | bytes 139296 | tf_op jit(solution)/shard_map/ppermute | solution.py:377
  53.5 0.9 copy-done.1
  54.5 0.2 collective-permute-start.16
  54.6 1.1 collective-permute-start.17
  55.8 0.3 collective-permute-start.18
  56.1 0.9 copy-done
  57.0 1.4 %collective-permute-start.19 = (bf16[129,16,128]{2,1,0:T(8,128)(2,1)S(1)}, bf16[129,16,128]{2,1,0:T(8,128)(2,1)S(1)}, u32[]{:S(2)}, u32[]{:S(2)}) collective-permute-start(bf16[129,16,128]{2,1,0:T(8,128)(2,1)S(1)} %join_kv.1.refs_4_), channel_id=1, source_target_pairs={{0,2},{2,4},{4,6},{6,0},{8,14},{10,8},{12,10},{14,12},{1,3},{3,5},... | collective-permute-start | bytes 1585160 | tf_op jit(solution)/shard_map/ppermute | solution.py:383
  58.4 0.1 collective-permute-start.20
  58.6 6.9 %collective-permute-done.19.refs_5_ = bf16[129,16,128]{2,1,0:T(8,128)(2,1)S(1)} collective-permute-done((bf16[129,16,128]{2,1,0:T(8,128)(2,1)S(1)}, bf16[129,16,128]{2,1,0:T(8,128)(2,1)S(1)}, u32[]{:S(2)}, u32[]{:S(2)}) %collective-permute-start.19) | collective-permute-done | bytes 528416 | tf_op jit(solution)/shard_map/ppermute | solution.py:383
  65.5 5.3 %collective-permute-done.20.refs_6_ = bf16[129,16,128]{2,1,0:T(8,128)(2,1)S(1)} collective-permute-done((bf16[129,16,128]{2,1,0:T(8,128)(2,1)S(1)}, bf16[129,16,128]{2,1,0:T(8,128)(2,1)S(1)}, u32[]{:S(2)}, u32[]{:S(2)}) %collective-permute-start.20) | collective-permute-done | bytes 528416 | tf_op jit(solution)/shard_map/ppermute | solution.py:383
  70.8 1.3 %collective-permute-done.16.refs_3_ = bf16[193,16,128]{2,1,0:T(8,128)(2,1)S(1)} collective-permute-done((bf16[193,16,128]{2,1,0:T(8,128)(2,1)S(1)}, bf16[193,16,128]{2,1,0:T(8,128)(2,1)S(1)}, u32[]{:S(2)}, u32[]{:S(2)}) %collective-permute-start.16) | collective-permute-done | bytes 790560 | tf_op jit(solution)/shard_map/ppermute | solution.py:371
  72.0 3.3 %collective-permute-done.18.refs_2_ = bf16[193,16,128]{2,1,0:T(8,128)(2,1)S(1)} collective-permute-done((bf16[193,16,128]{2,1,0:T(8,128)(2,1)S(1)}, bf16[193,16,128]{2,1,0:T(8,128)(2,1)S(1)}, u32[]{:S(2)}, u32[]{:S(2)}) %collective-permute-start.18) | collective-permute-done | bytes 790560 | tf_op jit(solution)/shard_map/ppermute | solution.py:377
  75.4 0.9 collective-permute-start.25
  76.3 0.1 collective-permute-start.21
  76.4 1.4 %collective-permute-start.22 = (bf16[129,16,128]{2,1,0:T(8,128)(2,1)S(1)}, bf16[129,16,128]{2,1,0:T(8,128)(2,1)S(1)}, u32[]{:S(2)}, u32[]{:S(2)}) collective-permute-start(bf16[129,16,128]{2,1,0:T(8,128)(2,1)S(1)} %slice.18), channel_id=1, source_target_pairs={{0,96},{8,40},{32,0},{40,72},{64,32},{72,104},{96,64},{104,8},{1,9... | collective-permute-start | bytes 1585160 | tf_op jit(solution)/shard_map/ppermute | solution.py:377
  77.9 0.6 collective-permute-start.23
  78.5 1.0 collective-permute-start.24
  79.5 2.8 %lay.4 = (bf16[2,1536,16,128]{3,2,1,0:T(8,128)(2,1)}, bf16[2,8,2,4,8,16,128]{6,5,4,3,2,1,0:T(8,128)(2,1)}, f32[2,16,128]{2,1,0:T(8,128)S(1)}, bf16[1159,16,128]{2,1,0:T(8,128)(2,1)S(1)}) custom-call(s32[1]{0:T(128)} %bitcast.place_ref, bf16[193,16,128]{2,1,0:T(8,128)(2,1)S(1)} %join.1.refs_0_, bf16[193,16,128]{2,1,0:T(8,128)(2,1)S(1)} %collective-permute-done.17.refs_1_, ...), custom_call_target="tpu_custom_call" | custom-call | bytes 11010048 | tf_op jit(solution)/shard_map/lay/pallas_call | solution.py:343
  82.3 1.2 collective-permute-done.23.refs_2_
  83.5 5.3 %collective-permute-done.24.refs_3_ = bf16[64,16,128]{2,1,0:T(8,128)(2,1)S(1)} collective-permute-done((bf16[64,16,128]{2,1,0:T(8,128)(2,1)S(1)}, bf16[64,16,128]{2,1,0:T(8,128)(2,1)S(1)}, u32[]{:S(2)}, u32[]{:S(2)}) %collective-permute-start.24) | collective-permute-done | bytes 262176 | tf_op jit(solution)/shard_map/ppermute | solution.py:371
  88.8 9.1 %collective-permute-done.21.refs_0_ = bf16[129,16,128]{2,1,0:T(8,128)(2,1)S(1)} collective-permute-done((bf16[129,16,128]{2,1,0:T(8,128)(2,1)S(1)}, bf16[129,16,128]{2,1,0:T(8,128)(2,1)S(1)}, u32[]{:S(2)}, u32[]{:S(2)}) %collective-permute-start.21) | collective-permute-done | bytes 528416 | tf_op jit(solution)/shard_map/ppermute | solution.py:377
  97.9 2.7 %collective-permute-start.29 = (bf16[1159,16,128]{2,1,0:T(8,128)(2,1)S(1)}, bf16[1159,16,128]{2,1,0:T(8,128)(2,1)S(1)}, u32[]{:S(2)}, u32[]{:S(2)}) collective-permute-start(bf16[1159,16,128]{2,1,0:T(8,128)(2,1)S(1)} %get-tuple-element.86), channel_id=1, source_target_pairs={{0,8},{8,0},{1,9},{9,1},{2,10},{10,2},{3,11},{11,3},{4,12},{12,4},... | collective-permute-start | bytes 14241800 | tf_op jit(solution)/shard_map/ppermute | solution.py:367
  100.6 1.0 collective-permute-start.28
  101.6 0.4 collective-permute-start.26
  102.1 0.5 collective-permute-start.27
  102.6 1.7 %lay.5 = (bf16[2,1536,16,128]{3,2,1,0:T(8,128)(2,1)}, bf16[2,8,2,4,8,16,128]{6,5,4,3,2,1,0:T(8,128)(2,1)}, f32[2,16,128]{2,1,0:T(8,128)S(1)}, bf16[579,16,128]{2,1,0:T(8,128)(2,1)S(1)}) custom-call(s32[1]{0:T(128)} %bitcast.place_ref, bf16[129,16,128]{2,1,0:T(8,128)(2,1)S(1)} %collective-permute-done.21.refs_0_, ...), custom_call_target="tpu_custom_call", output_to_operand_aliasing={{0}: (6, {}), {1}: (7, {})} | custom-call | bytes 7864320 | tf_op jit(solution)/shard_map/lay/pallas_call | solution.py:343
  104.3 4.6 %collective-permute-done.28.refs_2_ = bf16[129,16,128]{2,1,0:T(8,128)(2,1)S(1)} collective-permute-done((bf16[129,16,128]{2,1,0:T(8,128)(2,1)S(1)}, bf16[129,16,128]{2,1,0:T(8,128)(2,1)S(1)}, u32[]{:S(2)}, u32[]{:S(2)}) %collective-permute-start.28) | collective-permute-done | bytes 528416 | tf_op jit(solution)/shard_map/ppermute | solution.py:383
  109.0 1.2 collective-permute-done.27.refs_1_
  110.1 1.9 %collective-permute-start.30 = (bf16[579,16,128]{2,1,0:T(8,128)(2,1)S(1)}, bf16[579,16,128]{2,1,0:T(8,128)(2,1)S(1)}, u32[]{:S(2)}, u32[]{:S(2)}) collective-permute-start(bf16[579,16,128]{2,1,0:T(8,128)(2,1)S(1)} %get-tuple-element.97), channel_id=1, source_target_pairs={{0,8},{8,0},{1,9},{9,1},{2,10},{10,2},{3,11},{11,3},{4,12},{12,4},... | collective-permute-start | bytes 7114760 | tf_op jit(solution)/shard_map/ppermute | solution.py:367
  112.1 0.5 collective-permute-start.33
  112.6 2.9 %lay.6 = (bf16[2,1536,16,128]{3,2,1,0:T(8,128)(2,1)}, bf16[2,8,2,4,8,16,128]{6,5,4,3,2,1,0:T(8,128)(2,1)}, f32[2,16,128]{2,1,0:T(8,128)S(1)}) custom-call(s32[1]{0:T(128)} %bitcast.place_ref, bf16[129,16,128]{2,1,0:T(8,128)(2,1)S(1)} %collective-permute-done.26.refs_0_, ...), custom_call_target="tpu_custom_call", output_to_operand_aliasing={{0}: (5, {}), {1}: (6, {})} | custom-call | bytes 10485760 | tf_op jit(solution)/shard_map/lay/pallas_call | solution.py:343
  115.4 2.7 %collective-permute-done.32.refs_2_ = bf16[64,16,128]{2,1,0:T(8,128)(2,1)S(1)} collective-permute-done((bf16[64,16,128]{2,1,0:T(8,128)(2,1)S(1)}, bf16[64,16,128]{2,1,0:T(8,128)(2,1)S(1)}, u32[]{:S(2)}, u32[]{:S(2)}) %collective-permute-start.32) | collective-permute-done | bytes 262176 | tf_op jit(solution)/shard_map/ppermute | solution.py:367
  118.1 2.6 %lay.7 = (bf16[2,1536,16,128]{3,2,1,0:T(8,128)(2,1)}, bf16[2,8,2,4,8,16,128]{6,5,4,3,2,1,0:T(8,128)(2,1)}, f32[2,2,128]{2,1,0:T(2,128)}, f32[2,128]{1,0:T(2,128)}) custom-call(s32[1]{0:T(128)} %bitcast.place_ref, bf16[579,16,128]{2,1,0:T(8,128)(2,1)S(1)} %collective-permute-done.30.refs_0_, ...), custom_call_target="tpu_custom_call", output_to_operand_aliasing={{0}: (5, {}), {1}: (6, {})} | custom-call | bytes 8388608 | tf_op jit(solution)/shard_map/lay/pallas_call | solution.py:343
  (26 shorter events, 0.3 us)
Async XLA Ops:
  2.5 5.6 %collective-permute-start = (f32[8,128]{1,0:T(8,128)}, f32[8,128]{1,0:T(8,128)S(1)}, u32[]{:S(2)}, u32[]{:S(2)}) collective-permute-start(f32[8,128]{1,0:T(8,128)} %sum_of_squares.1), channel_id=1, source_target_pairs={{0,32},{32,64},{64,96},{96,0},{1,33},{33,65},{65,97},{97,1},{2,34}... | collective-permute-start | bytes 12296 | tf_op jit(solution)/shard_map/ppermute | solution.py:63
  4.5 4.2 %collective-permute-start.1 = (f32[8,128]{1,0:T(8,128)}, f32[8,128]{1,0:T(8,128)S(1)}, u32[]{:S(2)}, u32[]{:S(2)}) collective-permute-start(f32[8,128]{1,0:T(8,128)} %sum_of_squares.1), channel_id=1, source_target_pairs={{0,64},{32,96},{64,0},{96,32},{1,65},{33,97},{65,1},{97,33},{2,66}... | collective-permute-start | bytes 12296 | tf_op jit(solution)/shard_map/ppermute | solution.py:63
  7.0 3.0 %collective-permute-start.2 = (f32[8,128]{1,0:T(8,128)}, f32[8,128]{1,0:T(8,128)S(1)}, u32[]{:S(2)}, u32[]{:S(2)}) collective-permute-start(f32[8,128]{1,0:T(8,128)} %sum_of_squares.1), channel_id=1, source_target_pairs={{0,96},{32,0},{64,32},{96,64},{1,97},{33,1},{65,33},{97,65},{2,98}... | collective-permute-start | bytes 12296 | tf_op jit(solution)/shard_map/ppermute | solution.py:63
  10.7 5.7 %collective-permute-start.3 = (f32[8,128]{1,0:T(8,128)S(1)}, f32[8,128]{1,0:T(8,128)S(1)}, u32[]{:S(2)}, u32[]{:S(2)}) collective-permute-start(f32[8,128]{1,0:T(8,128)S(1)} %add_add_fusion.1), channel_id=1, source_target_pairs={{0,2},{2,4},{4,6},{6,0},{1,3},{3,5},{5,7},{7,1},{8,10},{10,12},{12... | collective-permute-start | bytes 12296 | tf_op jit(solution)/shard_map/ppermute | solution.py:63
  12.3 4.3 %collective-permute-start.4 = (f32[8,128]{1,0:T(8,128)S(1)}, f32[8,128]{1,0:T(8,128)S(1)}, u32[]{:S(2)}, u32[]{:S(2)}) collective-permute-start(f32[8,128]{1,0:T(8,128)S(1)} %add_add_fusion.1), channel_id=1, source_target_pairs={{0,4},{2,6},{4,0},{6,2},{1,5},{3,7},{5,1},{7,3},{8,12},{10,14},{12... | collective-permute-start | bytes 12296 | tf_op jit(solution)/shard_map/ppermute | solution.py:63
  15.6 2.5 %collective-permute-start.5 = (f32[8,128]{1,0:T(8,128)S(1)}, f32[8,128]{1,0:T(8,128)S(1)}, u32[]{:S(2)}, u32[]{:S(2)}) collective-permute-start(f32[8,128]{1,0:T(8,128)S(1)} %add_add_fusion.1), channel_id=1, source_target_pairs={{0,6},{2,0},{4,2},{6,4},{1,7},{3,1},{5,3},{7,5},{8,14},{10,8},{12,... | collective-permute-start | bytes 12296 | tf_op jit(solution)/shard_map/ppermute | solution.py:63
  18.1 2.5 %collective-permute-start.6 = (f32[8,128]{1,0:T(8,128)S(1)}, f32[8,128]{1,0:T(8,128)S(1)}, u32[]{:S(2)}, u32[]{:S(2)}) collective-permute-start(f32[8,128]{1,0:T(8,128)S(1)} %add_add_fusion), channel_id=1, source_target_pairs={{0,16},{16,0},{1,17},{17,1},{2,18},{18,2},{3,19},{19,3},{4,20},{20... | collective-permute-start | bytes 12296 | tf_op jit(solution)/shard_map/ppermute | solution.py:66
  20.5 3.7 %collective-permute-start.7 = (f32[8,128]{1,0:T(8,128)S(1)}, f32[8,128]{1,0:T(8,128)S(1)}, u32[]{:S(2)}, u32[]{:S(2)}) collective-permute-start(f32[8,128]{1,0:T(8,128)S(1)} %add.45), channel_id=1, source_target_pairs={{16,1},{1,16},{17,0},{0,17},{18,3},{3,18},{19,2},{2,19},{20,5},{5,... | collective-permute-start | bytes 12296 | tf_op jit(solution)/shard_map/ppermute | solution.py:66
  24.3 6.9 %collective-permute-start.8 = (f32[8,128]{1,0:T(8,128)S(1)}, f32[8,128]{1,0:T(8,128)S(1)}, u32[]{:S(2)}, u32[]{:S(2)}) collective-permute-start(f32[8,128]{1,0:T(8,128)S(1)} %add.46), channel_id=1, source_target_pairs={{0,8},{8,0},{1,9},{9,1},{2,10},{10,2},{3,11},{11,3},{4,12},{12,4},... | collective-permute-start | bytes 12296 | tf_op jit(solution)/shard_map/ppermute | solution.py:67
  36.4 8.1 %collective-permute-start.10 = (bf16[49,16,128]{2,1,0:T(8,128)(2,1)}, bf16[49,16,128]{2,1,0:T(8,128)(2,1)S(1)}, u32[]{:S(2)}, u32[]{:S(2)}) collective-permute-start(bf16[49,16,128]{2,1,0:T(8,128)(2,1)} %get-tuple-element.63), channel_id=1, source_target_pairs={{0,4},{2,6},{4,0},{6,2},{1,5},{3,7},{5,1},{7,3},{8,12},{10,14},{12... | collective-permute-start | bytes 602120 | tf_op jit(solution)/shard_map/ppermute | solution.py:398
  37.8 3.4 %collective-permute-start.12 = (bf16[17,16,128]{2,1,0:T(8,128)(2,1)}, bf16[17,16,128]{2,1,0:T(8,128)(2,1)S(1)}, u32[]{:S(2)}, u32[]{:S(2)}) collective-permute-start(bf16[17,16,128]{2,1,0:T(8,128)(2,1)} %get-tuple-element.70.refs_0_), channel_id=1, source_target_pairs={{0,16},{16,0},{1,17},{17,1},{2,18},{18,2},{3,19},{19,3},{4,20},{20... | collective-permute-start | bytes 208904 | tf_op jit(solution)/shard_map/ppermute | solution.py:371
  37.9 10.4 %collective-permute-start.11 = (bf16[49,16,128]{2,1,0:T(8,128)(2,1)}, bf16[49,16,128]{2,1,0:T(8,128)(2,1)S(1)}, u32[]{:S(2)}, u32[]{:S(2)}) collective-permute-start(bf16[49,16,128]{2,1,0:T(8,128)(2,1)} %get-tuple-element.64), channel_id=1, source_target_pairs={{0,6},{2,0},{4,2},{6,4},{1,7},{3,1},{5,3},{7,5},{8,14},{10,8},{12,... | collective-permute-start | bytes 602120 | tf_op jit(solution)/shard_map/ppermute | solution.py:398
  38.6 10.8 %collective-permute-start.9 = (bf16[49,16,128]{2,1,0:T(8,128)(2,1)}, bf16[49,16,128]{2,1,0:T(8,128)(2,1)S(1)}, u32[]{:S(2)}, u32[]{:S(2)}) collective-permute-start(bf16[49,16,128]{2,1,0:T(8,128)(2,1)} %get-tuple-element.62), channel_id=1, source_target_pairs={{0,2},{2,4},{4,6},{6,0},{1,3},{3,5},{5,7},{7,1},{8,10},{10,12},{12... | collective-permute-start | bytes 602120 | tf_op jit(solution)/shard_map/ppermute | solution.py:398
  42.1 7.4 %collective-permute-start.13 = (bf16[2,17,16,128]{3,2,1,0:T(8,128)(2,1)S(1)}, bf16[2,17,16,128]{3,2,1,0:T(8,128)(2,1)S(1)}, u32[]{:S(2)}, u32[]{:S(2)}) collective-permute-start(bf16[2,17,16,128]{3,2,1,0:T(8,128)(2,1)S(1)} %pad_maximum_fusion), channel_id=1, source_target_pairs={{0,32},{8,104},{32,64},{40,8},{64,96},{72,40},{96,0},{104,72},{1,3... | collective-permute-start | bytes 417800 | tf_op jit(solution)/shard_map/ppermute | solution.py:377
  44.5 6.5 %collective-permute-start.14 = (bf16[2,17,16,128]{3,2,1,0:T(8,128)(2,1)S(1)}, bf16[2,17,16,128]{3,2,1,0:T(8,128)(2,1)S(1)}, u32[]{:S(2)}, u32[]{:S(2)}) collective-permute-start(bf16[2,17,16,128]{3,2,1,0:T(8,128)(2,1)S(1)} %pad_maximum_fusion), channel_id=1, source_target_pairs={{0,64},{8,72},{32,96},{40,104},{64,0},{72,8},{96,32},{104,40},{1,6... | collective-permute-start | bytes 417800 | tf_op jit(solution)/shard_map/ppermute | solution.py:377
  44.5 9.0 %collective-permute-start.15 = (bf16[2,17,16,128]{3,2,1,0:T(8,128)(2,1)S(1)}, bf16[2,17,16,128]{3,2,1,0:T(8,128)(2,1)S(1)}, u32[]{:S(2)}, u32[]{:S(2)}) collective-permute-start(bf16[2,17,16,128]{3,2,1,0:T(8,128)(2,1)S(1)} %pad_maximum_fusion), channel_id=1, source_target_pairs={{0,96},{8,40},{32,0},{40,72},{64,32},{72,104},{96,64},{104,8},{1,9... | collective-permute-start | bytes 417800 | tf_op jit(solution)/shard_map/ppermute | solution.py:377
  53.5 0.9 copy-start.1
  54.5 17.6 %collective-permute-start.16 = (bf16[193,16,128]{2,1,0:T(8,128)(2,1)S(1)}, bf16[193,16,128]{2,1,0:T(8,128)(2,1)S(1)}, u32[]{:S(2)}, u32[]{:S(2)}) collective-permute-start(bf16[193,16,128]{2,1,0:T(8,128)(2,1)S(1)} %join.1.refs_0_), channel_id=1, source_target_pairs={{0,16},{16,0},{1,17},{17,1},{2,18},{18,2},{3,19},{19,3},{4,20},{20... | collective-permute-start | bytes 2371592 | tf_op jit(solution)/shard_map/ppermute | solution.py:371
  54.6 17.4 %collective-permute-start.17 = (bf16[193,16,128]{2,1,0:T(8,128)(2,1)S(1)}, bf16[193,16,128]{2,1,0:T(8,128)(2,1)S(1)}, u32[]{:S(2)}, u32[]{:S(2)}) collective-permute-start(bf16[193,16,128]{2,1,0:T(8,128)(2,1)S(1)} %join.1.refs_0_), channel_id=1, source_target_pairs={{0,32},{8,104},{32,64},{40,8},{64,96},{72,40},{96,0},{104,72},{1,3... | collective-permute-start | bytes 2371592 | tf_op jit(solution)/shard_map/ppermute | solution.py:377
  55.8 19.6 %collective-permute-start.18 = (bf16[193,16,128]{2,1,0:T(8,128)(2,1)S(1)}, bf16[193,16,128]{2,1,0:T(8,128)(2,1)S(1)}, u32[]{:S(2)}, u32[]{:S(2)}) collective-permute-start(bf16[193,16,128]{2,1,0:T(8,128)(2,1)S(1)} %join.1.refs_0_), channel_id=1, source_target_pairs={{0,96},{8,40},{32,0},{40,72},{64,32},{72,104},{96,64},{104,8},{1,9... | collective-permute-start | bytes 2371592 | tf_op jit(solution)/shard_map/ppermute | solution.py:377
  56.1 0.9 copy-start
  57.0 8.4 %collective-permute-start.19 = (bf16[129,16,128]{2,1,0:T(8,128)(2,1)S(1)}, bf16[129,16,128]{2,1,0:T(8,128)(2,1)S(1)}, u32[]{:S(2)}, u32[]{:S(2)}) collective-permute-start(bf16[129,16,128]{2,1,0:T(8,128)(2,1)S(1)} %join_kv.1.refs_4_), channel_id=1, source_target_pairs={{0,2},{2,4},{4,6},{6,0},{8,14},{10,8},{12,10},{14,12},{1,3},{3,5},... | collective-permute-start | bytes 1585160 | tf_op jit(solution)/shard_map/ppermute | solution.py:383
  58.4 12.4 %collective-permute-start.20 = (bf16[129,16,128]{2,1,0:T(8,128)(2,1)S(1)}, bf16[129,16,128]{2,1,0:T(8,128)(2,1)S(1)}, u32[]{:S(2)}, u32[]{:S(2)}) collective-permute-start(bf16[129,16,128]{2,1,0:T(8,128)(2,1)S(1)} %join_kv.1.refs_4_), channel_id=1, source_target_pairs={{0,6},{2,0},{4,2},{6,4},{8,10},{10,12},{12,14},{14,8},{1,7},{3,1},... | collective-permute-start | bytes 1585160 | tf_op jit(solution)/shard_map/ppermute | solution.py:383
  75.4 22.5 %collective-permute-start.25 = (bf16[193,16,128]{2,1,0:T(8,128)(2,1)S(1)}, bf16[193,16,128]{2,1,0:T(8,128)(2,1)S(1)}, u32[]{:S(2)}, u32[]{:S(2)}) collective-permute-start(bf16[193,16,128]{2,1,0:T(8,128)(2,1)S(1)} %collective-permute-done.17.refs_1_), channel_id=1, source_target_pairs={{0,32},{8,104},{32,64},{40,8},{64,96},{72,40},{96,0},{104,72},{1,3... | collective-permute-start | bytes 2371592 | tf_op jit(solution)/shard_map/ppermute | solution.py:377
  76.3 21.6 %collective-permute-start.21 = (bf16[129,16,128]{2,1,0:T(8,128)(2,1)S(1)}, bf16[129,16,128]{2,1,0:T(8,128)(2,1)S(1)}, u32[]{:S(2)}, u32[]{:S(2)}) collective-permute-start(bf16[129,16,128]{2,1,0:T(8,128)(2,1)S(1)} %slice.18), channel_id=1, source_target_pairs={{0,32},{8,104},{32,64},{40,8},{64,96},{72,40},{96,0},{104,72},{1,3... | collective-permute-start | bytes 1585160 | tf_op jit(solution)/shard_map/ppermute | solution.py:377
  76.4 21.5 %collective-permute-start.22 = (bf16[129,16,128]{2,1,0:T(8,128)(2,1)S(1)}, bf16[129,16,128]{2,1,0:T(8,128)(2,1)S(1)}, u32[]{:S(2)}, u32[]{:S(2)}) collective-permute-start(bf16[129,16,128]{2,1,0:T(8,128)(2,1)S(1)} %slice.18), channel_id=1, source_target_pairs={{0,96},{8,40},{32,0},{40,72},{64,32},{72,104},{96,64},{104,8},{1,9... | collective-permute-start | bytes 1585160 | tf_op jit(solution)/shard_map/ppermute | solution.py:377
  77.9 5.6 %collective-permute-start.23 = (bf16[64,16,128]{2,1,0:T(8,128)(2,1)S(1)}, bf16[64,16,128]{2,1,0:T(8,128)(2,1)S(1)}, u32[]{:S(2)}, u32[]{:S(2)}) collective-permute-start(bf16[64,16,128]{2,1,0:T(8,128)(2,1)S(1)} %slice.19), channel_id=1, source_target_pairs={{0,16},{16,0},{1,17},{17,1},{2,18},{18,2},{3,19},{19,3},{4,20},{20... | collective-permute-start | bytes 786440 | tf_op jit(solution)/shard_map/ppermute | solution.py:371
  78.5 10.2 %collective-permute-start.24 = (bf16[64,16,128]{2,1,0:T(8,128)(2,1)S(1)}, bf16[64,16,128]{2,1,0:T(8,128)(2,1)S(1)}, u32[]{:S(2)}, u32[]{:S(2)}) collective-permute-start(bf16[64,16,128]{2,1,0:T(8,128)(2,1)S(1)} %slice.20), channel_id=1, source_target_pairs={{0,16},{16,0},{1,17},{17,1},{2,18},{18,2},{3,19},{19,3},{4,20},{20... | collective-permute-start | bytes 786440 | tf_op jit(solution)/shard_map/ppermute | solution.py:371
  97.9 12.3 %collective-permute-start.29 = (bf16[1159,16,128]{2,1,0:T(8,128)(2,1)S(1)}, bf16[1159,16,128]{2,1,0:T(8,128)(2,1)S(1)}, u32[]{:S(2)}, u32[]{:S(2)}) collective-permute-start(bf16[1159,16,128]{2,1,0:T(8,128)(2,1)S(1)} %get-tuple-element.86), channel_id=1, source_target_pairs={{0,8},{8,0},{1,9},{9,1},{2,10},{10,2},{3,11},{11,3},{4,12},{12,4},... | collective-permute-start | bytes 14241800 | tf_op jit(solution)/shard_map/ppermute | solution.py:367
  100.6 8.4 %collective-permute-start.28 = (bf16[129,16,128]{2,1,0:T(8,128)(2,1)S(1)}, bf16[129,16,128]{2,1,0:T(8,128)(2,1)S(1)}, u32[]{:S(2)}, u32[]{:S(2)}) collective-permute-start(bf16[129,16,128]{2,1,0:T(8,128)(2,1)S(1)} %collective-permute-done.19.refs_5_), channel_id=1, source_target_pairs={{0,2},{2,4},{4,6},{6,0},{8,14},{10,8},{12,10},{14,12},{1,3},{3,5},... | collective-permute-start | bytes 1585160 | tf_op jit(solution)/shard_map/ppermute | solution.py:383
  101.6 8.5 %collective-permute-start.26 = (bf16[129,16,128]{2,1,0:T(8,128)(2,1)S(1)}, bf16[129,16,128]{2,1,0:T(8,128)(2,1)S(1)}, u32[]{:S(2)}, u32[]{:S(2)}) collective-permute-start(bf16[129,16,128]{2,1,0:T(8,128)(2,1)S(1)} %collective-permute-done.21.refs_0_), channel_id=1, source_target_pairs={{0,32},{8,104},{32,64},{40,8},{64,96},{72,40},{96,0},{104,72},{1,3... | collective-permute-start | bytes 1585160 | tf_op jit(solution)/shard_map/ppermute | solution.py:377
  102.1 8.1 %collective-permute-start.27 = (bf16[64,16,128]{2,1,0:T(8,128)(2,1)S(1)}, bf16[64,16,128]{2,1,0:T(8,128)(2,1)S(1)}, u32[]{:S(2)}, u32[]{:S(2)}) collective-permute-start(bf16[64,16,128]{2,1,0:T(8,128)(2,1)S(1)} %slice.21), channel_id=1, source_target_pairs={{0,16},{16,0},{1,17},{17,1},{2,18},{18,2},{3,19},{19,3},{4,20},{20... | collective-permute-start | bytes 786440 | tf_op jit(solution)/shard_map/ppermute | solution.py:371
  110.1 8.0 %collective-permute-start.30 = (bf16[579,16,128]{2,1,0:T(8,128)(2,1)S(1)}, bf16[579,16,128]{2,1,0:T(8,128)(2,1)S(1)}, u32[]{:S(2)}, u32[]{:S(2)}) collective-permute-start(bf16[579,16,128]{2,1,0:T(8,128)(2,1)S(1)} %get-tuple-element.97), channel_id=1, source_target_pairs={{0,8},{8,0},{1,9},{9,1},{2,10},{10,2},{3,11},{11,3},{4,12},{12,4},... | collective-permute-start | bytes 7114760 | tf_op jit(solution)/shard_map/ppermute | solution.py:367
  112.1 6.1 %collective-permute-start.31 = (bf16[129,16,128]{2,1,0:T(8,128)(2,1)S(1)}, bf16[129,16,128]{2,1,0:T(8,128)(2,1)S(1)}, u32[]{:S(2)}, u32[]{:S(2)}) collective-permute-start(bf16[129,16,128]{2,1,0:T(8,128)(2,1)S(1)} %collective-permute-done.26.refs_0_), channel_id=1, source_target_pairs={{0,8},{8,0},{1,9},{9,1},{2,10},{10,2},{3,11},{11,3},{4,12},{12,4},... | collective-permute-start | bytes 1585160 | tf_op jit(solution)/shard_map/ppermute | solution.py:367
  112.1 6.1 %collective-permute-start.33 = (bf16[129,16,128]{2,1,0:T(8,128)(2,1)S(1)}, bf16[129,16,128]{2,1,0:T(8,128)(2,1)S(1)}, u32[]{:S(2)}, u32[]{:S(2)}) collective-permute-start(bf16[129,16,128]{2,1,0:T(8,128)(2,1)S(1)} %collective-permute-done.28.refs_2_), channel_id=1, source_target_pairs={{0,8},{8,0},{1,9},{9,1},{2,10},{10,2},{3,11},{11,3},{4,12},{12,4},... | collective-permute-start | bytes 1585160 | tf_op jit(solution)/shard_map/ppermute | solution.py:367
  112.6 5.6 %collective-permute-start.32 = (bf16[64,16,128]{2,1,0:T(8,128)(2,1)S(1)}, bf16[64,16,128]{2,1,0:T(8,128)(2,1)S(1)}, u32[]{:S(2)}, u32[]{:S(2)}) collective-permute-start(bf16[64,16,128]{2,1,0:T(8,128)(2,1)S(1)} %collective-permute-done.27.refs_1_), channel_id=1, source_target_pairs={{0,8},{8,0},{1,9},{9,1},{2,10},{10,2},{3,11},{11,3},{4,12},{12,4},... | collective-permute-start | bytes 786440 | tf_op jit(solution)/shard_map/ppermute | solution.py:367

commit v5 on v4

--- a/solution.py
+++ b/solution.py
@@ -246,7 +246,7 @@
 SCALES = {"P": 0, "A": 0, "K": PLANE_T - 1}
 
 
-def lay(place, own, got, outs=None, pack=False, last=False):
+def lay(place, own, got, outs=None, pack=0, last=False):
     views = [(n, 0, piece, False) for n, (_, piece) in enumerate(own)]
     for n, (_, held) in enumerate(got):
         at = 0
@@ -254,9 +254,9 @@
             views.append((len(own) + n, at, piece, True))
             at += SIZE[piece[0]]
     arrays = [array for array, _ in own + got]
-    total = sum(SIZE[piece[0]] for _, piece in own)
+    total = sum(SIZE[piece[0]] for _, piece in own[:pack])
     with_scales = [view for view in views if view[2][0] != "B"]
-    count = 2 * len(views) + (len(own) if pack else 0)
+    count = 2 * len(views) + pack
 
     def kernel(place_ref, *refs):
         ins = refs[: len(arrays)]
@@ -278,7 +278,7 @@
             gets[-1].start()
         if pack:
             at = 0
-            for n, (_, piece) in enumerate(own):
+            for n, (_, piece) in enumerate(own[:pack]):
                 copy(ins[n], results[1].at[pl.ds(at, SIZE[piece[0]])])
                 at += SIZE[piece[0]]
         for n, base, (kind, steps, over_y), over_c in views:
@@ -411,20 +411,24 @@
     a1, a3 = along_x(qa), along_x(qa, 3)
     held1 = [("P", 0, False), ("P", 1, False), ("P", 3, False), ("P", 0, True)]
     held1 += [("K", 0, False), ("K", 1, False), ("K", 3, False)]
-    *outs, pack1 = lay(place, list(zip([p0, p1, p3, q0, w0, w1, w3], held1)), [], pack=True)
+    *outs, pack1 = lay(place, list(zip([p0, p1, p3, q0, w0, w1, w3], held1)), [], pack=7)
     a1, a3, b1, b3, p2, pack1, *outs = after(a1, a3, b1, b3, p2, pack1, *outs)
 
     b2, a2, w2 = swap_y(p2[A_T:FULL_T]), along_x(a1), along_z(w1)
-    got1 = swap_core(pack1)
-    held2 = [("A", 1, True), ("A", 3, True), ("B", 1, True), ("B", 3, True), ("P", 2, False)]
-    *outs, pack2 = lay(place, list(zip([a1, a3, b1, b3, p2], held2)), [], outs, pack=True)
-    a2, b2, w2, got1, pack2, *outs = after(a2, b2, w2, got1, pack2, *outs)
+    got1, got_p2 = swap_core(pack1), swap_core(p2)
+    held2 = [("A", 1, True), ("A", 3, True), ("B", 1, True), ("B", 3, True)]
+    held_p2 = [("P", 2, False)]
+    own = list(zip([a1, a3, b1, b3, p2], held2 + held_p2))
+    *outs, pack2 = lay(place, own, [], outs, pack=4)
+    a2, b2, w2, got1, got_p2, pack2, *outs = after(a2, b2, w2, got1, got_p2, pack2, *outs)
 
     held3 = [("A", 2, True), ("B", 2, True), ("K", 2, False)]
     own = [a2, b2, w2]
-    got = [(swap_core(pack2), held2)] + [(swap_core(v), [p]) for v, p in zip(own, held3)]
-    outs = lay(place, list(zip(own, held3)), [(got1, held1)], outs)
-    exp_rollout, kv_rollout, exp_scales, kv_scales = lay(place, [], got, outs, last=True)
+    got2 = swap_core(pack2)
+    got3 = [(swap_core(v), [p]) for v, p in zip(own, held3)]
+    outs = lay(place, list(zip(own, held3)), [(got1, held1), (got_p2, held_p2)], outs)
+    outs = lay(place, [], [(got2, held2)], outs)
+    exp_rollout, kv_rollout, exp_scales, kv_scales = lay(place, [], got3, outs, last=True)
     return (
         kv_new,
         exp_new,

time: 121 us -> 120 us (level)
  waiting for transfers between devices: 57.5 us -> 54.7 us
    ppermute x5 -> x6, waiting for transfers between devices: 2.69 us -> 0.02 us  [swap_core(): return lax.ppermute(v, 'c', ring(2, 1))]
    ppermute x5 -> x6, starting transfers between devices: 5.13 us -> 5.82 us  [swap_core(): return lax.ppermute(v, 'c', ring(2, 1))]
    pallas_call x4 -> x5, Pallas kernels: 10 us -> 10.6 us  [lay(): pl.pallas_call(kernel, out_shape=tuple(out_shape), in_specs=[pl.BlockSpec...]
  transfers between devices with their start and end apart: 34 -> 35, of which waited for: 22 -> 22; matrix products, arithmetic and copies ran while one was open for 1% -> 1% of each run, Pallas kernels for 6% -> 7%
where the time goes in v5:
time: 120 us; the launch traced here: 119 us
  waiting for transfers between devices  54.7 us (46%)
  starting transfers between devices  42.5 us (35%)
  Pallas kernels  17.2 us (14%)
  other arithmetic  2.19 us (2%)
  local copies, waits for them, and re-layouts  1.9 us (2%)
    ppermute x3, waiting for transfers between devices, along_z(): return lax.ppermute(v, ('c', 'z'), pairs)  16.9 us
    ppermute x9, waiting for transfers between devices, along_x(): return lax.ppermute(v, ('x', 'c'), pairs)  16.6 us
    ppermute x6, starting transfers between devices, sum_over_devices(): others = [lax.ppermute(v, axis, ring(4, k)) for k in (1, 2, 3)]  11.3 us
    pallas_call x5, Pallas kernels, lay(): pl.pallas_call(kernel, out_shape=tuple(out_shape), in_specs=[pl.BlockSpec...  10.6 us
    ppermute x5, waiting for transfers between devices, swap_y(): return lax.ppermute(v, 'yl', ring(2, 1))  10.4 us
    ppermute x9, starting transfers between devices, along_x(): return lax.ppermute(v, ('x', 'c'), pairs)  7.44 us
    ppermute x1, starting transfers between devices, sum_over_devices(): v = v + lax.ppermute(v, 'c', ring(2, 1))  6.04 us
    ppermute x6, starting transfers between devices, swap_core(): return lax.ppermute(v, 'c', ring(2, 1))  5.82 us
  transfers between devices with their start and end apart: 35, of which 22 were waited for; matrix products, arithmetic and copies ran while one was open for 1% of the time, Pallas kernels for 7%

profile of v5, /device:TPU:1, one launch (start us, length us, event | category | flops | bytes accessed | tf_op | source)
XLA Modules:
  0.0 119.3 jit_solution(5786167949788483791)
XLA Ops:
  0.6 1.9 %sum_of_squares.1 = f32[8,128]{1,0:T(8,128)} custom-call(f32[2,1,128,128]{3,2,1,0:T(8,128)} %refs_1_.1, f32[4,1,3,128,128]{4,3,2,1,0:T(8,128)} %refs_5_.1), custom_call_target="tpu_custom_call" | custom-call | tf_op jit(solution)/shard_map/sum_of_squares/pallas_call | solution.py:52
  2.5 2.0 %collective-permute-start = (f32[8,128]{1,0:T(8,128)}, f32[8,128]{1,0:T(8,128)S(1)}, u32[]{:S(2)}, u32[]{:S(2)}) collective-permute-start(f32[8,128]{1,0:T(8,128)} %sum_of_squares.1), channel_id=1, source_target_pairs={{0,32},{32,64},{64,96},{96,0},{1,33},{33,65},{65,97},{97,1},{2,34}... | collective-permute-start | bytes 12296 | tf_op jit(solution)/shard_map/ppermute | solution.py:63
  4.5 2.5 %collective-permute-start.1 = (f32[8,128]{1,0:T(8,128)}, f32[8,128]{1,0:T(8,128)S(1)}, u32[]{:S(2)}, u32[]{:S(2)}) collective-permute-start(f32[8,128]{1,0:T(8,128)} %sum_of_squares.1), channel_id=1, source_target_pairs={{0,64},{32,96},{64,0},{96,32},{1,65},{33,97},{65,1},{97,33},{2,66}... | collective-permute-start | bytes 12296 | tf_op jit(solution)/shard_map/ppermute | solution.py:63
  7.0 1.2 collective-permute-start.2
  8.2 0.6 collective-permute-done.1
  8.7 1.2 %collective-permute-done.2 = f32[8,128]{1,0:T(8,128)S(1)} collective-permute-done((f32[8,128]{1,0:T(8,128)}, f32[8,128]{1,0:T(8,128)S(1)}, u32[]{:S(2)}, u32[]{:S(2)}) %collective-permute-start.2) | collective-permute-done | bytes 4128 | tf_op jit(solution)/shard_map/ppermute | solution.py:63
  10.0 0.7 add_add_fusion.1
  10.7 1.6 %collective-permute-start.3 = (f32[8,128]{1,0:T(8,128)S(1)}, f32[8,128]{1,0:T(8,128)S(1)}, u32[]{:S(2)}, u32[]{:S(2)}) collective-permute-start(f32[8,128]{1,0:T(8,128)S(1)} %add_add_fusion.1), channel_id=1, source_target_pairs={{0,2},{2,4},{4,6},{6,0},{1,3},{3,5},{5,7},{7,1},{8,10},{10,12},{12... | collective-permute-start | bytes 12296 | tf_op jit(solution)/shard_map/ppermute | solution.py:63
  12.3 3.3 %collective-permute-start.4 = (f32[8,128]{1,0:T(8,128)S(1)}, f32[8,128]{1,0:T(8,128)S(1)}, u32[]{:S(2)}, u32[]{:S(2)}) collective-permute-start(f32[8,128]{1,0:T(8,128)S(1)} %add_add_fusion.1), channel_id=1, source_target_pairs={{0,4},{2,6},{4,0},{6,2},{1,5},{3,7},{5,1},{7,3},{8,12},{10,14},{12... | collective-permute-start | bytes 12296 | tf_op jit(solution)/shard_map/ppermute | solution.py:63
  15.6 0.7 collective-permute-start.5
  16.3 0.3 collective-permute-done.4
  16.6 1.4 %collective-permute-done.5 = f32[8,128]{1,0:T(8,128)S(1)} collective-permute-done((f32[8,128]{1,0:T(8,128)S(1)}, f32[8,128]{1,0:T(8,128)S(1)}, u32[]{:S(2)}, u32[]{:S(2)}) %collective-permute-start.5) | collective-permute-done | bytes 4128 | tf_op jit(solution)/shard_map/ppermute | solution.py:63
  18.1 1.3 %collective-permute-start.6 = (f32[8,128]{1,0:T(8,128)S(1)}, f32[8,128]{1,0:T(8,128)S(1)}, u32[]{:S(2)}, u32[]{:S(2)}) collective-permute-start(f32[8,128]{1,0:T(8,128)S(1)} %add_add_fusion), channel_id=1, source_target_pairs={{0,16},{16,0},{1,17},{17,1},{2,18},{18,2},{3,19},{19,3},{4,20},{20... | collective-permute-start | bytes 12296 | tf_op jit(solution)/shard_map/ppermute | solution.py:66
  19.4 1.2 collective-permute-done.6
  20.5 2.7 %collective-permute-start.7 = (f32[8,128]{1,0:T(8,128)S(1)}, f32[8,128]{1,0:T(8,128)S(1)}, u32[]{:S(2)}, u32[]{:S(2)}) collective-permute-start(f32[8,128]{1,0:T(8,128)S(1)} %add.45), channel_id=1, source_target_pairs={{16,1},{1,16},{17,0},{0,17},{18,3},{3,18},{19,2},{2,19},{20,5},{5,... | collective-permute-start | bytes 12296 | tf_op jit(solution)/shard_map/ppermute | solution.py:66
  23.3 1.0 collective-permute-done.7
  24.3 6.0 %collective-permute-start.8 = (f32[8,128]{1,0:T(8,128)S(1)}, f32[8,128]{1,0:T(8,128)S(1)}, u32[]{:S(2)}, u32[]{:S(2)}) collective-permute-start(f32[8,128]{1,0:T(8,128)S(1)} %add.46), channel_id=1, source_target_pairs={{0,8},{8,0},{1,9},{9,1},{2,10},{10,2},{3,11},{11,3},{4,12},{12,4},... | collective-permute-start | bytes 12296 | tf_op jit(solution)/shard_map/ppermute | solution.py:67
  30.3 0.8 collective-permute-done.8
  31.1 0.6 add.47.total_ref
  31.7 4.7 %update.1 = (f32[2,1,128,128]{3,2,1,0:T(8,128)}, f32[4,1,3,128,128]{4,3,2,1,0:T(8,128)}, bf16[49,16,128]{2,1,0:T(8,128)(2,1)}, bf16[49,16,128]{2,1,0:T(8,128)(2,...) custom-call(s32[1]{0:T(128)} %bitcast.place_ref, s32[4]{0:T(128)} %owner_ref.1, ...), custom_call_target="tpu_custom_call" | custom-call | tf_op jit(solution)/shard_map/update/pallas_call | solution.py:163
  36.4 1.4 %collective-permute-start.10 = (bf16[49,16,128]{2,1,0:T(8,128)(2,1)}, bf16[49,16,128]{2,1,0:T(8,128)(2,1)S(1)}, u32[]{:S(2)}, u32[]{:S(2)}) collective-permute-start(bf16[49,16,128]{2,1,0:T(8,128)(2,1)} %get-tuple-element.67), channel_id=1, source_target_pairs={{0,4},{2,6},{4,0},{6,2},{1,5},{3,7},{5,1},{7,3},{8,12},{10,14},{12... | collective-permute-start | bytes 602120 | tf_op jit(solution)/shard_map/ppermute | solution.py:398
  37.9 0.7 collective-permute-start.11
  38.6 0.7 collective-permute-start.9
  39.4 1.8 %collective-permute-done.12.refs_1_ = bf16[17,16,128]{2,1,0:T(8,128)(2,1)S(1)} collective-permute-done((bf16[17,16,128]{2,1,0:T(8,128)(2,1)}, bf16[17,16,128]{2,1,0:T(8,128)(2,1)S(1)}, u32[]{:S(2)}, u32[]{:S(2)}) %collective-permute-start.12) | collective-permute-done | bytes 69664 | tf_op jit(solution)/shard_map/ppermute | solution.py:371
  41.2 0.9 pad_maximum_fusion
  42.1 2.4 %collective-permute-start.13 = (bf16[2,17,16,128]{3,2,1,0:T(8,128)(2,1)S(1)}, bf16[2,17,16,128]{3,2,1,0:T(8,128)(2,1)S(1)}, u32[]{:S(2)}, u32[]{:S(2)}) collective-permute-start(bf16[2,17,16,128]{3,2,1,0:T(8,128)(2,1)S(1)} %pad_maximum_fusion), channel_id=1, source_target_pairs={{0,32},{8,104},{32,64},{40,8},{64,96},{72,40},{96,0},{104,72},{1,3... | collective-permute-start | bytes 417800 | tf_op jit(solution)/shard_map/ppermute | solution.py:377
  44.5 0.7 collective-permute-start.15
  45.2 3.1 %collective-permute-done.11.refs_3_ = bf16[49,16,128]{2,1,0:T(8,128)(2,1)S(1)} collective-permute-done((bf16[49,16,128]{2,1,0:T(8,128)(2,1)}, bf16[49,16,128]{2,1,0:T(8,128)(2,1)S(1)}, u32[]{:S(2)}, u32[]{:S(2)}) %collective-permute-start.11) | collective-permute-done | bytes 200736 | tf_op jit(solution)/shard_map/ppermute | solution.py:398
  48.3 1.1 collective-permute-done.9.refs_1_
  49.4 1.6 %collective-permute-done.14.refs_3_ = bf16[2,17,16,128]{3,2,1,0:T(8,128)(2,1)S(1)} collective-permute-done((bf16[2,17,16,128]{3,2,1,0:T(8,128)(2,1)S(1)}, bf16[2,17,16,128]{3,2,1,0:T(8,128)(2,1)S(1)}, u32[]{:S(2)}, u32[]{:S(2)}) %collective-permute-start.14) | collective-permute-done | bytes 139296 | tf_op jit(solution)/shard_map/ppermute | solution.py:377
  51.0 2.4 %collective-permute-done.15.refs_4_ = bf16[2,17,16,128]{3,2,1,0:T(8,128)(2,1)S(1)} collective-permute-done((bf16[2,17,16,128]{3,2,1,0:T(8,128)(2,1)S(1)}, bf16[2,17,16,128]{3,2,1,0:T(8,128)(2,1)S(1)}, u32[]{:S(2)}, u32[]{:S(2)}) %collective-permute-start.15) | collective-permute-done | bytes 139296 | tf_op jit(solution)/shard_map/ppermute | solution.py:377
  53.5 0.9 copy-done.1
  54.5 0.2 collective-permute-start.16
  54.6 1.1 collective-permute-start.17
  55.8 0.3 collective-permute-start.18
  56.1 0.9 copy-done
  57.0 1.4 %collective-permute-start.19 = (bf16[129,16,128]{2,1,0:T(8,128)(2,1)S(1)}, bf16[129,16,128]{2,1,0:T(8,128)(2,1)S(1)}, u32[]{:S(2)}, u32[]{:S(2)}) collective-permute-start(bf16[129,16,128]{2,1,0:T(8,128)(2,1)S(1)} %join_kv.1.refs_4_), channel_id=1, source_target_pairs={{0,2},{2,4},{4,6},{6,0},{8,14},{10,8},{12,10},{14,12},{1,3},{3,5},... | collective-permute-start | bytes 1585160 | tf_op jit(solution)/shard_map/ppermute | solution.py:383
  58.4 0.1 collective-permute-start.20
  58.6 6.9 %collective-permute-done.19.refs_5_ = bf16[129,16,128]{2,1,0:T(8,128)(2,1)S(1)} collective-permute-done((bf16[129,16,128]{2,1,0:T(8,128)(2,1)S(1)}, bf16[129,16,128]{2,1,0:T(8,128)(2,1)S(1)}, u32[]{:S(2)}, u32[]{:S(2)}) %collective-permute-start.19) | collective-permute-done | bytes 528416 | tf_op jit(solution)/shard_map/ppermute | solution.py:383
  65.5 5.3 %collective-permute-done.20.refs_6_ = bf16[129,16,128]{2,1,0:T(8,128)(2,1)S(1)} collective-permute-done((bf16[129,16,128]{2,1,0:T(8,128)(2,1)S(1)}, bf16[129,16,128]{2,1,0:T(8,128)(2,1)S(1)}, u32[]{:S(2)}, u32[]{:S(2)}) %collective-permute-start.20) | collective-permute-done | bytes 528416 | tf_op jit(solution)/shard_map/ppermute | solution.py:383
  70.8 1.3 %collective-permute-done.16.refs_3_ = bf16[193,16,128]{2,1,0:T(8,128)(2,1)S(1)} collective-permute-done((bf16[193,16,128]{2,1,0:T(8,128)(2,1)S(1)}, bf16[193,16,128]{2,1,0:T(8,128)(2,1)S(1)}, u32[]{:S(2)}, u32[]{:S(2)}) %collective-permute-start.16) | collective-permute-done | bytes 790560 | tf_op jit(solution)/shard_map/ppermute | solution.py:371
  72.0 3.3 %collective-permute-done.18.refs_2_ = bf16[193,16,128]{2,1,0:T(8,128)(2,1)S(1)} collective-permute-done((bf16[193,16,128]{2,1,0:T(8,128)(2,1)S(1)}, bf16[193,16,128]{2,1,0:T(8,128)(2,1)S(1)}, u32[]{:S(2)}, u32[]{:S(2)}) %collective-permute-start.18) | collective-permute-done | bytes 790560 | tf_op jit(solution)/shard_map/ppermute | solution.py:377
  75.4 0.9 collective-permute-start.25
  76.3 0.1 collective-permute-start.21
  76.4 1.4 %collective-permute-start.22 = (bf16[129,16,128]{2,1,0:T(8,128)(2,1)S(1)}, bf16[129,16,128]{2,1,0:T(8,128)(2,1)S(1)}, u32[]{:S(2)}, u32[]{:S(2)}) collective-permute-start(bf16[129,16,128]{2,1,0:T(8,128)(2,1)S(1)} %slice.18), channel_id=1, source_target_pairs={{0,96},{8,40},{32,0},{40,72},{64,32},{72,104},{96,64},{104,8},{1,9... | collective-permute-start | bytes 1585160 | tf_op jit(solution)/shard_map/ppermute | solution.py:377
  77.9 0.6 collective-permute-start.23
  78.5 1.0 collective-permute-start.24
  79.5 2.8 %lay.5 = (bf16[2,1536,16,128]{3,2,1,0:T(8,128)(2,1)}, bf16[2,8,2,4,8,16,128]{6,5,4,3,2,1,0:T(8,128)(2,1)}, f32[2,16,128]{2,1,0:T(8,128)S(1)}, bf16[1159,16,128]{2,1,0:T(8,128)(2,1)S(1)}) custom-call(s32[1]{0:T(128)} %bitcast.place_ref, bf16[193,16,128]{2,1,0:T(8,128)(2,1)S(1)} %join.1.refs_0_, bf16[193,16,128]{2,1,0:T(8,128)(2,1)S(1)} %collective-permute-done.17.refs_1_, ...), custom_call_target="tpu_custom_call" | custom-call | bytes 11010048 | tf_op jit(solution)/shard_map/lay/pallas_call | solution.py:343
  82.3 1.2 collective-permute-done.23.refs_2_
  83.5 5.3 %collective-permute-done.24.refs_3_ = bf16[64,16,128]{2,1,0:T(8,128)(2,1)S(1)} collective-permute-done((bf16[64,16,128]{2,1,0:T(8,128)(2,1)S(1)}, bf16[64,16,128]{2,1,0:T(8,128)(2,1)S(1)}, u32[]{:S(2)}, u32[]{:S(2)}) %collective-permute-start.24) | collective-permute-done | bytes 262176 | tf_op jit(solution)/shard_map/ppermute | solution.py:371
  88.8 9.1 %collective-permute-done.21.refs_0_ = bf16[129,16,128]{2,1,0:T(8,128)(2,1)S(1)} collective-permute-done((bf16[129,16,128]{2,1,0:T(8,128)(2,1)S(1)}, bf16[129,16,128]{2,1,0:T(8,128)(2,1)S(1)}, u32[]{:S(2)}, u32[]{:S(2)}) %collective-permute-start.21) | collective-permute-done | bytes 528416 | tf_op jit(solution)/shard_map/ppermute | solution.py:377
  97.9 2.7 %collective-permute-start.29 = (bf16[1159,16,128]{2,1,0:T(8,128)(2,1)S(1)}, bf16[1159,16,128]{2,1,0:T(8,128)(2,1)S(1)}, u32[]{:S(2)}, u32[]{:S(2)}) collective-permute-start(bf16[1159,16,128]{2,1,0:T(8,128)(2,1)S(1)} %get-tuple-element.90), channel_id=1, source_target_pairs={{0,8},{8,0},{1,9},{9,1},{2,10},{10,2},{3,11},{11,3},{4,12},{12,4},... | collective-permute-start | bytes 14241800 | tf_op jit(solution)/shard_map/ppermute | solution.py:367
  100.7 1.0 collective-permute-start.28
  101.7 0.4 collective-permute-start.26
  102.1 0.5 collective-permute-start.27
  102.7 1.7 %lay.6 = (bf16[2,1536,16,128]{3,2,1,0:T(8,128)(2,1)}, bf16[2,8,2,4,8,16,128]{6,5,4,3,2,1,0:T(8,128)(2,1)}, f32[2,16,128]{2,1,0:T(8,128)S(1)}, bf16[386,16,128]{2,1,0:T(8,128)(2,1)S(1)}) custom-call(s32[1]{0:T(128)} %bitcast.place_ref, bf16[129,16,128]{2,1,0:T(8,128)(2,1)S(1)} %collective-permute-done.21.refs_0_, ...), custom_call_target="tpu_custom_call", output_to_operand_aliasing={{0}: (6, {}), {1}: (7, {})} | custom-call | bytes 7340032 | tf_op jit(solution)/shard_map/lay/pallas_call | solution.py:343
  104.4 4.7 %collective-permute-done.28.refs_2_ = bf16[129,16,128]{2,1,0:T(8,128)(2,1)S(1)} collective-permute-done((bf16[129,16,128]{2,1,0:T(8,128)(2,1)S(1)}, bf16[129,16,128]{2,1,0:T(8,128)(2,1)S(1)}, u32[]{:S(2)}, u32[]{:S(2)}) %collective-permute-start.28) | collective-permute-done | bytes 528416 | tf_op jit(solution)/shard_map/ppermute | solution.py:383
  109.0 0.9 collective-permute-done.27.refs_1_
  109.9 0.1 collective-permute-done.26.refs_0_
  110.1 2.4 %collective-permute-start.34 = (bf16[386,16,128]{2,1,0:T(8,128)(2,1)S(1)}, bf16[386,16,128]{2,1,0:T(8,128)(2,1)S(1)}, u32[]{:S(2)}, u32[]{:S(2)}) collective-permute-start(bf16[386,16,128]{2,1,0:T(8,128)(2,1)S(1)} %get-tuple-element.104), channel_id=1, source_target_pairs={{0,8},{8,0},{1,9},{9,1},{2,10},{10,2},{3,11},{11,3},{4,12},{12,4},... | collective-permute-start | bytes 4743176 | tf_op jit(solution)/shard_map/ppermute | solution.py:367
  112.6 0.4 collective-permute-start.33
  113.1 3.1 %lay.7 = (bf16[2,1536,16,128]{3,2,1,0:T(8,128)(2,1)}, bf16[2,8,2,4,8,16,128]{6,5,4,3,2,1,0:T(8,128)(2,1)}, f32[2,16,128]{2,1,0:T(8,128)S(1)}) custom-call(s32[1]{0:T(128)} %bitcast.place_ref, bf16[129,16,128]{2,1,0:T(8,128)(2,1)S(1)} %collective-permute-done.26.refs_0_, ...), custom_call_target="tpu_custom_call", output_to_operand_aliasing={{0}: (6, {}), {1}: (7, {})} | custom-call | bytes 11534336 | tf_op jit(solution)/shard_map/lay/pallas_call | solution.py:343
  116.2 1.3 %lay.8 = (bf16[2,1536,16,128]{3,2,1,0:T(8,128)(2,1)}, bf16[2,8,2,4,8,16,128]{6,5,4,3,2,1,0:T(8,128)(2,1)}, f32[2,16,128]{2,1,0:T(8,128)S(1)}) custom-call(s32[1]{0:T(128)} %bitcast.place_ref, bf16[386,16,128]{2,1,0:T(8,128)(2,1)S(1)} %collective-permute-done.34.refs_0_, ...), custom_call_target="tpu_custom_call", output_to_operand_aliasing={{0}: (2, {}), {1}: (3, {})} | custom-call | bytes 4194304 | tf_op jit(solution)/shard_map/lay/pallas_call | solution.py:343
  117.5 1.7 %lay.9 = (bf16[2,1536,16,128]{3,2,1,0:T(8,128)(2,1)}, bf16[2,8,2,4,8,16,128]{6,5,4,3,2,1,0:T(8,128)(2,1)}, f32[2,2,128]{2,1,0:T(2,128)}, f32[2,128]{1,0:T(2,128)}) custom-call(s32[1]{0:T(128)} %bitcast.place_ref, bf16[129,16,128]{2,1,0:T(8,128)(2,1)S(1)} %collective-permute-done.31.refs_0_, ...), custom_call_target="tpu_custom_call", output_to_operand_aliasing={{0}: (4, {}), {1}: (5, {})} | custom-call | bytes 3145728 | tf_op jit(solution)/shard_map/lay/pallas_call | solution.py:343
  (29 shorter events, 0.6 us)
Async XLA Ops:
  2.5 5.6 %collective-permute-start = (f32[8,128]{1,0:T(8,128)}, f32[8,128]{1,0:T(8,128)S(1)}, u32[]{:S(2)}, u32[]{:S(2)}) collective-permute-start(f32[8,128]{1,0:T(8,128)} %sum_of_squares.1), channel_id=1, source_target_pairs={{0,32},{32,64},{64,96},{96,0},{1,33},{33,65},{65,97},{97,1},{2,34}... | collective-permute-start | bytes 12296 | tf_op jit(solution)/shard_map/ppermute | solution.py:63
  4.5 4.2 %collective-permute-start.1 = (f32[8,128]{1,0:T(8,128)}, f32[8,128]{1,0:T(8,128)S(1)}, u32[]{:S(2)}, u32[]{:S(2)}) collective-permute-start(f32[8,128]{1,0:T(8,128)} %sum_of_squares.1), channel_id=1, source_target_pairs={{0,64},{32,96},{64,0},{96,32},{1,65},{33,97},{65,1},{97,33},{2,66}... | collective-permute-start | bytes 12296 | tf_op jit(solution)/shard_map/ppermute | solution.py:63
  7.0 3.0 %collective-permute-start.2 = (f32[8,128]{1,0:T(8,128)}, f32[8,128]{1,0:T(8,128)S(1)}, u32[]{:S(2)}, u32[]{:S(2)}) collective-permute-start(f32[8,128]{1,0:T(8,128)} %sum_of_squares.1), channel_id=1, source_target_pairs={{0,96},{32,0},{64,32},{96,64},{1,97},{33,1},{65,33},{97,65},{2,98}... | collective-permute-start | bytes 12296 | tf_op jit(solution)/shard_map/ppermute | solution.py:63
  10.7 5.7 %collective-permute-start.3 = (f32[8,128]{1,0:T(8,128)S(1)}, f32[8,128]{1,0:T(8,128)S(1)}, u32[]{:S(2)}, u32[]{:S(2)}) collective-permute-start(f32[8,128]{1,0:T(8,128)S(1)} %add_add_fusion.1), channel_id=1, source_target_pairs={{0,2},{2,4},{4,6},{6,0},{1,3},{3,5},{5,7},{7,1},{8,10},{10,12},{12... | collective-permute-start | bytes 12296 | tf_op jit(solution)/shard_map/ppermute | solution.py:63
  12.3 4.3 %collective-permute-start.4 = (f32[8,128]{1,0:T(8,128)S(1)}, f32[8,128]{1,0:T(8,128)S(1)}, u32[]{:S(2)}, u32[]{:S(2)}) collective-permute-start(f32[8,128]{1,0:T(8,128)S(1)} %add_add_fusion.1), channel_id=1, source_target_pairs={{0,4},{2,6},{4,0},{6,2},{1,5},{3,7},{5,1},{7,3},{8,12},{10,14},{12... | collective-permute-start | bytes 12296 | tf_op jit(solution)/shard_map/ppermute | solution.py:63
  15.6 2.5 %collective-permute-start.5 = (f32[8,128]{1,0:T(8,128)S(1)}, f32[8,128]{1,0:T(8,128)S(1)}, u32[]{:S(2)}, u32[]{:S(2)}) collective-permute-start(f32[8,128]{1,0:T(8,128)S(1)} %add_add_fusion.1), channel_id=1, source_target_pairs={{0,6},{2,0},{4,2},{6,4},{1,7},{3,1},{5,3},{7,5},{8,14},{10,8},{12,... | collective-permute-start | bytes 12296 | tf_op jit(solution)/shard_map/ppermute | solution.py:63
  18.1 2.5 %collective-permute-start.6 = (f32[8,128]{1,0:T(8,128)S(1)}, f32[8,128]{1,0:T(8,128)S(1)}, u32[]{:S(2)}, u32[]{:S(2)}) collective-permute-start(f32[8,128]{1,0:T(8,128)S(1)} %add_add_fusion), channel_id=1, source_target_pairs={{0,16},{16,0},{1,17},{17,1},{2,18},{18,2},{3,19},{19,3},{4,20},{20... | collective-permute-start | bytes 12296 | tf_op jit(solution)/shard_map/ppermute | solution.py:66
  20.5 3.7 %collective-permute-start.7 = (f32[8,128]{1,0:T(8,128)S(1)}, f32[8,128]{1,0:T(8,128)S(1)}, u32[]{:S(2)}, u32[]{:S(2)}) collective-permute-start(f32[8,128]{1,0:T(8,128)S(1)} %add.45), channel_id=1, source_target_pairs={{16,1},{1,16},{17,0},{0,17},{18,3},{3,18},{19,2},{2,19},{20,5},{5,... | collective-permute-start | bytes 12296 | tf_op jit(solution)/shard_map/ppermute | solution.py:66
  24.3 6.9 %collective-permute-start.8 = (f32[8,128]{1,0:T(8,128)S(1)}, f32[8,128]{1,0:T(8,128)S(1)}, u32[]{:S(2)}, u32[]{:S(2)}) collective-permute-start(f32[8,128]{1,0:T(8,128)S(1)} %add.46), channel_id=1, source_target_pairs={{0,8},{8,0},{1,9},{9,1},{2,10},{10,2},{3,11},{11,3},{4,12},{12,4},... | collective-permute-start | bytes 12296 | tf_op jit(solution)/shard_map/ppermute | solution.py:67
  36.4 8.1 %collective-permute-start.10 = (bf16[49,16,128]{2,1,0:T(8,128)(2,1)}, bf16[49,16,128]{2,1,0:T(8,128)(2,1)S(1)}, u32[]{:S(2)}, u32[]{:S(2)}) collective-permute-start(bf16[49,16,128]{2,1,0:T(8,128)(2,1)} %get-tuple-element.67), channel_id=1, source_target_pairs={{0,4},{2,6},{4,0},{6,2},{1,5},{3,7},{5,1},{7,3},{8,12},{10,14},{12... | collective-permute-start | bytes 602120 | tf_op jit(solution)/shard_map/ppermute | solution.py:398
  37.8 3.4 %collective-permute-start.12 = (bf16[17,16,128]{2,1,0:T(8,128)(2,1)}, bf16[17,16,128]{2,1,0:T(8,128)(2,1)S(1)}, u32[]{:S(2)}, u32[]{:S(2)}) collective-permute-start(bf16[17,16,128]{2,1,0:T(8,128)(2,1)} %get-tuple-element.74.refs_0_), channel_id=1, source_target_pairs={{0,16},{16,0},{1,17},{17,1},{2,18},{18,2},{3,19},{19,3},{4,20},{20... | collective-permute-start | bytes 208904 | tf_op jit(solution)/shard_map/ppermute | solution.py:371
  37.9 10.4 %collective-permute-start.11 = (bf16[49,16,128]{2,1,0:T(8,128)(2,1)}, bf16[49,16,128]{2,1,0:T(8,128)(2,1)S(1)}, u32[]{:S(2)}, u32[]{:S(2)}) collective-permute-start(bf16[49,16,128]{2,1,0:T(8,128)(2,1)} %get-tuple-element.68), channel_id=1, source_target_pairs={{0,6},{2,0},{4,2},{6,4},{1,7},{3,1},{5,3},{7,5},{8,14},{10,8},{12,... | collective-permute-start | bytes 602120 | tf_op jit(solution)/shard_map/ppermute | solution.py:398
  38.6 10.8 %collective-permute-start.9 = (bf16[49,16,128]{2,1,0:T(8,128)(2,1)}, bf16[49,16,128]{2,1,0:T(8,128)(2,1)S(1)}, u32[]{:S(2)}, u32[]{:S(2)}) collective-permute-start(bf16[49,16,128]{2,1,0:T(8,128)(2,1)} %get-tuple-element.66), channel_id=1, source_target_pairs={{0,2},{2,4},{4,6},{6,0},{1,3},{3,5},{5,7},{7,1},{8,10},{10,12},{12... | collective-permute-start | bytes 602120 | tf_op jit(solution)/shard_map/ppermute | solution.py:398
  42.1 7.4 %collective-permute-start.13 = (bf16[2,17,16,128]{3,2,1,0:T(8,128)(2,1)S(1)}, bf16[2,17,16,128]{3,2,1,0:T(8,128)(2,1)S(1)}, u32[]{:S(2)}, u32[]{:S(2)}) collective-permute-start(bf16[2,17,16,128]{3,2,1,0:T(8,128)(2,1)S(1)} %pad_maximum_fusion), channel_id=1, source_target_pairs={{0,32},{8,104},{32,64},{40,8},{64,96},{72,40},{96,0},{104,72},{1,3... | collective-permute-start | bytes 417800 | tf_op jit(solution)/shard_map/ppermute | solution.py:377
  44.5 6.5 %collective-permute-start.14 = (bf16[2,17,16,128]{3,2,1,0:T(8,128)(2,1)S(1)}, bf16[2,17,16,128]{3,2,1,0:T(8,128)(2,1)S(1)}, u32[]{:S(2)}, u32[]{:S(2)}) collective-permute-start(bf16[2,17,16,128]{3,2,1,0:T(8,128)(2,1)S(1)} %pad_maximum_fusion), channel_id=1, source_target_pairs={{0,64},{8,72},{32,96},{40,104},{64,0},{72,8},{96,32},{104,40},{1,6... | collective-permute-start | bytes 417800 | tf_op jit(solution)/shard_map/ppermute | solution.py:377
  44.5 9.0 %collective-permute-start.15 = (bf16[2,17,16,128]{3,2,1,0:T(8,128)(2,1)S(1)}, bf16[2,17,16,128]{3,2,1,0:T(8,128)(2,1)S(1)}, u32[]{:S(2)}, u32[]{:S(2)}) collective-permute-start(bf16[2,17,16,128]{3,2,1,0:T(8,128)(2,1)S(1)} %pad_maximum_fusion), channel_id=1, source_target_pairs={{0,96},{8,40},{32,0},{40,72},{64,32},{72,104},{96,64},{104,8},{1,9... | collective-permute-start | bytes 417800 | tf_op jit(solution)/shard_map/ppermute | solution.py:377
  53.5 0.9 copy-start.1
  54.5 17.6 %collective-permute-start.16 = (bf16[193,16,128]{2,1,0:T(8,128)(2,1)S(1)}, bf16[193,16,128]{2,1,0:T(8,128)(2,1)S(1)}, u32[]{:S(2)}, u32[]{:S(2)}) collective-permute-start(bf16[193,16,128]{2,1,0:T(8,128)(2,1)S(1)} %join.1.refs_0_), channel_id=1, source_target_pairs={{0,16},{16,0},{1,17},{17,1},{2,18},{18,2},{3,19},{19,3},{4,20},{20... | collective-permute-start | bytes 2371592 | tf_op jit(solution)/shard_map/ppermute | solution.py:371
  54.6 17.4 %collective-permute-start.17 = (bf16[193,16,128]{2,1,0:T(8,128)(2,1)S(1)}, bf16[193,16,128]{2,1,0:T(8,128)(2,1)S(1)}, u32[]{:S(2)}, u32[]{:S(2)}) collective-permute-start(bf16[193,16,128]{2,1,0:T(8,128)(2,1)S(1)} %join.1.refs_0_), channel_id=1, source_target_pairs={{0,32},{8,104},{32,64},{40,8},{64,96},{72,40},{96,0},{104,72},{1,3... | collective-permute-start | bytes 2371592 | tf_op jit(solution)/shard_map/ppermute | solution.py:377
  55.8 19.6 %collective-permute-start.18 = (bf16[193,16,128]{2,1,0:T(8,128)(2,1)S(1)}, bf16[193,16,128]{2,1,0:T(8,128)(2,1)S(1)}, u32[]{:S(2)}, u32[]{:S(2)}) collective-permute-start(bf16[193,16,128]{2,1,0:T(8,128)(2,1)S(1)} %join.1.refs_0_), channel_id=1, source_target_pairs={{0,96},{8,40},{32,0},{40,72},{64,32},{72,104},{96,64},{104,8},{1,9... | collective-permute-start | bytes 2371592 | tf_op jit(solution)/shard_map/ppermute | solution.py:377
  56.1 0.9 copy-start
  57.0 8.4 %collective-permute-start.19 = (bf16[129,16,128]{2,1,0:T(8,128)(2,1)S(1)}, bf16[129,16,128]{2,1,0:T(8,128)(2,1)S(1)}, u32[]{:S(2)}, u32[]{:S(2)}) collective-permute-start(bf16[129,16,128]{2,1,0:T(8,128)(2,1)S(1)} %join_kv.1.refs_4_), channel_id=1, source_target_pairs={{0,2},{2,4},{4,6},{6,0},{8,14},{10,8},{12,10},{14,12},{1,3},{3,5},... | collective-permute-start | bytes 1585160 | tf_op jit(solution)/shard_map/ppermute | solution.py:383
  58.4 12.4 %collective-permute-start.20 = (bf16[129,16,128]{2,1,0:T(8,128)(2,1)S(1)}, bf16[129,16,128]{2,1,0:T(8,128)(2,1)S(1)}, u32[]{:S(2)}, u32[]{:S(2)}) collective-permute-start(bf16[129,16,128]{2,1,0:T(8,128)(2,1)S(1)} %join_kv.1.refs_4_), channel_id=1, source_target_pairs={{0,6},{2,0},{4,2},{6,4},{8,10},{10,12},{12,14},{14,8},{1,7},{3,1},... | collective-permute-start | bytes 1585160 | tf_op jit(solution)/shard_map/ppermute | solution.py:383
  75.4 22.5 %collective-permute-start.25 = (bf16[193,16,128]{2,1,0:T(8,128)(2,1)S(1)}, bf16[193,16,128]{2,1,0:T(8,128)(2,1)S(1)}, u32[]{:S(2)}, u32[]{:S(2)}) collective-permute-start(bf16[193,16,128]{2,1,0:T(8,128)(2,1)S(1)} %collective-permute-done.17.refs_1_), channel_id=1, source_target_pairs={{0,32},{8,104},{32,64},{40,8},{64,96},{72,40},{96,0},{104,72},{1,3... | collective-permute-start | bytes 2371592 | tf_op jit(solution)/shard_map/ppermute | solution.py:377
  76.3 21.6 %collective-permute-start.21 = (bf16[129,16,128]{2,1,0:T(8,128)(2,1)S(1)}, bf16[129,16,128]{2,1,0:T(8,128)(2,1)S(1)}, u32[]{:S(2)}, u32[]{:S(2)}) collective-permute-start(bf16[129,16,128]{2,1,0:T(8,128)(2,1)S(1)} %slice.18), channel_id=1, source_target_pairs={{0,32},{8,104},{32,64},{40,8},{64,96},{72,40},{96,0},{104,72},{1,3... | collective-permute-start | bytes 1585160 | tf_op jit(solution)/shard_map/ppermute | solution.py:377
  76.4 21.5 %collective-permute-start.22 = (bf16[129,16,128]{2,1,0:T(8,128)(2,1)S(1)}, bf16[129,16,128]{2,1,0:T(8,128)(2,1)S(1)}, u32[]{:S(2)}, u32[]{:S(2)}) collective-permute-start(bf16[129,16,128]{2,1,0:T(8,128)(2,1)S(1)} %slice.18), channel_id=1, source_target_pairs={{0,96},{8,40},{32,0},{40,72},{64,32},{72,104},{96,64},{104,8},{1,9... | collective-permute-start | bytes 1585160 | tf_op jit(solution)/shard_map/ppermute | solution.py:377
  77.9 5.6 %collective-permute-start.23 = (bf16[64,16,128]{2,1,0:T(8,128)(2,1)S(1)}, bf16[64,16,128]{2,1,0:T(8,128)(2,1)S(1)}, u32[]{:S(2)}, u32[]{:S(2)}) collective-permute-start(bf16[64,16,128]{2,1,0:T(8,128)(2,1)S(1)} %slice.19), channel_id=1, source_target_pairs={{0,16},{16,0},{1,17},{17,1},{2,18},{18,2},{3,19},{19,3},{4,20},{20... | collective-permute-start | bytes 786440 | tf_op jit(solution)/shard_map/ppermute | solution.py:371
  78.5 10.2 %collective-permute-start.24 = (bf16[64,16,128]{2,1,0:T(8,128)(2,1)S(1)}, bf16[64,16,128]{2,1,0:T(8,128)(2,1)S(1)}, u32[]{:S(2)}, u32[]{:S(2)}) collective-permute-start(bf16[64,16,128]{2,1,0:T(8,128)(2,1)S(1)} %slice.20), channel_id=1, source_target_pairs={{0,16},{16,0},{1,17},{17,1},{2,18},{18,2},{3,19},{19,3},{4,20},{20... | collective-permute-start | bytes 786440 | tf_op jit(solution)/shard_map/ppermute | solution.py:371
  97.9 12.2 %collective-permute-start.29 = (bf16[1159,16,128]{2,1,0:T(8,128)(2,1)S(1)}, bf16[1159,16,128]{2,1,0:T(8,128)(2,1)S(1)}, u32[]{:S(2)}, u32[]{:S(2)}) collective-permute-start(bf16[1159,16,128]{2,1,0:T(8,128)(2,1)S(1)} %get-tuple-element.90), channel_id=1, source_target_pairs={{0,8},{8,0},{1,9},{9,1},{2,10},{10,2},{3,11},{11,3},{4,12},{12,4},... | collective-permute-start | bytes 14241800 | tf_op jit(solution)/shard_map/ppermute | solution.py:367
  100.6 9.5 %collective-permute-start.30 = (bf16[193,16,128]{2,1,0:T(8,128)(2,1)S(1)}, bf16[193,16,128]{2,1,0:T(8,128)(2,1)S(1)}, u32[]{:S(2)}, u32[]{:S(2)}) collective-permute-start(bf16[193,16,128]{2,1,0:T(8,128)(2,1)S(1)} %collective-permute-done.25.refs_4_), channel_id=1, source_target_pairs={{0,8},{8,0},{1,9},{9,1},{2,10},{10,2},{3,11},{11,3},{4,12},{12,4},... | collective-permute-start | bytes 2371592 | tf_op jit(solution)/shard_map/ppermute | solution.py:367
  100.7 8.4 %collective-permute-start.28 = (bf16[129,16,128]{2,1,0:T(8,128)(2,1)S(1)}, bf16[129,16,128]{2,1,0:T(8,128)(2,1)S(1)}, u32[]{:S(2)}, u32[]{:S(2)}) collective-permute-start(bf16[129,16,128]{2,1,0:T(8,128)(2,1)S(1)} %collective-permute-done.19.refs_5_), channel_id=1, source_target_pairs={{0,2},{2,4},{4,6},{6,0},{8,14},{10,8},{12,10},{14,12},{1,3},{3,5},... | collective-permute-start | bytes 1585160 | tf_op jit(solution)/shard_map/ppermute | solution.py:383
  101.7 8.4 %collective-permute-start.26 = (bf16[129,16,128]{2,1,0:T(8,128)(2,1)S(1)}, bf16[129,16,128]{2,1,0:T(8,128)(2,1)S(1)}, u32[]{:S(2)}, u32[]{:S(2)}) collective-permute-start(bf16[129,16,128]{2,1,0:T(8,128)(2,1)S(1)} %collective-permute-done.21.refs_0_), channel_id=1, source_target_pairs={{0,32},{8,104},{32,64},{40,8},{64,96},{72,40},{96,0},{104,72},{1,3... | collective-permute-start | bytes 1585160 | tf_op jit(solution)/shard_map/ppermute | solution.py:377
  102.1 7.8 %collective-permute-start.27 = (bf16[64,16,128]{2,1,0:T(8,128)(2,1)S(1)}, bf16[64,16,128]{2,1,0:T(8,128)(2,1)S(1)}, u32[]{:S(2)}, u32[]{:S(2)}) collective-permute-start(bf16[64,16,128]{2,1,0:T(8,128)(2,1)S(1)} %slice.21), channel_id=1, source_target_pairs={{0,16},{16,0},{1,17},{17,1},{2,18},{18,2},{3,19},{19,3},{4,20},{20... | collective-permute-start | bytes 786440 | tf_op jit(solution)/shard_map/ppermute | solution.py:371
  110.1 6.2 %collective-permute-start.34 = (bf16[386,16,128]{2,1,0:T(8,128)(2,1)S(1)}, bf16[386,16,128]{2,1,0:T(8,128)(2,1)S(1)}, u32[]{:S(2)}, u32[]{:S(2)}) collective-permute-start(bf16[386,16,128]{2,1,0:T(8,128)(2,1)S(1)} %get-tuple-element.104), channel_id=1, source_target_pairs={{0,8},{8,0},{1,9},{9,1},{2,10},{10,2},{3,11},{11,3},{4,12},{12,4},... | collective-permute-start | bytes 4743176 | tf_op jit(solution)/shard_map/ppermute | solution.py:367
  112.5 5.0 %collective-permute-start.31 = (bf16[129,16,128]{2,1,0:T(8,128)(2,1)S(1)}, bf16[129,16,128]{2,1,0:T(8,128)(2,1)S(1)}, u32[]{:S(2)}, u32[]{:S(2)}) collective-permute-start(bf16[129,16,128]{2,1,0:T(8,128)(2,1)S(1)} %collective-permute-done.26.refs_0_), channel_id=1, source_target_pairs={{0,8},{8,0},{1,9},{9,1},{2,10},{10,2},{3,11},{11,3},{4,12},{12,4},... | collective-permute-start | bytes 1585160 | tf_op jit(solution)/shard_map/ppermute | solution.py:367
  112.6 4.9 %collective-permute-start.33 = (bf16[129,16,128]{2,1,0:T(8,128)(2,1)S(1)}, bf16[129,16,128]{2,1,0:T(8,128)(2,1)S(1)}, u32[]{:S(2)}, u32[]{:S(2)}) collective-permute-start(bf16[129,16,128]{2,1,0:T(8,128)(2,1)S(1)} %collective-permute-done.28.refs_2_), channel_id=1, source_target_pairs={{0,8},{8,0},{1,9},{9,1},{2,10},{10,2},{3,11},{11,3},{4,12},{12,4},... | collective-permute-start | bytes 1585160 | tf_op jit(solution)/shard_map/ppermute | solution.py:367
  113.0 4.5 %collective-permute-start.32 = (bf16[64,16,128]{2,1,0:T(8,128)(2,1)S(1)}, bf16[64,16,128]{2,1,0:T(8,128)(2,1)S(1)}, u32[]{:S(2)}, u32[]{:S(2)}) collective-permute-start(bf16[64,16,128]{2,1,0:T(8,128)(2,1)S(1)} %collective-permute-done.27.refs_1_), channel_id=1, source_target_pairs={{0,8},{8,0},{1,9},{9,1},{2,10},{10,2},{3,11},{11,3},{4,12},{12,4},... | collective-permute-start | bytes 786440 | tf_op jit(solution)/shard_map/ppermute | solution.py:367

commit v6 on v5

--- a/solution.py
+++ b/solution.py
@@ -28,7 +28,7 @@
 SLOT_T = 24
 PART_T = 1 + 2 * SLOT_T
 FULL_T = 1 + 8 * SLOT_T
-A_T = 129
+A_T = 113
 KV_T = 8
 PLANE_T = 2 * 8 * KV_T + 1
 
@@ -59,8 +59,8 @@
 
 
 def sum_over_devices(v):
-    for axis in ("x", "z"):
-        others = [lax.ppermute(v, axis, ring(4, k)) for k in (1, 2, 3)]
+    for along in (along_x, along_z):
+        others = [along(v, k) for k in (1, 2, 3)]
         v = v + others[0] + others[1] + others[2]
     for pairs in ([(0, 2), (2, 0), (1, 3), (3, 1)], [(2, 1), (1, 2), (3, 0), (0, 3)]):
         v = v + lax.ppermute(v, ("yl", "yh"), pairs)
@@ -149,7 +149,7 @@
         for k in range(4):
             scales = jnp.zeros((TILE, LANES), jnp.float32)
             for h in range(SLOTS):
-                chosen, occupied = slot_of(owners, lax.rem(shard + k, 4), h)
+                chosen, occupied = slot_of(owners, lax.rem(shard + steps_of(place, k), 4), h)
                 picked = values[chosen]
                 at = 1 + h * SLOT_T
                 parts[k][at : at + SLOT_T] = jnp.where(
@@ -184,13 +184,18 @@
     )(place, owner, total, *kv, *exp)
 
 
+def steps_of(place, k):
+    core = lax.rem(lax.div(place, 4), 2)
+    return jnp.where(core == 0, k, (4 - k) % 4)
+
+
 def join(place, parts):
     def kernel(place_ref, *refs):
         out = refs[4]
         shard = lax.rem(place_ref[0], 4)
         tile = jnp.zeros((TILE, LANES), jnp.float32)
         for k in range(4):
-            z = lax.rem(shard - k + 4, 4)
+            z = lax.rem(shard - steps_of(place_ref[0], k) + 4, 4)
             tile += refs[k][0].astype(jnp.float32)
             for h in range(SLOTS):
                 got = refs[k][1 + h * SLOT_T : 1 + (h + 1) * SLOT_T]
@@ -395,7 +400,7 @@
         (kv_param, kv_grad, kv_mean, kv_square),
         (exp_param, exp_grad, exp_mean, exp_square),
     )
-    parts = [parts[0]] + [lax.ppermute(parts[k], "z", ring(4, k)) for k in (1, 2, 3)]
+    parts = [parts[0]] + [along_z(parts[k], k) for k in (1, 2, 3)]
     kv_across = swap_y(kv_part)
     kv_two = jnp.stack([kv_part, kv_across])
     kv_far = [along_x(kv_two, k) for k in (1, 2, 3)]
@@ -427,8 +432,8 @@
     got2 = swap_core(pack2)
     got3 = [(swap_core(v), [p]) for v, p in zip(own, held3)]
     outs = lay(place, list(zip(own, held3)), [(got1, held1), (got_p2, held_p2)], outs)
-    outs = lay(place, [], [(got2, held2)], outs)
-    exp_rollout, kv_rollout, exp_scales, kv_scales = lay(place, [], got3, outs, last=True)
+    got = [(got2, held2)] + got3
+    exp_rollout, kv_rollout, exp_scales, kv_scales = lay(place, [], got, outs, last=True)
     return (
         kv_new,
         exp_new,

time: 120 us -> 118 us (0.983)
  starting transfers between devices: 42.5 us -> 38.3 us
  waiting for transfers between devices: 54.7 us -> 57.3 us
    ppermute x9 -> x0, starting transfers between devices: 14.2 us -> none  [the longest x6 11.3 us: sum_over_devices(): others = [lax.ppermute(v, axis, ring(4, k)) for k in (1, 2, 3)]]
    ppermute x3 -> x9, starting transfers between devices: 2.55 us -> 10.9 us  [along_z(): return lax.ppermute(v, ('c', 'z'), pairs)]
    ppermute x9 -> x0, waiting for transfers between devices: 7.78 us -> none  [the longest x3 4.24 us: per_device(): lax.ppermute(parts[k], 'z', ring(4, k))]
    ppermute x3 -> x9, waiting for transfers between devices: 16.9 us -> 22.8 us  [along_z(): return lax.ppermute(v, ('c', 'z'), pairs)]
    ppermute x9 -> x12, starting transfers between devices: 7.44 us -> 10.6 us  [along_x(): return lax.ppermute(v, ('x', 'c'), pairs)]
    ppermute x5, waiting for transfers between devices: 10.4 us -> 12.3 us  [swap_y(): return lax.ppermute(v, 'yl', ring(2, 1))]
    ppermute x6, starting transfers between devices: 5.82 us -> 4.36 us  [swap_core(): return lax.ppermute(v, 'c', ring(2, 1))]
    ppermute x9 -> x12, waiting for transfers between devices: 16.6 us -> 17.9 us  [along_x(): return lax.ppermute(v, ('x', 'c'), pairs)]
  transfers between devices with their start and end apart: 35 -> 35, of which waited for: 22 -> 21; matrix products, arithmetic and copies ran while one was open for 1% -> 1% of each run, Pallas kernels for 7% -> 7%
where the time goes in v6:
time: 118 us
  waiting for transfers between devices  57.3 us (49%)
  starting transfers between devices  38.3 us (32%)
  Pallas kernels  17.3 us (15%)
  other arithmetic  2.19 us (2%)
  local copies, waits for them, and re-layouts  1.91 us (2%)
    ppermute x9, waiting for transfers between devices, along_z(): return lax.ppermute(v, ('c', 'z'), pairs)  22.8 us
    ppermute x12, waiting for transfers between devices, along_x(): return lax.ppermute(v, ('x', 'c'), pairs)  17.9 us
    ppermute x5, waiting for transfers between devices, swap_y(): return lax.ppermute(v, 'yl', ring(2, 1))  12.3 us
    ppermute x9, starting transfers between devices, along_z(): return lax.ppermute(v, ('c', 'z'), pairs)  10.9 us
    ppermute x12, starting transfers between devices, along_x(): return lax.ppermute(v, ('x', 'c'), pairs)  10.6 us
    pallas_call x4, Pallas kernels, lay(): pl.pallas_call(kernel, out_shape=tuple(out_shape), in_specs=[pl.BlockSpec...  10.6 us
    ppermute x1, starting transfers between devices, sum_over_devices(): v = v + lax.ppermute(v, 'c', ring(2, 1))  5.1 us
    pallas_call x1, Pallas kernels, update(): pl.pallas_call(kernel, out_shape=(jax.ShapeDtypeStruct((2, 1, BLK, BLK),...  4.71 us
  transfers between devices with their start and end apart: 35, of which 21 were waited for; matrix products, arithmetic and copies ran while one was open for 1% of the time, Pallas kernels for 7%

profile of v6, /device:TPU:1, one launch (start us, length us, event | category | flops | bytes accessed | tf_op | source)
XLA Modules:
  0.0 117.7 jit_solution(955171160894675386)
XLA Ops:
  0.6 1.9 %sum_of_squares.1 = f32[8,128]{1,0:T(8,128)} custom-call(f32[2,1,128,128]{3,2,1,0:T(8,128)} %refs_1_.1, f32[4,1,3,128,128]{4,3,2,1,0:T(8,128)} %refs_5_.1), custom_call_target="tpu_custom_call" | custom-call | tf_op jit(solution)/shard_map/sum_of_squares/pallas_call | solution.py:52
  2.5 3.3 %collective-permute-start = (f32[8,128]{1,0:T(8,128)}, f32[8,128]{1,0:T(8,128)S(1)}, u32[]{:S(2)}, u32[]{:S(2)}) collective-permute-start(f32[8,128]{1,0:T(8,128)} %sum_of_squares.1), channel_id=1, source_target_pairs={{0,32},{8,104},{32,64},{40,8},{64,96},{72,40},{96,0},{104,72},{1,3... | collective-permute-start | bytes 12296 | tf_op jit(solution)/shard_map/ppermute | solution.py:382
  5.8 0.5 collective-permute-start.1
  6.3 0.6 collective-permute-start.2
  6.9 3.0 %collective-permute-done.1 = f32[8,128]{1,0:T(8,128)S(1)} collective-permute-done((f32[8,128]{1,0:T(8,128)}, f32[8,128]{1,0:T(8,128)S(1)}, u32[]{:S(2)}, u32[]{:S(2)}) %collective-permute-start.1) | collective-permute-done | bytes 4128 | tf_op jit(solution)/shard_map/ppermute | solution.py:382
  10.0 0.4 collective-permute-done.2
  10.4 0.7 add_add_fusion.1
  11.1 3.8 %collective-permute-start.3 = (f32[8,128]{1,0:T(8,128)S(1)}, f32[8,128]{1,0:T(8,128)S(1)}, u32[]{:S(2)}, u32[]{:S(2)}) collective-permute-start(f32[8,128]{1,0:T(8,128)S(1)} %add_add_fusion.1), channel_id=1, source_target_pairs={{0,2},{2,4},{4,6},{6,0},{8,14},{10,8},{12,10},{14,12},{1,3},{3,5},... | collective-permute-start | bytes 12296 | tf_op jit(solution)/shard_map/ppermute | solution.py:388
  14.9 0.7 collective-permute-start.5
  15.6 0.1 collective-permute-done.3
  15.6 3.2 %collective-permute-done.4 = f32[8,128]{1,0:T(8,128)S(1)} collective-permute-done((f32[8,128]{1,0:T(8,128)S(1)}, f32[8,128]{1,0:T(8,128)S(1)}, u32[]{:S(2)}, u32[]{:S(2)}) %collective-permute-start.4) | collective-permute-done | bytes 4128 | tf_op jit(solution)/shard_map/ppermute | solution.py:388
  18.8 0.0 collective-permute-done.5
  18.9 1.4 %collective-permute-start.6 = (f32[8,128]{1,0:T(8,128)S(1)}, f32[8,128]{1,0:T(8,128)S(1)}, u32[]{:S(2)}, u32[]{:S(2)}) collective-permute-start(f32[8,128]{1,0:T(8,128)S(1)} %add_add_fusion), channel_id=1, source_target_pairs={{0,16},{16,0},{1,17},{17,1},{2,18},{18,2},{3,19},{19,3},{4,20},{20... | collective-permute-start | bytes 12296 | tf_op jit(solution)/shard_map/ppermute | solution.py:66
  20.2 1.2 %collective-permute-done.6 = f32[8,128]{1,0:T(8,128)S(1)} collective-permute-done((f32[8,128]{1,0:T(8,128)S(1)}, f32[8,128]{1,0:T(8,128)S(1)}, u32[]{:S(2)}, u32[]{:S(2)}) %collective-permute-start.6) | collective-permute-done | bytes 4128 | tf_op jit(solution)/shard_map/ppermute | solution.py:66
  21.5 2.7 %collective-permute-start.7 = (f32[8,128]{1,0:T(8,128)S(1)}, f32[8,128]{1,0:T(8,128)S(1)}, u32[]{:S(2)}, u32[]{:S(2)}) collective-permute-start(f32[8,128]{1,0:T(8,128)S(1)} %add.45), channel_id=1, source_target_pairs={{16,1},{1,16},{17,0},{0,17},{18,3},{3,18},{19,2},{2,19},{20,5},{5,... | collective-permute-start | bytes 12296 | tf_op jit(solution)/shard_map/ppermute | solution.py:66
  24.2 1.0 collective-permute-done.7
  25.2 5.1 %collective-permute-start.8 = (f32[8,128]{1,0:T(8,128)S(1)}, f32[8,128]{1,0:T(8,128)S(1)}, u32[]{:S(2)}, u32[]{:S(2)}) collective-permute-start(f32[8,128]{1,0:T(8,128)S(1)} %add.46), channel_id=1, source_target_pairs={{0,8},{8,0},{1,9},{9,1},{2,10},{10,2},{3,11},{11,3},{4,12},{12,4},... | collective-permute-start | bytes 12296 | tf_op jit(solution)/shard_map/ppermute | solution.py:67
  30.3 0.8 collective-permute-done.8
  31.1 0.6 add.47.total_ref
  31.7 4.7 %update.1 = (f32[2,1,128,128]{3,2,1,0:T(8,128)}, f32[4,1,3,128,128]{4,3,2,1,0:T(8,128)}, bf16[49,16,128]{2,1,0:T(8,128)(2,1)}, bf16[49,16,128]{2,1,0:T(8,128)(2,...) custom-call(s32[1]{0:T(128)} %bitcast.place_ref, s32[4]{0:T(128)} %owner_ref.1, ...), custom_call_target="tpu_custom_call" | custom-call | tf_op jit(solution)/shard_map/update/pallas_call | solution.py:163
  36.4 1.4 %collective-permute-start.10 = (bf16[49,16,128]{2,1,0:T(8,128)(2,1)}, bf16[49,16,128]{2,1,0:T(8,128)(2,1)S(1)}, u32[]{:S(2)}, u32[]{:S(2)}) collective-permute-start(bf16[49,16,128]{2,1,0:T(8,128)(2,1)} %get-tuple-element.64), channel_id=1, source_target_pairs={{0,4},{2,6},{4,0},{6,2},{8,12},{10,14},{12,8},{14,10},{1,5},{3,7},... | collective-permute-start | bytes 602120 | tf_op jit(solution)/shard_map/ppermute | solution.py:388
  37.8 0.1 collective-permute-start.12
  37.9 1.2 %collective-permute-start.11 = (bf16[49,16,128]{2,1,0:T(8,128)(2,1)}, bf16[49,16,128]{2,1,0:T(8,128)(2,1)S(1)}, u32[]{:S(2)}, u32[]{:S(2)}) collective-permute-start(bf16[49,16,128]{2,1,0:T(8,128)(2,1)} %get-tuple-element.65), channel_id=1, source_target_pairs={{0,6},{2,0},{4,2},{6,4},{8,10},{10,12},{12,14},{14,8},{1,7},{3,1},... | collective-permute-start | bytes 602120 | tf_op jit(solution)/shard_map/ppermute | solution.py:388
  39.1 1.5 %collective-permute-start.9 = (bf16[49,16,128]{2,1,0:T(8,128)(2,1)}, bf16[49,16,128]{2,1,0:T(8,128)(2,1)S(1)}, u32[]{:S(2)}, u32[]{:S(2)}) collective-permute-start(bf16[49,16,128]{2,1,0:T(8,128)(2,1)} %get-tuple-element.63), channel_id=1, source_target_pairs={{0,2},{2,4},{4,6},{6,0},{8,14},{10,8},{12,10},{14,12},{1,3},{3,5},... | collective-permute-start | bytes 602120 | tf_op jit(solution)/shard_map/ppermute | solution.py:388
  40.6 0.6 collective-permute-done.12.refs_1_
  41.2 0.9 pad_maximum_fusion
  42.1 2.4 %collective-permute-start.13 = (bf16[2,17,16,128]{3,2,1,0:T(8,128)(2,1)S(1)}, bf16[2,17,16,128]{3,2,1,0:T(8,128)(2,1)S(1)}, u32[]{:S(2)}, u32[]{:S(2)}) collective-permute-start(bf16[2,17,16,128]{3,2,1,0:T(8,128)(2,1)S(1)} %pad_maximum_fusion), channel_id=1, source_target_pairs={{0,32},{8,104},{32,64},{40,8},{64,96},{72,40},{96,0},{104,72},{1,3... | collective-permute-start | bytes 417800 | tf_op jit(solution)/shard_map/ppermute | solution.py:382
  44.5 0.7 collective-permute-start.15
  45.2 4.2 %collective-permute-done.11.refs_3_ = bf16[49,16,128]{2,1,0:T(8,128)(2,1)S(1)} collective-permute-done((bf16[49,16,128]{2,1,0:T(8,128)(2,1)}, bf16[49,16,128]{2,1,0:T(8,128)(2,1)S(1)}, u32[]{:S(2)}, u32[]{:S(2)}) %collective-permute-start.11) | collective-permute-done | bytes 200736 | tf_op jit(solution)/shard_map/ppermute | solution.py:388
  49.4 1.6 %collective-permute-done.14.refs_3_ = bf16[2,17,16,128]{3,2,1,0:T(8,128)(2,1)S(1)} collective-permute-done((bf16[2,17,16,128]{3,2,1,0:T(8,128)(2,1)S(1)}, bf16[2,17,16,128]{3,2,1,0:T(8,128)(2,1)S(1)}, u32[]{:S(2)}, u32[]{:S(2)}) %collective-permute-start.14) | collective-permute-done | bytes 139296 | tf_op jit(solution)/shard_map/ppermute | solution.py:382
  51.1 2.4 %collective-permute-done.15.refs_4_ = bf16[2,17,16,128]{3,2,1,0:T(8,128)(2,1)S(1)} collective-permute-done((bf16[2,17,16,128]{3,2,1,0:T(8,128)(2,1)S(1)}, bf16[2,17,16,128]{3,2,1,0:T(8,128)(2,1)S(1)}, u32[]{:S(2)}, u32[]{:S(2)}) %collective-permute-start.15) | collective-permute-done | bytes 139296 | tf_op jit(solution)/shard_map/ppermute | solution.py:382
  53.5 0.9 copy-done.1
  54.4 0.1 join.1.refs_0_
  54.5 0.3 collective-permute-start.16
  54.8 1.5 %collective-permute-start.17 = (bf16[193,16,128]{2,1,0:T(8,128)(2,1)S(1)}, bf16[193,16,128]{2,1,0:T(8,128)(2,1)S(1)}, u32[]{:S(2)}, u32[]{:S(2)}) collective-permute-start(bf16[193,16,128]{2,1,0:T(8,128)(2,1)S(1)} %join.1.refs_0_), channel_id=1, source_target_pairs={{0,32},{8,104},{32,64},{40,8},{64,96},{72,40},{96,0},{104,72},{1,3... | collective-permute-start | bytes 2371592 | tf_op jit(solution)/shard_map/ppermute | solution.py:382
  56.3 0.9 copy-done
  57.2 0.9 collective-permute-start.19
  58.2 0.6 collective-permute-start.20
  58.8 6.9 %collective-permute-done.19.refs_5_ = bf16[129,16,128]{2,1,0:T(8,128)(2,1)S(1)} collective-permute-done((bf16[129,16,128]{2,1,0:T(8,128)(2,1)S(1)}, bf16[129,16,128]{2,1,0:T(8,128)(2,1)S(1)}, u32[]{:S(2)}, u32[]{:S(2)}) %collective-permute-start.19) | collective-permute-done | bytes 528416 | tf_op jit(solution)/shard_map/ppermute | solution.py:388
  65.7 4.4 %collective-permute-done.20.refs_6_ = bf16[129,16,128]{2,1,0:T(8,128)(2,1)S(1)} collective-permute-done((bf16[129,16,128]{2,1,0:T(8,128)(2,1)S(1)}, bf16[129,16,128]{2,1,0:T(8,128)(2,1)S(1)}, u32[]{:S(2)}, u32[]{:S(2)}) %collective-permute-start.20) | collective-permute-done | bytes 528416 | tf_op jit(solution)/shard_map/ppermute | solution.py:388
  70.1 2.0 %collective-permute-done.16.refs_3_ = bf16[193,16,128]{2,1,0:T(8,128)(2,1)S(1)} collective-permute-done((bf16[193,16,128]{2,1,0:T(8,128)(2,1)S(1)}, bf16[193,16,128]{2,1,0:T(8,128)(2,1)S(1)}, u32[]{:S(2)}, u32[]{:S(2)}) %collective-permute-start.16) | collective-permute-done | bytes 790560 | tf_op jit(solution)/shard_map/ppermute | solution.py:376
  72.1 4.2 %collective-permute-done.18.refs_2_ = bf16[193,16,128]{2,1,0:T(8,128)(2,1)S(1)} collective-permute-done((bf16[193,16,128]{2,1,0:T(8,128)(2,1)S(1)}, bf16[193,16,128]{2,1,0:T(8,128)(2,1)S(1)}, u32[]{:S(2)}, u32[]{:S(2)}) %collective-permute-start.18) | collective-permute-done | bytes 790560 | tf_op jit(solution)/shard_map/ppermute | solution.py:382
  76.3 0.1 collective-permute-start.21
  76.4 1.5 %collective-permute-start.22 = (bf16[113,16,128]{2,1,0:T(8,128)(2,1)S(1)}, bf16[113,16,128]{2,1,0:T(8,128)(2,1)S(1)}, u32[]{:S(2)}, u32[]{:S(2)}) collective-permute-start(bf16[113,16,128]{2,1,0:T(8,128)(2,1)S(1)} %slice.18), channel_id=1, source_target_pairs={{0,96},{8,40},{32,0},{40,72},{64,32},{72,104},{96,64},{104,8},{1,9... | collective-permute-start | bytes 1388552 | tf_op jit(solution)/shard_map/ppermute | solution.py:382
  77.9 0.6 collective-permute-start.23
  78.5 1.0 collective-permute-start.24
  79.6 2.8 %lay.4 = (bf16[2,1536,16,128]{3,2,1,0:T(8,128)(2,1)}, bf16[2,8,2,4,8,16,128]{6,5,4,3,2,1,0:T(8,128)(2,1)}, f32[2,16,128]{2,1,0:T(8,128)S(1)}, bf16[1159,16,128]{2,1,0:T(8,128)(2,1)S(1)}) custom-call(s32[1]{0:T(128)} %bitcast.place_ref, bf16[193,16,128]{2,1,0:T(8,128)(2,1)S(1)} %join.1.refs_0_, bf16[193,16,128]{2,1,0:T(8,128)(2,1)S(1)} %collective-permute-done.17.refs_1_, ...), custom_call_target="tpu_custom_call" | custom-call | bytes 11010048 | tf_op jit(solution)/shard_map/lay/pallas_call | solution.py:348
  82.4 1.9 %collective-permute-done.23.refs_2_ = bf16[80,16,128]{2,1,0:T(8,128)(2,1)S(1)} collective-permute-done((bf16[80,16,128]{2,1,0:T(8,128)(2,1)S(1)}, bf16[80,16,128]{2,1,0:T(8,128)(2,1)S(1)}, u32[]{:S(2)}, u32[]{:S(2)}) %collective-permute-start.23) | collective-permute-done | bytes 327712 | tf_op jit(solution)/shard_map/ppermute | solution.py:376
  84.2 6.9 %collective-permute-done.24.refs_3_ = bf16[80,16,128]{2,1,0:T(8,128)(2,1)S(1)} collective-permute-done((bf16[80,16,128]{2,1,0:T(8,128)(2,1)S(1)}, bf16[80,16,128]{2,1,0:T(8,128)(2,1)S(1)}, u32[]{:S(2)}, u32[]{:S(2)}) %collective-permute-start.24) | collective-permute-done | bytes 327712 | tf_op jit(solution)/shard_map/ppermute | solution.py:376
  91.2 6.2 %collective-permute-done.21.refs_0_ = bf16[113,16,128]{2,1,0:T(8,128)(2,1)S(1)} collective-permute-done((bf16[113,16,128]{2,1,0:T(8,128)(2,1)S(1)}, bf16[113,16,128]{2,1,0:T(8,128)(2,1)S(1)}, u32[]{:S(2)}, u32[]{:S(2)}) %collective-permute-start.21) | collective-permute-done | bytes 462880 | tf_op jit(solution)/shard_map/ppermute | solution.py:382
  97.4 1.8 %collective-permute-start.29 = (bf16[1159,16,128]{2,1,0:T(8,128)(2,1)S(1)}, bf16[1159,16,128]{2,1,0:T(8,128)(2,1)S(1)}, u32[]{:S(2)}, u32[]{:S(2)}) collective-permute-start(bf16[1159,16,128]{2,1,0:T(8,128)(2,1)S(1)} %get-tuple-element.87), channel_id=1, source_target_pairs={{0,8},{8,0},{1,9},{9,1},{2,10},{10,2},{3,11},{11,3},{4,12},{12,4},... | collective-permute-start | bytes 14241800 | tf_op jit(solution)/shard_map/ppermute | solution.py:372
  99.2 0.1 collective-permute-start.30
  99.3 0.8 collective-permute-start.28
  100.1 1.2 %collective-permute-start.27 = (bf16[80,16,128]{2,1,0:T(8,128)(2,1)S(1)}, bf16[80,16,128]{2,1,0:T(8,128)(2,1)S(1)}, u32[]{:S(2)}, u32[]{:S(2)}) collective-permute-start(bf16[80,16,128]{2,1,0:T(8,128)(2,1)S(1)} %slice.21), channel_id=1, source_target_pairs={{0,16},{16,0},{1,17},{17,1},{2,18},{18,2},{3,19},{19,3},{4,20},{20... | collective-permute-start | bytes 983048 | tf_op jit(solution)/shard_map/ppermute | solution.py:376
  101.3 2.3 %lay.5 = (bf16[2,1536,16,128]{3,2,1,0:T(8,128)(2,1)}, bf16[2,8,2,4,8,16,128]{6,5,4,3,2,1,0:T(8,128)(2,1)}, f32[2,16,128]{2,1,0:T(8,128)S(1)}, bf16[386,16,128]{2,1,0:T(8,128)(2,1)S(1)}) custom-call(s32[1]{0:T(128)} %bitcast.place_ref, bf16[113,16,128]{2,1,0:T(8,128)(2,1)S(1)} %collective-permute-done.21.refs_0_, ...), custom_call_target="tpu_custom_call", output_to_operand_aliasing={{0}: (6, {}), {1}: (7, {})} | custom-call | bytes 7340032 | tf_op jit(solution)/shard_map/lay/pallas_call | solution.py:348
  103.6 4.0 %collective-permute-done.28.refs_2_ = bf16[129,16,128]{2,1,0:T(8,128)(2,1)S(1)} collective-permute-done((bf16[129,16,128]{2,1,0:T(8,128)(2,1)S(1)}, bf16[129,16,128]{2,1,0:T(8,128)(2,1)S(1)}, u32[]{:S(2)}, u32[]{:S(2)}) %collective-permute-start.28) | collective-permute-done | bytes 528416 | tf_op jit(solution)/shard_map/ppermute | solution.py:388
  107.6 0.9 collective-permute-done.27.refs_1_
  108.6 1.9 %collective-permute-start.31 = (bf16[386,16,128]{2,1,0:T(8,128)(2,1)S(1)}, bf16[386,16,128]{2,1,0:T(8,128)(2,1)S(1)}, u32[]{:S(2)}, u32[]{:S(2)}) collective-permute-start(bf16[386,16,128]{2,1,0:T(8,128)(2,1)S(1)} %get-tuple-element.98), channel_id=1, source_target_pairs={{0,8},{8,0},{1,9},{9,1},{2,10},{10,2},{3,11},{11,3},{4,12},{12,4},... | collective-permute-start | bytes 4743176 | tf_op jit(solution)/shard_map/ppermute | solution.py:372
  110.4 0.1 collective-permute-start.34
  110.5 0.4 collective-permute-start.32
  110.9 0.1 collective-permute-start.33
  111.0 3.1 %lay.6 = (bf16[2,1536,16,128]{3,2,1,0:T(8,128)(2,1)}, bf16[2,8,2,4,8,16,128]{6,5,4,3,2,1,0:T(8,128)(2,1)}, f32[2,16,128]{2,1,0:T(8,128)S(1)}) custom-call(s32[1]{0:T(128)} %bitcast.place_ref, bf16[113,16,128]{2,1,0:T(8,128)(2,1)S(1)} %collective-permute-done.26.refs_0_, ...), custom_call_target="tpu_custom_call", output_to_operand_aliasing={{0}: (6, {}), {1}: (7, {})} | custom-call | bytes 11534336 | tf_op jit(solution)/shard_map/lay/pallas_call | solution.py:348
  114.2 1.2 %collective-permute-done.33.refs_2_ = bf16[80,16,128]{2,1,0:T(8,128)(2,1)S(1)} collective-permute-done((bf16[80,16,128]{2,1,0:T(8,128)(2,1)S(1)}, bf16[80,16,128]{2,1,0:T(8,128)(2,1)S(1)}, u32[]{:S(2)}, u32[]{:S(2)}) %collective-permute-start.33) | collective-permute-done | bytes 327712 | tf_op jit(solution)/shard_map/ppermute | solution.py:372
  115.4 2.3 %lay.7 = (bf16[2,1536,16,128]{3,2,1,0:T(8,128)(2,1)}, bf16[2,8,2,4,8,16,128]{6,5,4,3,2,1,0:T(8,128)(2,1)}, f32[2,2,128]{2,1,0:T(2,128)}, f32[2,128]{1,0:T(2,128)}) custom-call(s32[1]{0:T(128)} %bitcast.place_ref, bf16[386,16,128]{2,1,0:T(8,128)(2,1)S(1)} %collective-permute-done.31.refs_0_, ...), custom_call_target="tpu_custom_call", output_to_operand_aliasing={{0}: (5, {}), {1}: (6, {})} | custom-call | bytes 7340032 | tf_op jit(solution)/shard_map/lay/pallas_call | solution.py:348
  (28 shorter events, 0.2 us)
Async XLA Ops:
  2.5 4.4 %collective-permute-start = (f32[8,128]{1,0:T(8,128)}, f32[8,128]{1,0:T(8,128)S(1)}, u32[]{:S(2)}, u32[]{:S(2)}) collective-permute-start(f32[8,128]{1,0:T(8,128)} %sum_of_squares.1), channel_id=1, source_target_pairs={{0,32},{8,104},{32,64},{40,8},{64,96},{72,40},{96,0},{104,72},{1,3... | collective-permute-start | bytes 12296 | tf_op jit(solution)/shard_map/ppermute | solution.py:382
  5.8 4.2 %collective-permute-start.1 = (f32[8,128]{1,0:T(8,128)}, f32[8,128]{1,0:T(8,128)S(1)}, u32[]{:S(2)}, u32[]{:S(2)}) collective-permute-start(f32[8,128]{1,0:T(8,128)} %sum_of_squares.1), channel_id=1, source_target_pairs={{0,64},{8,72},{32,96},{40,104},{64,0},{72,8},{96,32},{104,40},{1,6... | collective-permute-start | bytes 12296 | tf_op jit(solution)/shard_map/ppermute | solution.py:382
  6.3 4.1 %collective-permute-start.2 = (f32[8,128]{1,0:T(8,128)}, f32[8,128]{1,0:T(8,128)S(1)}, u32[]{:S(2)}, u32[]{:S(2)}) collective-permute-start(f32[8,128]{1,0:T(8,128)} %sum_of_squares.1), channel_id=1, source_target_pairs={{0,96},{8,40},{32,0},{40,72},{64,32},{72,104},{96,64},{104,8},{1,9... | collective-permute-start | bytes 12296 | tf_op jit(solution)/shard_map/ppermute | solution.py:382
  11.1 4.5 %collective-permute-start.3 = (f32[8,128]{1,0:T(8,128)S(1)}, f32[8,128]{1,0:T(8,128)S(1)}, u32[]{:S(2)}, u32[]{:S(2)}) collective-permute-start(f32[8,128]{1,0:T(8,128)S(1)} %add_add_fusion.1), channel_id=1, source_target_pairs={{0,2},{2,4},{4,6},{6,0},{8,14},{10,8},{12,10},{14,12},{1,3},{3,5},... | collective-permute-start | bytes 12296 | tf_op jit(solution)/shard_map/ppermute | solution.py:388
  14.9 4.0 %collective-permute-start.4 = (f32[8,128]{1,0:T(8,128)S(1)}, f32[8,128]{1,0:T(8,128)S(1)}, u32[]{:S(2)}, u32[]{:S(2)}) collective-permute-start(f32[8,128]{1,0:T(8,128)S(1)} %add_add_fusion.1), channel_id=1, source_target_pairs={{0,4},{2,6},{4,0},{6,2},{8,12},{10,14},{12,8},{14,10},{1,5},{3,7},... | collective-permute-start | bytes 12296 | tf_op jit(solution)/shard_map/ppermute | solution.py:388
  14.9 4.0 %collective-permute-start.5 = (f32[8,128]{1,0:T(8,128)S(1)}, f32[8,128]{1,0:T(8,128)S(1)}, u32[]{:S(2)}, u32[]{:S(2)}) collective-permute-start(f32[8,128]{1,0:T(8,128)S(1)} %add_add_fusion.1), channel_id=1, source_target_pairs={{0,6},{2,0},{4,2},{6,4},{8,10},{10,12},{12,14},{14,8},{1,7},{3,1},... | collective-permute-start | bytes 12296 | tf_op jit(solution)/shard_map/ppermute | solution.py:388
  18.9 2.6 %collective-permute-start.6 = (f32[8,128]{1,0:T(8,128)S(1)}, f32[8,128]{1,0:T(8,128)S(1)}, u32[]{:S(2)}, u32[]{:S(2)}) collective-permute-start(f32[8,128]{1,0:T(8,128)S(1)} %add_add_fusion), channel_id=1, source_target_pairs={{0,16},{16,0},{1,17},{17,1},{2,18},{18,2},{3,19},{19,3},{4,20},{20... | collective-permute-start | bytes 12296 | tf_op jit(solution)/shard_map/ppermute | solution.py:66
  21.5 3.7 %collective-permute-start.7 = (f32[8,128]{1,0:T(8,128)S(1)}, f32[8,128]{1,0:T(8,128)S(1)}, u32[]{:S(2)}, u32[]{:S(2)}) collective-permute-start(f32[8,128]{1,0:T(8,128)S(1)} %add.45), channel_id=1, source_target_pairs={{16,1},{1,16},{17,0},{0,17},{18,3},{3,18},{19,2},{2,19},{20,5},{5,... | collective-permute-start | bytes 12296 | tf_op jit(solution)/shard_map/ppermute | solution.py:66
  25.2 5.9 %collective-permute-start.8 = (f32[8,128]{1,0:T(8,128)S(1)}, f32[8,128]{1,0:T(8,128)S(1)}, u32[]{:S(2)}, u32[]{:S(2)}) collective-permute-start(f32[8,128]{1,0:T(8,128)S(1)} %add.46), channel_id=1, source_target_pairs={{0,8},{8,0},{1,9},{9,1},{2,10},{10,2},{3,11},{11,3},{4,12},{12,4},... | collective-permute-start | bytes 12296 | tf_op jit(solution)/shard_map/ppermute | solution.py:67
  36.4 8.1 %collective-permute-start.10 = (bf16[49,16,128]{2,1,0:T(8,128)(2,1)}, bf16[49,16,128]{2,1,0:T(8,128)(2,1)S(1)}, u32[]{:S(2)}, u32[]{:S(2)}) collective-permute-start(bf16[49,16,128]{2,1,0:T(8,128)(2,1)} %get-tuple-element.64), channel_id=1, source_target_pairs={{0,4},{2,6},{4,0},{6,2},{8,12},{10,14},{12,8},{14,10},{1,5},{3,7},... | collective-permute-start | bytes 602120 | tf_op jit(solution)/shard_map/ppermute | solution.py:388
  37.8 3.4 %collective-permute-start.12 = (bf16[17,16,128]{2,1,0:T(8,128)(2,1)}, bf16[17,16,128]{2,1,0:T(8,128)(2,1)S(1)}, u32[]{:S(2)}, u32[]{:S(2)}) collective-permute-start(bf16[17,16,128]{2,1,0:T(8,128)(2,1)} %get-tuple-element.71.refs_0_), channel_id=1, source_target_pairs={{0,16},{16,0},{1,17},{17,1},{2,18},{18,2},{3,19},{19,3},{4,20},{20... | collective-permute-start | bytes 208904 | tf_op jit(solution)/shard_map/ppermute | solution.py:376
  37.9 11.5 %collective-permute-start.11 = (bf16[49,16,128]{2,1,0:T(8,128)(2,1)}, bf16[49,16,128]{2,1,0:T(8,128)(2,1)S(1)}, u32[]{:S(2)}, u32[]{:S(2)}) collective-permute-start(bf16[49,16,128]{2,1,0:T(8,128)(2,1)} %get-tuple-element.65), channel_id=1, source_target_pairs={{0,6},{2,0},{4,2},{6,4},{8,10},{10,12},{12,14},{14,8},{1,7},{3,1},... | collective-permute-start | bytes 602120 | tf_op jit(solution)/shard_map/ppermute | solution.py:388
  39.1 10.3 %collective-permute-start.9 = (bf16[49,16,128]{2,1,0:T(8,128)(2,1)}, bf16[49,16,128]{2,1,0:T(8,128)(2,1)S(1)}, u32[]{:S(2)}, u32[]{:S(2)}) collective-permute-start(bf16[49,16,128]{2,1,0:T(8,128)(2,1)} %get-tuple-element.63), channel_id=1, source_target_pairs={{0,2},{2,4},{4,6},{6,0},{8,14},{10,8},{12,10},{14,12},{1,3},{3,5},... | collective-permute-start | bytes 602120 | tf_op jit(solution)/shard_map/ppermute | solution.py:388
  42.1 7.4 %collective-permute-start.13 = (bf16[2,17,16,128]{3,2,1,0:T(8,128)(2,1)S(1)}, bf16[2,17,16,128]{3,2,1,0:T(8,128)(2,1)S(1)}, u32[]{:S(2)}, u32[]{:S(2)}) collective-permute-start(bf16[2,17,16,128]{3,2,1,0:T(8,128)(2,1)S(1)} %pad_maximum_fusion), channel_id=1, source_target_pairs={{0,32},{8,104},{32,64},{40,8},{64,96},{72,40},{96,0},{104,72},{1,3... | collective-permute-start | bytes 417800 | tf_op jit(solution)/shard_map/ppermute | solution.py:382
  44.5 6.5 %collective-permute-start.14 = (bf16[2,17,16,128]{3,2,1,0:T(8,128)(2,1)S(1)}, bf16[2,17,16,128]{3,2,1,0:T(8,128)(2,1)S(1)}, u32[]{:S(2)}, u32[]{:S(2)}) collective-permute-start(bf16[2,17,16,128]{3,2,1,0:T(8,128)(2,1)S(1)} %pad_maximum_fusion), channel_id=1, source_target_pairs={{0,64},{8,72},{32,96},{40,104},{64,0},{72,8},{96,32},{104,40},{1,6... | collective-permute-start | bytes 417800 | tf_op jit(solution)/shard_map/ppermute | solution.py:382
  44.5 9.0 %collective-permute-start.15 = (bf16[2,17,16,128]{3,2,1,0:T(8,128)(2,1)S(1)}, bf16[2,17,16,128]{3,2,1,0:T(8,128)(2,1)S(1)}, u32[]{:S(2)}, u32[]{:S(2)}) collective-permute-start(bf16[2,17,16,128]{3,2,1,0:T(8,128)(2,1)S(1)} %pad_maximum_fusion), channel_id=1, source_target_pairs={{0,96},{8,40},{32,0},{40,72},{64,32},{72,104},{96,64},{104,8},{1,9... | collective-permute-start | bytes 417800 | tf_op jit(solution)/shard_map/ppermute | solution.py:382
  53.5 0.9 copy-start.1
  54.5 17.6 %collective-permute-start.16 = (bf16[193,16,128]{2,1,0:T(8,128)(2,1)S(1)}, bf16[193,16,128]{2,1,0:T(8,128)(2,1)S(1)}, u32[]{:S(2)}, u32[]{:S(2)}) collective-permute-start(bf16[193,16,128]{2,1,0:T(8,128)(2,1)S(1)} %join.1.refs_0_), channel_id=1, source_target_pairs={{0,16},{16,0},{1,17},{17,1},{2,18},{18,2},{3,19},{19,3},{4,20},{20... | collective-permute-start | bytes 2371592 | tf_op jit(solution)/shard_map/ppermute | solution.py:376
  54.8 17.3 %collective-permute-start.17 = (bf16[193,16,128]{2,1,0:T(8,128)(2,1)S(1)}, bf16[193,16,128]{2,1,0:T(8,128)(2,1)S(1)}, u32[]{:S(2)}, u32[]{:S(2)}) collective-permute-start(bf16[193,16,128]{2,1,0:T(8,128)(2,1)S(1)} %join.1.refs_0_), channel_id=1, source_target_pairs={{0,32},{8,104},{32,64},{40,8},{64,96},{72,40},{96,0},{104,72},{1,3... | collective-permute-start | bytes 2371592 | tf_op jit(solution)/shard_map/ppermute | solution.py:382
  56.3 20.0 %collective-permute-start.18 = (bf16[193,16,128]{2,1,0:T(8,128)(2,1)S(1)}, bf16[193,16,128]{2,1,0:T(8,128)(2,1)S(1)}, u32[]{:S(2)}, u32[]{:S(2)}) collective-permute-start(bf16[193,16,128]{2,1,0:T(8,128)(2,1)S(1)} %join.1.refs_0_), channel_id=1, source_target_pairs={{0,96},{8,40},{32,0},{40,72},{64,32},{72,104},{96,64},{104,8},{1,9... | collective-permute-start | bytes 2371592 | tf_op jit(solution)/shard_map/ppermute | solution.py:382
  56.3 0.9 copy-start
  57.2 8.4 %collective-permute-start.19 = (bf16[129,16,128]{2,1,0:T(8,128)(2,1)S(1)}, bf16[129,16,128]{2,1,0:T(8,128)(2,1)S(1)}, u32[]{:S(2)}, u32[]{:S(2)}) collective-permute-start(bf16[129,16,128]{2,1,0:T(8,128)(2,1)S(1)} %join_kv.1.refs_4_), channel_id=1, source_target_pairs={{0,2},{2,4},{4,6},{6,0},{8,14},{10,8},{12,10},{14,12},{1,3},{3,5},... | collective-permute-start | bytes 1585160 | tf_op jit(solution)/shard_map/ppermute | solution.py:388
  58.2 11.9 %collective-permute-start.20 = (bf16[129,16,128]{2,1,0:T(8,128)(2,1)S(1)}, bf16[129,16,128]{2,1,0:T(8,128)(2,1)S(1)}, u32[]{:S(2)}, u32[]{:S(2)}) collective-permute-start(bf16[129,16,128]{2,1,0:T(8,128)(2,1)S(1)} %join_kv.1.refs_4_), channel_id=1, source_target_pairs={{0,6},{2,0},{4,2},{6,4},{8,10},{10,12},{12,14},{14,8},{1,7},{3,1},... | collective-permute-start | bytes 1585160 | tf_op jit(solution)/shard_map/ppermute | solution.py:388
  76.3 21.1 %collective-permute-start.25 = (bf16[193,16,128]{2,1,0:T(8,128)(2,1)S(1)}, bf16[193,16,128]{2,1,0:T(8,128)(2,1)S(1)}, u32[]{:S(2)}, u32[]{:S(2)}) collective-permute-start(bf16[193,16,128]{2,1,0:T(8,128)(2,1)S(1)} %collective-permute-done.17.refs_1_), channel_id=1, source_target_pairs={{0,32},{8,104},{32,64},{40,8},{64,96},{72,40},{96,0},{104,72},{1,3... | collective-permute-start | bytes 2371592 | tf_op jit(solution)/shard_map/ppermute | solution.py:382
  76.3 21.1 %collective-permute-start.21 = (bf16[113,16,128]{2,1,0:T(8,128)(2,1)S(1)}, bf16[113,16,128]{2,1,0:T(8,128)(2,1)S(1)}, u32[]{:S(2)}, u32[]{:S(2)}) collective-permute-start(bf16[113,16,128]{2,1,0:T(8,128)(2,1)S(1)} %slice.18), channel_id=1, source_target_pairs={{0,32},{8,104},{32,64},{40,8},{64,96},{72,40},{96,0},{104,72},{1,3... | collective-permute-start | bytes 1388552 | tf_op jit(solution)/shard_map/ppermute | solution.py:382
  76.4 21.0 %collective-permute-start.22 = (bf16[113,16,128]{2,1,0:T(8,128)(2,1)S(1)}, bf16[113,16,128]{2,1,0:T(8,128)(2,1)S(1)}, u32[]{:S(2)}, u32[]{:S(2)}) collective-permute-start(bf16[113,16,128]{2,1,0:T(8,128)(2,1)S(1)} %slice.18), channel_id=1, source_target_pairs={{0,96},{8,40},{32,0},{40,72},{64,32},{72,104},{96,64},{104,8},{1,9... | collective-permute-start | bytes 1388552 | tf_op jit(solution)/shard_map/ppermute | solution.py:382
  77.9 6.3 %collective-permute-start.23 = (bf16[80,16,128]{2,1,0:T(8,128)(2,1)S(1)}, bf16[80,16,128]{2,1,0:T(8,128)(2,1)S(1)}, u32[]{:S(2)}, u32[]{:S(2)}) collective-permute-start(bf16[80,16,128]{2,1,0:T(8,128)(2,1)S(1)} %slice.19), channel_id=1, source_target_pairs={{0,16},{16,0},{1,17},{17,1},{2,18},{18,2},{3,19},{19,3},{4,20},{20... | collective-permute-start | bytes 983048 | tf_op jit(solution)/shard_map/ppermute | solution.py:376
  78.5 12.6 %collective-permute-start.24 = (bf16[80,16,128]{2,1,0:T(8,128)(2,1)S(1)}, bf16[80,16,128]{2,1,0:T(8,128)(2,1)S(1)}, u32[]{:S(2)}, u32[]{:S(2)}) collective-permute-start(bf16[80,16,128]{2,1,0:T(8,128)(2,1)S(1)} %slice.20), channel_id=1, source_target_pairs={{0,16},{16,0},{1,17},{17,1},{2,18},{18,2},{3,19},{19,3},{4,20},{20... | collective-permute-start | bytes 983048 | tf_op jit(solution)/shard_map/ppermute | solution.py:376
  97.4 11.2 %collective-permute-start.29 = (bf16[1159,16,128]{2,1,0:T(8,128)(2,1)S(1)}, bf16[1159,16,128]{2,1,0:T(8,128)(2,1)S(1)}, u32[]{:S(2)}, u32[]{:S(2)}) collective-permute-start(bf16[1159,16,128]{2,1,0:T(8,128)(2,1)S(1)} %get-tuple-element.87), channel_id=1, source_target_pairs={{0,8},{8,0},{1,9},{9,1},{2,10},{10,2},{3,11},{11,3},{4,12},{12,4},... | collective-permute-start | bytes 14241800 | tf_op jit(solution)/shard_map/ppermute | solution.py:372
  99.2 9.4 %collective-permute-start.30 = (bf16[193,16,128]{2,1,0:T(8,128)(2,1)S(1)}, bf16[193,16,128]{2,1,0:T(8,128)(2,1)S(1)}, u32[]{:S(2)}, u32[]{:S(2)}) collective-permute-start(bf16[193,16,128]{2,1,0:T(8,128)(2,1)S(1)} %collective-permute-done.25.refs_4_), channel_id=1, source_target_pairs={{0,8},{8,0},{1,9},{9,1},{2,10},{10,2},{3,11},{11,3},{4,12},{12,4},... | collective-permute-start | bytes 2371592 | tf_op jit(solution)/shard_map/ppermute | solution.py:372
  99.3 8.4 %collective-permute-start.28 = (bf16[129,16,128]{2,1,0:T(8,128)(2,1)S(1)}, bf16[129,16,128]{2,1,0:T(8,128)(2,1)S(1)}, u32[]{:S(2)}, u32[]{:S(2)}) collective-permute-start(bf16[129,16,128]{2,1,0:T(8,128)(2,1)S(1)} %collective-permute-done.19.refs_5_), channel_id=1, source_target_pairs={{0,2},{2,4},{4,6},{6,0},{8,14},{10,8},{12,10},{14,12},{1,3},{3,5},... | collective-permute-start | bytes 1585160 | tf_op jit(solution)/shard_map/ppermute | solution.py:388
  100.1 8.5 %collective-permute-start.26 = (bf16[113,16,128]{2,1,0:T(8,128)(2,1)S(1)}, bf16[113,16,128]{2,1,0:T(8,128)(2,1)S(1)}, u32[]{:S(2)}, u32[]{:S(2)}) collective-permute-start(bf16[113,16,128]{2,1,0:T(8,128)(2,1)S(1)} %collective-permute-done.21.refs_0_), channel_id=1, source_target_pairs={{0,32},{8,104},{32,64},{40,8},{64,96},{72,40},{96,0},{104,72},{1,3... | collective-permute-start | bytes 1388552 | tf_op jit(solution)/shard_map/ppermute | solution.py:382
  100.1 8.4 %collective-permute-start.27 = (bf16[80,16,128]{2,1,0:T(8,128)(2,1)S(1)}, bf16[80,16,128]{2,1,0:T(8,128)(2,1)S(1)}, u32[]{:S(2)}, u32[]{:S(2)}) collective-permute-start(bf16[80,16,128]{2,1,0:T(8,128)(2,1)S(1)} %slice.21), channel_id=1, source_target_pairs={{0,16},{16,0},{1,17},{17,1},{2,18},{18,2},{3,19},{19,3},{4,20},{20... | collective-permute-start | bytes 983048 | tf_op jit(solution)/shard_map/ppermute | solution.py:376
  108.6 6.8 %collective-permute-start.31 = (bf16[386,16,128]{2,1,0:T(8,128)(2,1)S(1)}, bf16[386,16,128]{2,1,0:T(8,128)(2,1)S(1)}, u32[]{:S(2)}, u32[]{:S(2)}) collective-permute-start(bf16[386,16,128]{2,1,0:T(8,128)(2,1)S(1)} %get-tuple-element.98), channel_id=1, source_target_pairs={{0,8},{8,0},{1,9},{9,1},{2,10},{10,2},{3,11},{11,3},{4,12},{12,4},... | collective-permute-start | bytes 4743176 | tf_op jit(solution)/shard_map/ppermute | solution.py:372
  110.4 4.9 %collective-permute-start.34 = (bf16[129,16,128]{2,1,0:T(8,128)(2,1)S(1)}, bf16[129,16,128]{2,1,0:T(8,128)(2,1)S(1)}, u32[]{:S(2)}, u32[]{:S(2)}) collective-permute-start(bf16[129,16,128]{2,1,0:T(8,128)(2,1)S(1)} %collective-permute-done.28.refs_2_), channel_id=1, source_target_pairs={{0,8},{8,0},{1,9},{9,1},{2,10},{10,2},{3,11},{11,3},{4,12},{12,4},... | collective-permute-start | bytes 1585160 | tf_op jit(solution)/shard_map/ppermute | solution.py:372
  110.5 4.8 %collective-permute-start.32 = (bf16[113,16,128]{2,1,0:T(8,128)(2,1)S(1)}, bf16[113,16,128]{2,1,0:T(8,128)(2,1)S(1)}, u32[]{:S(2)}, u32[]{:S(2)}) collective-permute-start(bf16[113,16,128]{2,1,0:T(8,128)(2,1)S(1)} %collective-permute-done.26.refs_0_), channel_id=1, source_target_pairs={{0,8},{8,0},{1,9},{9,1},{2,10},{10,2},{3,11},{11,3},{4,12},{12,4},... | collective-permute-start | bytes 1388552 | tf_op jit(solution)/shard_map/ppermute | solution.py:372
  110.9 4.4 %collective-permute-start.33 = (bf16[80,16,128]{2,1,0:T(8,128)(2,1)S(1)}, bf16[80,16,128]{2,1,0:T(8,128)(2,1)S(1)}, u32[]{:S(2)}, u32[]{:S(2)}) collective-permute-start(bf16[80,16,128]{2,1,0:T(8,128)(2,1)S(1)} %collective-permute-done.27.refs_1_), channel_id=1, source_target_pairs={{0,8},{8,0},{1,9},{9,1},{2,10},{10,2},{3,11},{11,3},{4,12},{12,4},... | collective-permute-start | bytes 983048 | tf_op jit(solution)/shard_map/ppermute | solution.py:372
